TPU v7x, 32 devices: a whole 2x2x4 slice. The times are simulated.
32 devices in a mesh: expert: 8 (over z, y), tensor: 4 (over x, core).
Axes of the slice: x: 2, y: 2, z: 4, core: 2. Of those that a mesh axis runs over, the one named last changes fastest.
Arguments:
- tokens: bfloat16 [6144, 2048], P('expert'), may hold values from -6 to 6
- out_grad: bfloat16 [6144, 2048], P('expert'), may hold values from -6 to 6
- attn_gain: float32 [2048], replicated, may hold values from 0.5 to 1.5
- attn_router: float32 [2048, 8], replicated, may hold values from -0.09375 to 0.09375
- w_query: bfloat16 [2048, 2048], P(None, 'tensor'), may hold values from -0.125 to 0.125
- w_key: bfloat16 [2048, 2048], P(None, 'tensor'), may hold values from -0.125 to 0.125
- w_value: bfloat16 [2048, 2048], P(None, 'tensor'), may hold values from -0.125 to 0.125
- w_out: bfloat16 [2048, 2048], P('tensor'), may hold values from -1 to 1
- mlp_gain: float32 [2048], replicated, may hold values from 0.5 to 1.5
- mlp_router: float32 [2048, 8], replicated, may hold values from -0.09375 to 0.09375
- w_gate: bfloat16 [8, 2048, 5632], P('expert', None, 'tensor'), may hold values from -0.125 to 0.125
- w_up: bfloat16 [8, 2048, 5632], P('expert', None, 'tensor'), may hold values from -0.125 to 0.125
- w_down: bfloat16 [8, 5632, 2048], P('expert', 'tensor'), may hold values from -0.078125 to 0.078125
- deal: int32 [6144], P('expert'), may hold values from 0 to 6143, as said below
- seq_lengths: int32 [8, 3], P('expert'), may hold values from 1 to 640, 768 in all within a row
- attn_routes: int32 [6144, 2], P('expert'), may hold values from 0 to 7, all different within a row
- mlp_routes: int32 [6144, 2], P('expert'), may hold values from 0 to 7, all different within a row
- slot_order: int32 [8, 1536], P('expert'), may hold values from 0 to 1535, each once within a row
Outputs:
- mixed: bfloat16 [6144, 2048], P('expert', 'tensor')
- tokens_grad: bfloat16 [6144, 2048], P('expert', 'tensor')
- attn_gain_grad: float32 [2048], replicated
- attn_router_grad: float32 [2048, 8], replicated
- w_query_grad: float32 [2048, 2048], P(None, 'tensor')
- w_key_grad: float32 [2048, 2048], P(None, 'tensor')
- w_value_grad: float32 [2048, 2048], P(None, 'tensor')
- w_out_grad: float32 [2048, 2048], P('tensor')
- mlp_gain_grad: float32 [2048], replicated
- mlp_router_grad: float32 [2048, 8], replicated
- w_gate_grad: float32 [8, 2048, 5632], P('expert', None, 'tensor')
- w_up_grad: float32 [8, 2048, 5632], P('expert', None, 'tensor')
- w_down_grad: float32 [8, 5632, 2048], P('expert', 'tensor')
Inputs may be any that keep to these rules, and one draw needn't show every extreme that they name: `deal`: each layout position occurs once. The tokens of rows s * 768 to (s + 1) * 768 - 1 that go to group g fill exactly the positions g * 768 + s * 96 to g * 768 + (s + 1) * 96 - 1, 96 of them for every s and g. `seq_lengths`: each row sums to 768; its largest length is 640. `attn_routes`: A position's two experts differ. `mlp_routes`: A position's two experts differ. `slot_order`: each row holds every number once.
All inputs are finite; a program needn't handle non-finite values.
Results may differ from a plain program's by a relative error of at most 0.018.
Values may be sent and summed in bfloat16 or wider, within the bound.
A program may use at most 320 MiB of HBM per device.

v0:
```python
import math

import jax
import jax.numpy as jnp
from jax import lax
from jax.sharding import PartitionSpec as P

HEAD = 128
QH = 2


PRECISE = lax.Precision.HIGHEST
EPSILON = 1e-06
MASKED = -1e30


def half_turn(values):
    middle = values.shape[-1] // 2
    return jnp.concatenate([-values[..., middle:], values[..., :middle]], axis=-1)


def undo_turn(values, cosine, sine):
    return values * cosine - half_turn(values * sine)


def rotary_tables(lengths, tok_rows):
    seq_ends = jnp.cumsum(lengths)
    seq_starts = seq_ends - lengths
    places = jnp.arange(tok_rows, dtype=jnp.int32)
    segment = jnp.sum((places[:, None] >= seq_ends[None, :]).astype(jnp.int32), axis=1)
    matches = segment[:, None] == jnp.arange(lengths.shape[0], dtype=jnp.int32)[None, :]
    seq_first = jnp.sum(jnp.where(matches, seq_starts[None, :], 0), axis=1)
    offsets = (places - seq_first).astype(jnp.float32)
    frequency = jnp.exp(-math.log(10000.0) * jnp.arange(0, HEAD, 2, dtype=jnp.float32) / HEAD)
    angles = offsets[:, None] * frequency[None, :]
    angles = jnp.concatenate([angles, angles], axis=1)
    return (segment, jnp.cos(angles)[:, None, :], jnp.sin(angles)[:, None, :])


def pair_gates(logits, routes):
    columns = logits.shape[1]
    chosen_mask = (
        routes[:, :, None] == jnp.arange(columns, dtype=jnp.int32)[None, None, :]
    ).astype(jnp.float32)
    picked = jnp.sum(chosen_mask * logits[:, None, :], axis=2)
    return (jax.nn.softmax(picked, axis=1), chosen_mask)


def pair_back(gates, chosen_mask, gate_grads):
    inner = gates * (gate_grads - jnp.sum(gates * gate_grads, axis=1, keepdims=True))
    return jnp.sum(chosen_mask * inner[:, :, None], axis=1)


def slot_table(routes, priority, expert_count, capacity):
    target = routes.reshape(-1)
    pair_count = target.shape[0]
    by_priority = (
        jnp.zeros((pair_count,), jnp.int32)
        .at[priority]
        .set(jnp.arange(pair_count, dtype=jnp.int32))
    )
    ranked = target[by_priority]
    matched = (ranked[:, None] == jnp.arange(expert_count, dtype=jnp.int32)[None, :]).astype(
        jnp.int32
    )
    earlier = jnp.cumsum(matched, axis=0) - matched
    ranked_slot = jnp.sum(earlier * matched, axis=1)
    position = ranked_slot[priority]
    return (target, position, position < capacity)


def norm_stats(values, gain):
    factor = lax.rsqrt(jnp.mean(values * values, axis=1, keepdims=True) + EPSILON)
    scaled = values * factor
    return (factor, scaled, scaled * gain)


def norm_back(grad_out, factor, scaled, gain):
    inner = grad_out * gain
    return factor * (inner - scaled * jnp.mean(inner * scaled, axis=1, keepdims=True))


def block_scores(query, keys, segment, start, block_rows, scale):
    places = jnp.arange(keys.shape[0], dtype=jnp.int32)
    allowed = (segment[start : start + block_rows, None] == segment[None, :]) & (
        places[:, None] >= places[None, :]
    )
    raw = jnp.einsum("qhd,khd->hqk", query, keys, preferred_element_type=jnp.float32) * scale
    return jnp.where(allowed[None], raw, MASKED)


def send_rows(buffer, sharers):
    model_width = buffer.shape[2]
    copies = jnp.repeat(buffer, sharers, axis=0)
    arrived = lax.all_to_all(copies, "expert", split_axis=0, concat_axis=0, tiled=True)
    return arrived.reshape(-1, model_width)


def return_rows(partial_rows, group_count, expert_count, capacity):
    share = lax.psum_scatter(partial_rows, "tensor", scatter_dimension=1, tiled=True)
    col_width = share.shape[1]
    arrived = lax.all_to_all(
        share.reshape(group_count, capacity, col_width).astype(jnp.bfloat16),
        "expert",
        split_axis=0,
        concat_axis=0,
        tiled=True,
    ).astype(jnp.float32)
    summed = jnp.sum(
        arrived.reshape(expert_count, group_count // expert_count, capacity, col_width), axis=1
    )
    return summed.astype(jnp.bfloat16).reshape(expert_count * capacity, col_width)


def body(
    tokens,
    out_grad,
    attn_gain,
    attn_router,
    w_query,
    w_key,
    w_value,
    w_out,
    mlp_gain,
    mlp_router,
    w_gate,
    w_up,
    w_down,
    deal,
    seq_lengths,
    attn_routes,
    mlp_routes,
    slot_order,
):
    tok_rows, model_width = tokens.shape
    group_count = lax.axis_size("expert")
    part_count = lax.axis_size("tensor")
    group_index = lax.axis_index("expert")
    part_index = lax.axis_index("tensor")
    bucket_rows = tok_rows // group_count
    col_width = model_width // part_count
    col_first = part_index * col_width
    deal_rank = deal // tok_rows * bucket_rows + (deal % tok_rows - group_index * bucket_rows)
    deal_order = (
        jnp.zeros((tok_rows,), jnp.int32).at[deal_rank].set(jnp.arange(tok_rows, dtype=jnp.int32))
    )
    dealt_rows, dealt_grads = (
        lax.all_to_all(
            tokens[deal_order].reshape(group_count, bucket_rows, model_width),
            "expert",
            split_axis=0,
            concat_axis=0,
            tiled=True,
        ),
        lax.all_to_all(
            out_grad[deal_order].reshape(group_count, bucket_rows, model_width),
            "expert",
            split_axis=0,
            concat_axis=0,
            tiled=True,
        ),
    )
    resid_in = dealt_rows.reshape(tok_rows, model_width).astype(jnp.float32)
    resid_grad = dealt_grads.reshape(tok_rows, model_width).astype(jnp.float32)
    segment, cosine, sine = rotary_tables(seq_lengths[0], tok_rows)
    scale = 1.0 / math.sqrt(HEAD)
    local_heads = w_query.shape[1] // HEAD
    local_experts = local_heads // QH
    span = QH * HEAD
    factor_one, scaled_one, normed_one = norm_stats(resid_in, attn_gain)
    normed_low = normed_one.astype(jnp.bfloat16)
    attn_gates, attn_mask = pair_gates(
        jnp.dot(normed_one, attn_router, precision=PRECISE), attn_routes
    )
    gate_table = jnp.sum(attn_gates[:, :, None] * attn_mask, axis=1)
    gate_local = lax.dynamic_slice_in_dim(gate_table, part_index * local_experts, local_experts, 1)
    query_pre = jnp.dot(normed_low, w_query, preferred_element_type=jnp.float32).reshape(
        tok_rows, local_heads, HEAD
    )
    key_pre = jnp.dot(normed_low, w_key, preferred_element_type=jnp.float32).reshape(
        tok_rows, local_heads, HEAD
    )
    values = (
        jnp.dot(normed_low, w_value, preferred_element_type=jnp.float32)
        .astype(jnp.bfloat16)
        .reshape(tok_rows, local_heads, HEAD)
    )
    query = (query_pre * cosine + half_turn(query_pre) * sine).astype(jnp.bfloat16)
    keys = (key_pre * cosine + half_turn(key_pre) * sine).astype(jnp.bfloat16)
    start = 0
    scores = block_scores(query, keys, segment, start, tok_rows, scale)
    top_score = jnp.max(scores, axis=-1, keepdims=True)
    expo = jnp.exp(scores - top_score)
    totals = jnp.sum(expo, axis=-1, keepdims=True)
    probs = (expo / totals).astype(jnp.bfloat16)
    head_blocks = jnp.einsum("hqk,khd->qhd", probs, values, preferred_element_type=jnp.float32)
    log_totals = [top_score + jnp.log(totals)]
    heads_low = head_blocks.astype(jnp.bfloat16).reshape(tok_rows, local_heads * HEAD)
    branch_terms = []
    attn_part = jnp.zeros((tok_rows, model_width), jnp.float32)
    for expert in range(local_experts):
        contrib = jnp.dot(
            heads_low[:, expert * span : (expert + 1) * span],
            w_out[expert * span : (expert + 1) * span],
            preferred_element_type=jnp.float32,
        )
        branch_terms.append(contrib)
        attn_part = attn_part + gate_local[:, expert : expert + 1] * contrib
    hidden = resid_in + lax.psum(attn_part, "tensor")
    factor_two, scaled_two, normed_two = norm_stats(hidden, mlp_gain)
    normed_two_low = normed_two.astype(jnp.bfloat16)
    mlp_gates, mlp_mask = pair_gates(jnp.dot(normed_two, mlp_router, precision=PRECISE), mlp_routes)
    expert_count = mlp_router.shape[1]
    sharers = group_count // expert_count
    capacity = 5 * tok_rows // (2 * expert_count)
    target, position, kept = slot_table(mlp_routes, slot_order[0], expert_count, capacity)
    destination = jnp.where(kept, target * capacity + position, expert_count * capacity)
    pair_ids = jnp.arange(2 * tok_rows, dtype=jnp.int32)
    owner = (
        jnp.full((expert_count * capacity + 1,), 2 * tok_rows, jnp.int32)
        .at[destination]
        .set(pair_ids)[:-1]
    )
    owner_token = owner // 2
    padded_rows = jnp.concatenate(
        [normed_two_low, jnp.zeros((1, model_width), jnp.bfloat16)], axis=0
    )
    inbox = send_rows(
        padded_rows[owner_token].reshape(expert_count, capacity, model_width), sharers
    )
    gate_w = w_gate[0]
    up_w = w_up[0]
    down_w = w_down[0]
    gate_pre = jnp.dot(inbox, gate_w, preferred_element_type=jnp.float32)
    up_pre = jnp.dot(inbox, up_w, preferred_element_type=jnp.float32)
    middle = (jax.nn.silu(gate_pre) * up_pre).astype(jnp.bfloat16)
    made = return_rows(
        jnp.dot(middle, down_w, preferred_element_type=jnp.float32),
        group_count,
        expert_count,
        capacity,
    )
    made_ext = jnp.concatenate([made, jnp.zeros((1, col_width), jnp.bfloat16)], axis=0)
    pair_values = made_ext[destination].reshape(tok_rows, 2, col_width).astype(jnp.float32)
    hidden_cols = lax.dynamic_slice_in_dim(hidden, col_first, col_width, 1)
    mixed_cols = hidden_cols + jnp.sum(mlp_gates[:, :, None] * pair_values, axis=1)
    grad_cols = lax.dynamic_slice_in_dim(resid_grad, col_first, col_width, 1)
    gate_terms = jnp.sum(pair_values * grad_cols[:, None, :], axis=2)
    gates_ext = jnp.concatenate([mlp_gates.reshape(-1), jnp.zeros((1,), jnp.float32)])
    grads_ext = jnp.concatenate([resid_grad, jnp.zeros((1, model_width), jnp.float32)], axis=0)
    grad_buffer = (gates_ext[owner][:, None] * grads_ext[owner_token]).astype(jnp.bfloat16)
    grad_inbox = send_rows(grad_buffer.reshape(expert_count, capacity, model_width), sharers)
    middle_grad = jnp.einsum("sd,fd->sf", grad_inbox, down_w, preferred_element_type=jnp.float32)
    down_grad = jnp.einsum("sf,sd->fd", middle, grad_inbox, preferred_element_type=jnp.float32)
    sigmoid_gate = jax.nn.sigmoid(gate_pre)
    gate_grad_low = (
        middle_grad * up_pre * sigmoid_gate * (1.0 + gate_pre * (1.0 - sigmoid_gate))
    ).astype(jnp.bfloat16)
    up_grad_low = (middle_grad * gate_pre * sigmoid_gate).astype(jnp.bfloat16)
    gate_w_grad = jnp.einsum("sd,sf->df", inbox, gate_grad_low, preferred_element_type=jnp.float32)
    up_w_grad = jnp.einsum("sd,sf->df", inbox, up_grad_low, preferred_element_type=jnp.float32)
    inbox_grad = jnp.einsum(
        "sf,df->sd", gate_grad_low, gate_w, preferred_element_type=jnp.float32
    ) + jnp.einsum("sf,df->sd", up_grad_low, up_w, preferred_element_type=jnp.float32)
    row_grads = return_rows(inbox_grad, group_count, expert_count, capacity)
    row_grads_ext = jnp.concatenate([row_grads, jnp.zeros((1, col_width), jnp.bfloat16)], axis=0)
    pair_grad_sum = jnp.sum(
        row_grads_ext[destination].reshape(tok_rows, 2, col_width).astype(jnp.float32), axis=1
    )
    norm_two_grad, gate_all = (
        lax.all_gather(pair_grad_sum, "tensor", axis=1, tiled=True),
        lax.all_gather(gate_terms, "tensor", axis=1, tiled=True),
    )
    mlp_gate_grad = jnp.sum(gate_all.reshape(tok_rows, part_count, 2), axis=1)
    mlp_logit_grad = pair_back(mlp_gates, mlp_mask, mlp_gate_grad)
    norm_two_grad = norm_two_grad + jnp.dot(mlp_logit_grad, mlp_router.T, precision=PRECISE)
    mlp_router_grad = jnp.dot(normed_two.T, mlp_logit_grad, precision=PRECISE)
    mlp_gain_grad = jnp.sum(norm_two_grad * scaled_two, axis=0)
    hidden_grad = resid_grad + norm_back(norm_two_grad, factor_two, scaled_two, mlp_gain)
    local_gate_grad = jnp.stack(
        [jnp.sum(branch_terms[expert] * hidden_grad, axis=1) for expert in range(local_experts)],
        axis=1,
    )
    out_grads = []
    out_w_grads = []
    for expert in range(local_experts):
        branch_grad = (gate_local[:, expert : expert + 1] * hidden_grad).astype(jnp.bfloat16)
        out_w_grads.append(
            jnp.einsum(
                "tc,td->cd",
                heads_low[:, expert * span : (expert + 1) * span],
                branch_grad,
                preferred_element_type=jnp.float32,
            )
        )
        out_grads.append(
            jnp.einsum(
                "td,cd->tc",
                branch_grad,
                w_out[expert * span : (expert + 1) * span],
                preferred_element_type=jnp.float32,
            )
        )
    out_w_grad = jnp.concatenate(out_w_grads, axis=0)
    heads_grad = (
        jnp.concatenate(out_grads, axis=1).astype(jnp.bfloat16).reshape(tok_rows, local_heads, HEAD)
    )
    key_grad = jnp.zeros((tok_rows, local_heads, HEAD), jnp.float32)
    value_grad = jnp.zeros((tok_rows, local_heads, HEAD), jnp.float32)
    query_blocks = []
    for number, start in enumerate(range(0, tok_rows, tok_rows)):
        scores = block_scores(query, keys, segment, start, tok_rows, scale)
        probs = jnp.exp(scores - log_totals[number])
        value_grad = jnp.einsum(
            "hqk,qhd->khd",
            probs.astype(jnp.bfloat16),
            heads_grad,
            preferred_element_type=jnp.float32,
        )
        prob_grad = jnp.einsum(
            "qhd,khd->hqk", heads_grad, values, preferred_element_type=jnp.float32
        )
        score_grad = (
            probs * (prob_grad - jnp.sum(probs * prob_grad, axis=-1, keepdims=True))
        ).astype(jnp.bfloat16)
        query_blocks.append(
            jnp.einsum("hqk,khd->qhd", score_grad, keys, preferred_element_type=jnp.float32) * scale
        )
        key_grad = (
            jnp.einsum("hqk,qhd->khd", score_grad, query, preferred_element_type=jnp.float32)
            * scale
        )
    query_grad = query_blocks[0]
    query_pre_grad = (
        undo_turn(query_grad, cosine, sine)
        .astype(jnp.bfloat16)
        .reshape(tok_rows, local_heads * HEAD)
    )
    key_pre_grad = (
        undo_turn(key_grad, cosine, sine).astype(jnp.bfloat16).reshape(tok_rows, local_heads * HEAD)
    )
    value_pre_grad = value_grad.astype(jnp.bfloat16).reshape(tok_rows, local_heads * HEAD)
    query_w_grad = jnp.einsum(
        "td,tc->dc", normed_low, query_pre_grad, preferred_element_type=jnp.float32
    )
    key_w_grad = jnp.einsum(
        "td,tc->dc", normed_low, key_pre_grad, preferred_element_type=jnp.float32
    )
    value_w_grad = jnp.einsum(
        "td,tc->dc", normed_low, value_pre_grad, preferred_element_type=jnp.float32
    )
    norm_one_part = jnp.einsum(
        "tc,dc->td", query_pre_grad, w_query, preferred_element_type=jnp.float32
    )
    norm_one_part = norm_one_part + jnp.einsum(
        "tc,dc->td", key_pre_grad, w_key, preferred_element_type=jnp.float32
    )
    norm_one_part = norm_one_part + jnp.einsum(
        "tc,dc->td", value_pre_grad, w_value, preferred_element_type=jnp.float32
    )
    mask_local = lax.dynamic_slice_in_dim(attn_mask, part_index * local_experts, local_experts, 2)
    attn_pair_grad = jnp.sum(mask_local * local_gate_grad[:, None, :], axis=2)
    attn_logit_grad = pair_back(attn_gates, attn_mask, attn_pair_grad)
    norm_one_part = norm_one_part + jnp.dot(attn_logit_grad, attn_router.T, precision=PRECISE)
    router_part = jnp.dot(normed_one.T, attn_logit_grad, precision=PRECISE)
    norm_one_grad, attn_router_grad = lax.psum((norm_one_part, router_part), "tensor")
    attn_gain_grad = jnp.sum(norm_one_grad * scaled_one, axis=0)
    input_grad = hidden_grad + norm_back(norm_one_grad, factor_one, scaled_one, attn_gain)
    summed = (
        lax.psum(query_w_grad.astype(jnp.bfloat16), "expert").astype(jnp.float32),
        lax.psum(key_w_grad.astype(jnp.bfloat16), "expert").astype(jnp.float32),
        lax.psum(value_w_grad.astype(jnp.bfloat16), "expert").astype(jnp.float32),
        lax.psum(out_w_grad.astype(jnp.bfloat16), "expert").astype(jnp.float32),
        lax.psum(attn_gain_grad.astype(jnp.bfloat16), "expert").astype(jnp.float32),
        lax.psum(attn_router_grad.astype(jnp.bfloat16), "expert").astype(jnp.float32),
        lax.psum(mlp_gain_grad.astype(jnp.bfloat16), "expert").astype(jnp.float32),
        lax.psum(mlp_router_grad.astype(jnp.bfloat16), "expert").astype(jnp.float32),
    )
    input_cols = lax.dynamic_slice_in_dim(input_grad, col_first, col_width, 1)
    back_mixed, back_grad = (
        lax.all_to_all(
            mixed_cols.astype(jnp.bfloat16).reshape(group_count, bucket_rows, col_width),
            "expert",
            split_axis=0,
            concat_axis=0,
            tiled=True,
        ),
        lax.all_to_all(
            input_cols.astype(jnp.bfloat16).reshape(group_count, bucket_rows, col_width),
            "expert",
            split_axis=0,
            concat_axis=0,
            tiled=True,
        ),
    )
    mixed = back_mixed.reshape(tok_rows, col_width)[deal_rank]
    tokens_grad = back_grad.reshape(tok_rows, col_width)[deal_rank]
    return (
        mixed,
        tokens_grad,
        summed[4],
        summed[5],
        summed[0],
        summed[1],
        summed[2],
        summed[3],
        summed[6],
        summed[7],
        gate_w_grad[None],
        up_w_grad[None],
        down_grad[None],
    )


def solution(mesh):
    placed = (
        P("expert", None),
        P("expert", None),
        P(),
        P(),
        P(None, "tensor"),
        P(None, "tensor"),
        P(None, "tensor"),
        P("tensor", None),
        P(),
        P(),
        P("expert", None, "tensor"),
        P("expert", None, "tensor"),
        P("expert", "tensor", None),
        P("expert"),
        P("expert", None),
        P("expert", None),
        P("expert", None),
        P("expert", None),
    )
    return jax.shard_map(
        body,
        mesh=mesh,
        in_specs=placed,
        out_specs=(
            P("expert", "tensor"),
            P("expert", "tensor"),
            P(),
            P(),
            P(None, "tensor"),
            P(None, "tensor"),
            P(None, "tensor"),
            P("tensor", None),
            P(),
            P(),
            P("expert", None, "tensor"),
            P("expert", None, "tensor"),
            P("expert", "tensor", None),
        ),
        check_vma=False,
    )
```

profile of v0, /device:TPU:20, one launch (start us, length us, event | category | flops | bytes accessed | tf_op | source)
XLA Modules:
  0.0 1604.0 jit_solution(5776849371772808103)
XLA Ops:
  15.7 6.1 all-to-all-start
  38.0 51.3 %all-to-all-done = bf16[8,96,2048]{2,1,0:T(8,128)(2,1)} async-done(((bf16[8,96,2048]{2,1,0:T(8,128)(2,1)}), bf16[8,96,2048]{2,1,0:T(8,128)(2,1)}, u32[]{:S(2)}, u32[]{:S(2)}) %all-to-all-start) | async-done | bytes 3145760 | tf_op jit(solution)/shard_map/all_to_all | solution.py:148
  89.3 7.7 all-to-all-start.4
  138.9 6.2 multiply_add_fusion.1
  146.4 6.2 scatter_custom_fusion.1
  152.6 8.4 gather_fusion.1
  164.4 8.4 gather_fusion.2
  172.8 6.4 scatter_custom_fusion.2
  179.2 86.7 %all-reduce.11.cloned.1.call-done = f32[768,2048]{1,0:T(8,128)} async-done(((f32[768,2048]{1,0:T(8,128)}), f32[768,2048]{1,0:T(8,128)}) %all-reduce.11.cloned.1.call-update) | async-done | bytes 6291472 | tf_op jit(solution)/shard_map/psum | solution.py:209
  275.8 18.6 %gather_fusion.3 = bf16[1920,2048]{1,0:T(8,128)(2,1)} fusion(bf16[769,2048]{1,0:T(8,128)(2,1)} %concatenate.54, s32[2048]{0:T(1024)S(1)} %pad_clamp_fusion.2), kind=kCustom, calls=%fused_computation.3 | custom fusion | bytes 15736320 | tf_op jit(solution)/shard_map/gather | solution.py:229
  294.4 6.0 all-to-all-start.1
  308.9 18.6 %gather_fusion.8 = f32[1920,2048]{1,0:T(8,128)} fusion(f32[769,2048]{1,0:T(8,128)} %concatenate.57, s32[2048]{0:T(1024)S(1)} %pad_clamp_fusion.2), kind=kCustom, calls=%fused_computation.8 | custom fusion | bytes 31464960 | tf_op jit(solution)/shard_map/gather | solution.py:251
  327.6 7.7 fusion.18
  337.7 10.4 gather_fusion.7
  348.2 8.7 multiply_convert_fusion
  356.9 111.8 %all-to-all-done.1 = bf16[8,240,2048]{2,1,0:T(8,128)(2,1)} async-done(((bf16[8,240,2048]{2,1,0:T(8,128)(2,1)}), bf16[8,240,2048]{2,1,0:T(8,128)(2,1)}, u32[]{:S(2)}, u32[]{:S(2)}) %all-to-all-start.1) | async-done | bytes 7864352 | tf_op jit(solution)/shard_map/all_to_all | solution.py:95
  468.7 8.2 all-to-all-start.5
  477.2 17.9 %fusion.10 = f32[1920,1408]{1,0:T(8,128)} fusion(bf16[1920,2048]{1,0:T(8,128)(2,1)} %bitcast.21, bf16[1,2048,1408]{2,1,0:T(8,128)(2,1)} %param.29), kind=kOutput, calls=%fused_computation.55 | convolution fusion | flops 11072962560 | bytes 24444928 | tf_op jit(solution)/shard_map/dot_general | solution.py:235
  495.1 17.9 %fusion.14 = f32[1920,1408]{1,0:T(8,128)} fusion(bf16[1920,2048]{1,0:T(8,128)(2,1)} %bitcast.21, bf16[1,2048,1408]{2,1,0:T(8,128)(2,1)} %param.28), kind=kOutput, calls=%fused_computation.59 | convolution fusion | flops 11072962560 | bytes 24444928 | tf_op jit(solution)/shard_map/dot_general | solution.py:234
  513.0 131.5 %all-to-all-done.5 = bf16[8,240,2048]{2,1,0:T(8,128)(2,1)} async-done(((bf16[8,240,2048]{2,1,0:T(8,128)(2,1)}), bf16[8,240,2048]{2,1,0:T(8,128)(2,1)}, u32[]{:S(2)}, u32[]{:S(2)}) %all-to-all-start.5) | async-done | bytes 7864352 | tf_op jit(solution)/shard_map/all_to_all | solution.py:95
  644.5 25.6 %multiply_convert_fusion.1 = (bf16[1920,1408]{1,0:T(8,128)(2,1)}, bf16[1920,1408]{1,0:T(8,128)(2,1)}, bf16[1920,1408]{1,0:T(8,128)(2,1)}) fusion(f32[1920,1408]{1,0:T(8,128)} %fusion.14, f32[1920,1408]{1,0:T(8,128)} %fusion.10, bf16[1920,2048]{1,0:T(8,128)(2,1)} %bitcast.33, bf16[1,1408,2048]{2,1,0:T(8,128)(2,1)} %param.30), kind=kOutput, calls=%fused_computation.15 | convolution fusion | flops 11116216320 | bytes 51478528 | tf_op jit(solution)/shard_map/sd,fd->sf/dot_general | solution.py:253
  670.1 18.3 %fusion.12 = f32[1920,2048]{1,0:T(8,128)} fusion(bf16[1920,1408]{1,0:T(8,128)(2,1)} %get-tuple-element.36, bf16[1,2048,1408]{2,1,0:T(8,128)(2,1)} %param.28), kind=kOutput, calls=%fused_computation.57 | convolution fusion | flops 11072962560 | bytes 26902528 | tf_op jit(solution)/shard_map/sf,df->sd/dot_general | solution.py:262
  688.5 21.8 %convolution_add_fusion = f32[1920,2048]{1,0:T(8,128)} fusion(f32[1920,2048]{1,0:T(8,128)} %fusion.12, bf16[1920,1408]{1,0:T(8,128)(2,1)} %get-tuple-element.35, bf16[1,2048,1408]{2,1,0:T(8,128)(2,1)} %param.29), kind=kOutput, calls=%fused_computation.29 | convolution fusion | flops 11076894720 | bytes 42631168 | tf_op jit(solution)/shard_map/sf,df->sd/dot_general | solution.py:264
  710.4 18.9 %fusion.7 = f32[1920,2048]{1,0:T(8,128)} fusion(bf16[1920,1408]{1,0:T(8,128)(2,1)} %get-tuple-element.37, bf16[1,1408,2048]{2,1,0:T(8,128)(2,1)} %param.30), kind=kOutput, calls=%fused_computation.52 | convolution fusion | flops 11072962560 | bytes 26902528 | tf_op jit(solution)/shard_map/dot_general | solution.py:238
  729.3 103.0 %reduce-scatter.5.cloned.1.call-done = f32[1920,512]{1,0:T(8,128)} async-done(((f32[1920,2048]{1,0:T(8,128)}), f32[1920,512]{1,0:T(8,128)}) %reduce-scatter.5.cloned.1.call-update) | async-done | bytes 3932176 | tf_op jit(solution)/shard_map/reduce_scatter | solution.py:100
  836.0 6.0 all-to-all-start.6
  842.0 42.1 %all-to-all-done.6 = bf16[8,240,512]{2,1,0:T(8,128)(2,1)S(1)} async-done(((bf16[8,240,512]{2,1,0:T(8,128)(2,1)}), bf16[8,240,512]{2,1,0:T(8,128)(2,1)S(1)}, u32[]{:S(2)}, u32[]{:S(2)}) %all-to-all-start.6) | async-done | bytes 1966112 | tf_op jit(solution)/shard_map/all_to_all | solution.py:102
  887.1 5.6 gather_fusion.9
  901.4 53.4 %reduce-scatter.3.cloned.1.call-done = f32[1920,512]{1,0:T(8,128)} async-done(((f32[1920,2048]{1,0:T(8,128)}), f32[1920,512]{1,0:T(8,128)}) %reduce-scatter.3.cloned.1.call-update) | async-done | bytes 3932176 | tf_op jit(solution)/shard_map/reduce_scatter | solution.py:100
  958.4 6.0 all-to-all-start.2
  968.6 38.0 %all-to-all-done.2 = bf16[8,240,512]{2,1,0:T(8,128)(2,1)S(1)} async-done(((bf16[8,240,512]{2,1,0:T(8,128)(2,1)}), bf16[8,240,512]{2,1,0:T(8,128)(2,1)S(1)}, u32[]{:S(2)}, u32[]{:S(2)}) %all-to-all-start.2) | async-done | bytes 1966112 | tf_op jit(solution)/shard_map/all_to_all | solution.py:102
  1018.4 8.7 multiply_reduce_fusion.8
  1035.8 10.7 multiply_reduce_fusion.1
  1046.4 9.1 multiply_reduce_fusion.5
  1058.7 7.6 multiply_reduce_fusion
  1066.3 6.4 fusion.49
  1072.7 10.3 multiply_convert_fusion.4
  1097.1 8.3 add_add_fusion
  1106.1 7.3 fusion.37
  1118.9 14.2 psum.80
  1151.0 76.1 %all-reduce.13.cloned.1.call-done = f32[768,2048]{1,0:T(8,128)} async-done(((f32[768,2048]{1,0:T(8,128)}), f32[768,2048]{1,0:T(8,128)}) %all-reduce.13.cloned.1.call-update) | async-done | bytes 6291472 | tf_op jit(solution)/shard_map/psum | solution.py:366
  1227.1 6.9 multiply_reduce_fusion.2
  1235.7 19.0 %convolution_bitcast_fusion = f32[1,2048,1408]{2,1,0:T(8,128)} fusion(bf16[1920,2048]{1,0:T(8,128)(2,1)} %bitcast.21, bf16[1920,1408]{1,0:T(8,128)(2,1)} %get-tuple-element.35), kind=kOutput, calls=%fused_computation.25 | convolution fusion | flops 11072962560 | bytes 24805376 | tf_op jit(solution)/shard_map/sd,sf->df/dot_general | solution.py:261
  1257.2 6.0 all-to-all-start.3
  1263.2 18.6 %convolution_bitcast_fusion.1 = f32[1,2048,1408]{2,1,0:T(8,128)} fusion(bf16[1920,2048]{1,0:T(8,128)(2,1)} %bitcast.21, bf16[1920,1408]{1,0:T(8,128)(2,1)} %get-tuple-element.36), kind=kOutput, calls=%fused_computation.26 | convolution fusion | flops 11072962560 | bytes 24805376 | tf_op jit(solution)/shard_map/sd,sf->df/dot_general | solution.py:260
  1285.4 6.3 all-to-all-start.7
  1291.7 18.7 %convolution_bitcast_fusion.2 = f32[1,1408,2048]{2,1,0:T(8,128)} fusion(bf16[1920,1408]{1,0:T(8,128)(2,1)} %get-tuple-element.37, bf16[1920,2048]{1,0:T(8,128)(2,1)} %bitcast.33), kind=kOutput, calls=%fused_computation.27 | convolution fusion | flops 11072962560 | bytes 24805376 | tf_op jit(solution)/shard_map/sf,sd->fd/dot_general | solution.py:254
  1322.5 262.0 %all-reduce.17.cloned.1.call-done = (bf16[2048,512]{1,0:T(8,128)(2,1)}, bf16[2048,512]{1,0:T(8,128)(2,1)}, bf16[2048,512]{1,0:T(8,128)(2,1)}, bf16[512,2048]{1,0:T(8,128)(2,1)}) async-done(((bf16[2048,512]{1,0:T(8,128)(2,1)}, bf16[2048,512]{1,0:T(8,128)(2,1)}, bf16[2048,512]{1,0:T(8,128)(2,1)}, bf16[512,2048]{1,0:T(8,128)(2,1)}), (bf16[2048,512]{1,0:T(8,128)(2,1)}, bf16[2048,512]{1,0:T(8,128)(2,1)}, ...) | async-done | bytes 8388624 | tf_op jit(solution)/shard_map/psum | solution.py:370
  (330 shorter events, 208.0 us)
Async XLA Ops:
  15.7 73.5 %all-to-all-start = ((bf16[8,96,2048]{2,1,0:T(8,128)(2,1)}), bf16[8,96,2048]{2,1,0:T(8,128)(2,1)}, u32[]{:S(2)}, u32[]{:S(2)}) async-start(bf16[8,96,2048]{2,1,0:T(8,128)(2,1)} %bitcast.168), calls=%async_computation | async-start | bytes 6291456 | tf_op jit(solution)/shard_map/all_to_all | solution.py:148
  21.9 8.0 copy-start.87
  21.9 8.2 copy-start.4
  34.5 65.4 %copy-start.55 = (f32[2048]{0:T(1024)S(1)}, f32[2048]{0:T(1024)}, u32[]{:S(2)}) copy-start(f32[2048]{0:T(1024)} %param.20) | copy-start | bytes 24580
  89.3 205.1 %all-to-all-start.4 = ((bf16[8,96,2048]{2,1,0:T(8,128)(2,1)}), bf16[8,96,2048]{2,1,0:T(8,128)(2,1)}, u32[]{:S(2)}, u32[]{:S(2)}) async-start(bf16[8,96,2048]{2,1,0:T(8,128)(2,1)} %bitcast.167), calls=%async_computation.5 | async-start | bytes 6291456 | tf_op jit(solution)/shard_map/all_to_all | solution.py:155
  97.0 168.9 %all-reduce.11.cloned.1.call-start = ((), (), s32[]{:S(2)}) async-start(), calls=%async_computation.10 | async-start | bytes 12582912 | tf_op jit(solution)/shard_map/psum | solution.py:209
  99.9 9.3 copy-start.74
  109.2 13.7 copy-start.21
  109.2 7.5 copy-start.47
  114.2 8.0 copy-start.65
  127.8 8.0 copy-start.3
  127.8 8.0 copy-start.60
  129.1 6.7 copy-start.79
  137.8 7.3 copy-start.22
  138.8 6.4 copy-start.6
  138.9 6.3 copy-start.72
  172.8 6.4 copy-start.81
  179.2 93.9 %copy-start.53 = (f32[2048]{0:T(1024)S(1)}, f32[2048]{0:T(1024)}, u32[]{:S(2)}) copy-start(f32[2048]{0:T(1024)} %param.26) | copy-start | bytes 24580
  270.5 57.0 %copy-start.58 = (f32[768]{0:T(1024)}, f32[768]{0:T(1024)S(1)}, u32[]{:S(2)}) copy-start(f32[768]{0:T(1024)S(1)} %add_rsqrt_fusion) | copy-start | bytes 9220
  294.4 174.3 %all-to-all-start.1 = ((bf16[8,240,2048]{2,1,0:T(8,128)(2,1)}), bf16[8,240,2048]{2,1,0:T(8,128)(2,1)}, u32[]{:S(2)}, u32[]{:S(2)}) async-start(bf16[8,240,2048]{2,1,0:T(8,128)(2,1)} %bitcast.166), calls=%async_computation.1 | async-start | bytes 15728640 | tf_op jit(solution)/shard_map/all_to_all | solution.py:95
  308.9 18.6 %copy-start.46 = (f32[2048,8]{0,1:T(8,128)S(1)}, f32[2048,8]{0,1:T(8,128)}, u32[]{:S(2)}) copy-start(f32[2048,8]{0,1:T(8,128)} %param.27) | copy-start | bytes 196612
  468.7 175.8 %all-to-all-start.5 = ((bf16[8,240,2048]{2,1,0:T(8,128)(2,1)}), bf16[8,240,2048]{2,1,0:T(8,128)(2,1)}, u32[]{:S(2)}, u32[]{:S(2)}) async-start(bf16[8,240,2048]{2,1,0:T(8,128)(2,1)} %multiply_convert_fusion), calls=%async_computation.6 | async-start | bytes 15728640 | tf_op jit(solution)/shard_map/all_to_all | solution.py:95
  476.9 355.4 %reduce-scatter.5.cloned.1.call-start = ((), (), s32[]{:S(2)}) async-start(), calls=%async_computation.12 | async-start | bytes 19660800 | tf_op jit(solution)/shard_map/reduce_scatter | solution.py:100
  710.3 244.5 %reduce-scatter.3.cloned.1.call-start = ((), (), s32[]{:S(2)}) async-start(), calls=%async_computation.11 | async-start | bytes 19660800 | tf_op jit(solution)/shard_map/reduce_scatter | solution.py:100
  729.3 112.6 %copy-start.82 = (s32[1536]{0:T(1024)S(1)}, s32[1536]{0:T(1024)}, u32[]{:S(2)}) copy-start(s32[1536]{0:T(1024)} %copy-done.81) | copy-start | bytes 18436
  836.0 48.2 %all-to-all-start.6 = ((bf16[8,240,512]{2,1,0:T(8,128)(2,1)}), bf16[8,240,512]{2,1,0:T(8,128)(2,1)S(1)}, u32[]{:S(2)}, u32[]{:S(2)}) async-start(bf16[8,240,512]{2,1,0:T(8,128)(2,1)} %bitcast.174), calls=%async_computation.8 | async-start | bytes 3932160 | tf_op jit(solution)/shard_map/all_to_all | solution.py:102
  842.0 193.8 %all-gather.3.cloned.1.call-start = ((), (), s32[]{:S(2)}) async-start(), calls=%async_computation.13 | async-start | bytes 7864320 | tf_op jit(solution)/shard_map/all_gather | solution.py:271
  901.3 63.1 %copy-start.67 = (s32[768,2]{0,1:T(2,128)S(1)}, s32[768,2]{0,1:T(2,128)}, u32[]{:S(2)}) copy-start(s32[768,2]{0,1:T(2,128)} %param.33) | copy-start | bytes 18436
  901.4 66.6 %copy-start.61 = (f32[4,768]{1,0:T(4,128)S(1)}, f32[4,768]{1,0:T(4,128)}, u32[]{:S(2)}) copy-start(f32[4,768]{1,0:T(4,128)} %copy-done.60) | copy-start | bytes 36868
  901.4 66.6 %copy-start.80 = (f32[4,768]{1,0:T(4,128)S(1)}, f32[4,768]{1,0:T(4,128)}, u32[]{:S(2)}) copy-start(f32[4,768]{1,0:T(4,128)} %copy-done.79) | copy-start | bytes 36868
  958.4 48.2 %all-to-all-start.2 = ((bf16[8,240,512]{2,1,0:T(8,128)(2,1)}), bf16[8,240,512]{2,1,0:T(8,128)(2,1)S(1)}, u32[]{:S(2)}, u32[]{:S(2)}) async-start(bf16[8,240,512]{2,1,0:T(8,128)(2,1)} %bitcast.172), calls=%async_computation.3 | async-start | bytes 3932160 | tf_op jit(solution)/shard_map/all_to_all | solution.py:102
  964.5 262.6 %all-reduce.13.cloned.1.call-start = ((), (), s32[]{:S(2)}) async-start(), calls=%async_computation.14 | async-start | bytes 12582912 | tf_op jit(solution)/shard_map/psum | solution.py:366
  1009.6 8.9 copy-start.25
  1015.0 18.6 %copy-start.52 = (f32[768,2]{0,1:T(2,128)S(1)}, f32[768,2]{0,1:T(2,128)}, u32[]{:S(2)}) copy-start(f32[768,2]{0,1:T(2,128)} %copy-done.51) | copy-start | bytes 18436
  1015.0 20.8 %copy-start.54 = (f32[2048]{0:T(1024)S(1)}, f32[2048]{0:T(1024)}, u32[]{:S(2)}) copy-start(f32[2048]{0:T(1024)} %param.26) | copy-start | bytes 24580
  1035.7 10.7 copy-start.59
  1046.4 9.2 copy-start.11
  1046.4 9.2 copy-start.73
  1072.7 10.3 copy-start.19
  1105.4 8.0 copy-start.56
  1105.4 208.4 %all-reduce.15.cloned.1.call-start = ((), (), s32[]{:S(2)}) async-start(), calls=%async_computation.15 | async-start | bytes 147456 | tf_op jit(solution)/shard_map/psum | solution.py:374
  1106.1 27.1 %copy-start.23 = (bf16[4,128,768]{2,1,0:T(8,128)(2,1)S(1)}, bf16[4,128,768]{2,1,0:T(8,128)(2,1)}, u32[]{:S(2)}) copy-start(bf16[4,128,768]{2,1,0:T(8,128)(2,1)} %copy-done.22) | copy-start | bytes 2359300
  1147.8 79.4 %copy-start.75 = (f32[768]{0:T(1024)S(1)}, f32[768]{0:T(1024)}, u32[]{:S(2)}) copy-start(f32[768]{0:T(1024)} %copy-done.74) | copy-start | bytes 9220
  1234.0 350.5 %all-reduce.17.cloned.1.call-start = ((), (), s32[]{:S(2)}) async-start(), calls=%async_computation.16 | async-start | bytes 16777216 | tf_op jit(solution)/shard_map/psum | solution.py:370
  1235.6 19.0 %copy-start.20 = (f32[768,512]{1,0:T(8,128)S(1)}, f32[768,512]{1,0:T(8,128)}, u32[]{:S(2)}) copy-start(f32[768,512]{1,0:T(8,128)} %get-tuple-element.20) | copy-start | bytes 4718596
  1257.2 28.2 %all-to-all-start.3 = ((bf16[8,96,512]{2,1,0:T(8,128)(2,1)}), bf16[8,96,512]{2,1,0:T(8,128)(2,1)S(1)}, u32[]{:S(2)}, u32[]{:S(2)}) async-start(bf16[8,96,512]{2,1,0:T(8,128)(2,1)} %bitcast.27), calls=%async_computation.4 | async-start | bytes 1572864 | tf_op jit(solution)/shard_map/all_to_all | solution.py:381
  1285.4 33.7 %all-to-all-start.7 = ((bf16[8,96,512]{2,1,0:T(8,128)(2,1)}), bf16[8,96,512]{2,1,0:T(8,128)(2,1)S(1)}, u32[]{:S(2)}, u32[]{:S(2)}) async-start(bf16[8,96,512]{2,1,0:T(8,128)(2,1)} %bitcast.47), calls=%async_computation.9 | async-start | bytes 1572864 | tf_op jit(solution)/shard_map/all_to_all | solution.py:388
  1584.5 7.0 copy-start.37
  (55 other events, 137.2 us)
Sparse Core Ops, SparseCore 0:
  145.4 120.4 all-reduce.10
  710.4 121.8 reduce-scatter.4
  834.9 119.8 reduce-scatter.2
  956.8 46.3 all-gather.2
  1105.5 121.5 all-reduce.12
  1234.1 73.5 all-reduce.14
  1312.8 271.6 all-reduce.16
where the time goes:
time: 1610 us; the launch traced here: 1600 us
  waiting for transfers between devices  956 us (59%)
  matrix products  286 us (18%)
  local copies, waits for them, and re-layouts  158 us (10%)
  other arithmetic  115 us (7%)
  starting transfers between devices  53 us (3%)
  blocking collectives  19.4 us (1%)
  between operations  16.1 us (1%)
    psum x1, waiting for transfers between devices, body(): lax.psum(query_w_grad.astype(jnp.bfloat16), 'expert').astype(jnp.float32)  262 us
    all_to_all x2, waiting for transfers between devices, send_rows(): lax.all_to_all(copies, 'expert', split_axis=0, concat_axis=0, tiled=True)  243 us
    reduce_scatter x2, waiting for transfers between devices, return_rows(): lax.psum_scatter(partial_rows, 'tensor', scatter_dimension=1, tiled=True)  156 us
    psum x1, waiting for transfers between devices, body(): hidden = resid_in + lax.psum(attn_part, 'tensor')  86.7 us
    all_to_all x2, waiting for transfers between devices, return_rows(): lax.all_to_all(share.reshape(group_count, capacity, col_width).astype(jnp...  80.2 us
    psum x1, waiting for transfers between devices, body(): lax.psum((norm_one_part, router_part), 'tensor')  76.1 us
    all_to_all x1, waiting for transfers between devices, body(): lax.all_to_all(tokens[deal_order].reshape(group_count, bucket_rows, model...  51.3 us
  transfers between devices with their start and end apart: 15, of which 10 were waited for; matrix products, arithmetic and copies ran while one was open for 24% of the time, Pallas kernels for 0%

commit v1 on v0

v1 whole, which is shorter than its diff:
```python
import functools
import math

import jax
import jax.numpy as jnp
from jax import lax
from jax.experimental import pallas as pl
from jax.experimental.pallas import tpu as pltpu
from jax.sharding import PartitionSpec as P

HEAD = 128
QH = 2


PRECISE = lax.Precision.HIGHEST
EPSILON = 1e-06
MASKED = -1e30


def half_turn(values):
    middle = values.shape[-1] // 2
    return jnp.concatenate([-values[..., middle:], values[..., :middle]], axis=-1)


def undo_turn(values, cosine, sine):
    return values * cosine - half_turn(values * sine)


def rotary_tables(lengths, tok_rows):
    seq_ends = jnp.cumsum(lengths)
    seq_starts = seq_ends - lengths
    places = jnp.arange(tok_rows, dtype=jnp.int32)
    segment = jnp.sum((places[:, None] >= seq_ends[None, :]).astype(jnp.int32), axis=1)
    matches = segment[:, None] == jnp.arange(lengths.shape[0], dtype=jnp.int32)[None, :]
    seq_first = jnp.sum(jnp.where(matches, seq_starts[None, :], 0), axis=1)
    offsets = (places - seq_first).astype(jnp.float32)
    frequency = jnp.exp(-math.log(10000.0) * jnp.arange(0, HEAD, 2, dtype=jnp.float32) / HEAD)
    angles = offsets[:, None] * frequency[None, :]
    angles = jnp.concatenate([angles, angles], axis=1)
    return (segment, jnp.cos(angles)[:, None, :], jnp.sin(angles)[:, None, :])


def pair_gates(logits, routes):
    columns = logits.shape[1]
    chosen_mask = (
        routes[:, :, None] == jnp.arange(columns, dtype=jnp.int32)[None, None, :]
    ).astype(jnp.float32)
    picked = jnp.sum(chosen_mask * logits[:, None, :], axis=2)
    return (jax.nn.softmax(picked, axis=1), chosen_mask)


def pair_back(gates, chosen_mask, gate_grads):
    inner = gates * (gate_grads - jnp.sum(gates * gate_grads, axis=1, keepdims=True))
    return jnp.sum(chosen_mask * inner[:, :, None], axis=1)


def slot_table(routes, priority, capacity):
    target = routes.reshape(-1)
    ahead = (target[None, :] == target[:, None]) & (priority[None, :] < priority[:, None])
    position = jnp.sum(ahead.astype(jnp.int32), axis=1)
    return (target, position, position < capacity)


def norm_stats(values, gain):
    factor = lax.rsqrt(jnp.mean(values * values, axis=1, keepdims=True) + EPSILON)
    scaled = values * factor
    return (factor, scaled, scaled * gain)


def block_scores(query, keys, segment, start, block_rows, scale):
    places = jnp.arange(keys.shape[0], dtype=jnp.int32)
    allowed = (segment[start : start + block_rows, None] == segment[None, :]) & (
        places[:, None] >= places[None, :]
    )
    raw = jnp.einsum("qhd,khd->hqk", query, keys, preferred_element_type=jnp.float32) * scale
    return jnp.where(allowed[None], raw, MASKED)


MESH = pl.DeviceIdType.MESH
MIB = 1 << 20


def flip(number, other, count):
    total, bit = 0, 1
    while bit < count:
        total = total + lax.rem(lax.div(number, bit) + lax.div(other, bit), 2) * bit
        bit *= 2
    return total


def dot_nt(left, right):
    return lax.dot_general(
        left, right, (((1,), (1,)), ((), ())), preferred_element_type=jnp.float32
    )


class Place:
    def __init__(self):
        self.groups = lax.axis_size("expert")
        self.parts = lax.axis_size("tensor")
        self.spots = self.parts // 2
        self.expert = lax.axis_index("expert")
        self.tensor = lax.axis_index("tensor")
        self.spot = lax.div(self.tensor, 2)
        self.core = lax.rem(self.tensor, 2)

    def device(self, expert, tensor):
        return {"expert": expert, "tensor": tensor}

    def across(self, step):
        return lax.rem(self.spot + step, self.spots) * 2 + self.core

    def before(self, step):
        return lax.rem(self.spot + self.spots - step, self.spots) * 2 + self.core

    def meet(self, over_expert):
        peers = [self.device(self.expert, self.spot * 2 + 1 - self.core)]
        for step in range(1, self.spots):
            peers.append(self.device(self.expert, self.across(step)))
        if over_expert:
            for step in range(1, self.groups):
                peers.append(self.device(flip(self.expert, step, self.groups), self.tensor))
        barrier = pltpu.get_barrier_semaphore()
        for peer in peers:
            pl.semaphore_signal(barrier, inc=1, device_id=peer, device_id_type=MESH)
        pl.semaphore_wait(barrier, len(peers))


def remote(source, target, send, receive, device):
    return pltpu.make_async_remote_copy(
        src_ref=source,
        dst_ref=target,
        send_sem=send,
        recv_sem=receive,
        device_id=device,
        device_id_type=MESH,
    )


class Spread:
    @staticmethod
    def scratch(chunks, spots):
        return [
            pltpu.SemaphoreType.DMA((chunks,)),
            pltpu.SemaphoreType.DMA((chunks,)),
            pltpu.SemaphoreType.DMA((chunks, max(spots - 1, 1))),
            pltpu.SemaphoreType.DMA((chunks, max(spots - 1, 1))),
            pltpu.SemaphoreType.DMA((chunks, spots)),
            pltpu.SemaphoreType.DMA((chunks, spots)),
        ]

    def __init__(self, place, source, target, sems, over_expert, sharers=1):
        self.place, self.source, self.target = place, source, target
        self.first_send, self.first_land, self.side_send, self.side_land, self.core_send, self.core_land = sems
        self.over_expert, self.sharers = over_expert, sharers
        self.width = source.shape[3]
        self.chunks = target.shape[1]

    def owner(self, chunk):
        if self.over_expert:
            return flip(self.place.expert, chunk, self.place.groups)
        return chunk

    def spot_of(self, owner, tensor):
        first = pl.multiple_of(tensor * self.width, 128)
        return self.target.at[:, owner, :, pl.ds(first, self.width)]

    def block(self, owner):
        if self.sharers == 1:
            return self.source.at[:, owner]
        return self.source.at[:, lax.div(owner, self.sharers)]

    def start(self):
        place = self.place
        own = self.owner(0)
        if not self.over_expert:
            return
        for chunk in range(1, self.chunks):
            peer = self.owner(chunk)
            remote(
                self.block(peer),
                self.spot_of(place.expert, place.tensor),
                self.first_send.at[chunk],
                self.first_land.at[chunk],
                place.device(peer, place.tensor),
            ).start()
        copy = pltpu.make_async_copy(
            self.block(own), self.spot_of(own, place.tensor), self.first_send.at[0]
        )
        copy.start()
        copy.wait()

    def first(self, chunk):
        place = self.place
        owner = self.owner(chunk)
        mine = self.spot_of(owner, place.tensor)
        if self.over_expert:

            @pl.when(chunk > 0)
            def _():
                remote(
                    self.block(owner),
                    mine,
                    self.first_send.at[chunk],
                    self.first_land.at[chunk],
                    place.device(owner, place.tensor),
                ).wait_recv()

            held = mine
        else:
            pltpu.make_async_copy(self.block(owner), mine, self.first_send.at[chunk]).start()
            held = self.block(owner)
        for step in range(1, place.spots):
            remote(
                held,
                mine,
                self.side_send.at[chunk, step - 1],
                self.side_land.at[chunk, step - 1],
                place.device(place.expert, place.across(step)),
            ).start()
        remote(
            held,
            mine,
            self.core_send.at[chunk, 0],
            self.core_land.at[chunk, 0],
            place.device(place.expert, place.spot * 2 + 1 - place.core),
        ).start()

    def second(self, chunk):
        place = self.place
        owner = self.owner(chunk)
        for step in range(1, place.spots):
            came = self.spot_of(owner, place.before(step))
            remote(
                came,
                came,
                self.side_send.at[chunk, step - 1],
                self.side_land.at[chunk, step - 1],
                place.device(place.expert, place.across(step)),
            ).wait_recv()
            remote(
                came,
                came,
                self.core_send.at[chunk, step],
                self.core_land.at[chunk, step],
                place.device(place.expert, place.spot * 2 + 1 - place.core),
            ).start()

    def third(self, chunk):
        place = self.place
        owner = self.owner(chunk)
        flipped = 1 - 2 * place.core
        for step in range(place.spots):
            came = self.spot_of(owner, place.before(step) + flipped)
            remote(
                came,
                came,
                self.core_send.at[chunk, step],
                self.core_land.at[chunk, step],
                place.device(place.expert, place.spot * 2 + 1 - place.core),
            ).wait_recv()

    def finish(self, chunk):
        place = self.place
        owner = self.owner(chunk)
        mine = self.spot_of(owner, place.tensor)
        device = place.device(place.expert, place.tensor)
        if self.over_expert:

            @pl.when(chunk > 0)
            def _():
                remote(
                    self.block(owner),
                    mine,
                    self.first_send.at[chunk],
                    self.first_land.at[chunk],
                    device,
                ).wait_send()

        else:
            pltpu.make_async_copy(self.block(owner), mine, self.first_send.at[chunk]).wait()
        for step in range(1, place.spots):
            remote(
                mine,
                mine,
                self.side_send.at[chunk, step - 1],
                self.side_land.at[chunk, step - 1],
                device,
            ).wait_send()
        for step in range(place.spots):
            remote(
                mine, mine, self.core_send.at[chunk, step], self.core_land.at[chunk, step], device
            ).wait_send()


class Collect:
    @staticmethod
    def scratch(chunks, kinds, spots, rows, width):
        return [
            pltpu.VMEM((2, kinds, spots, 2, rows, width), jnp.bfloat16),
            pltpu.VMEM((2, kinds, max(spots - 1, 1), rows, width), jnp.bfloat16),
            pltpu.VMEM((chunks, kinds, spots, rows, width), jnp.bfloat16),
            pltpu.VMEM((chunks, kinds, max(spots - 1, 1), rows, width), jnp.bfloat16),
            pltpu.SemaphoreType.DMA((chunks,)),
            pltpu.SemaphoreType.DMA((chunks,)),
            pltpu.SemaphoreType.DMA((chunks, max(spots - 1, 1))),
            pltpu.SemaphoreType.DMA((chunks, max(spots - 1, 1))),
        ]

    def __init__(self, place, refs):
        self.place = place
        self.stage, self.side, self.core_in, self.side_in = refs[:4]
        self.core_send, self.core_land, self.side_send, self.side_land = refs[4:]
        self.chunks = self.core_in.shape[0]

    def core_copy(self, chunk):
        place = self.place
        return remote(
            self.stage.at[lax.rem(chunk, 2), :, :, 1 - place.core],
            self.core_in.at[chunk],
            self.core_send.at[chunk],
            self.core_land.at[chunk],
            place.device(place.expert, place.spot * 2 + 1 - place.core),
        )

    def side_copy(self, chunk, step):
        place = self.place
        return remote(
            self.side.at[lax.rem(chunk, 2), :, step - 1],
            self.side_in.at[chunk, :, step - 1],
            self.side_send.at[chunk, step - 1],
            self.side_land.at[chunk, step - 1],
            place.device(place.expert, place.across(step)),
        )

    def free_stage(self, chunk):
        @pl.when(chunk >= 2)
        def _():
            self.core_copy(chunk - 2).wait_send()

    def first(self, chunk):
        self.core_copy(chunk).start()

    def second(self, chunk):
        place = self.place
        slot = lax.rem(chunk, 2)
        self.core_copy(chunk).wait_recv()

        @pl.when(chunk >= 2)
        def _():
            for step in range(1, place.spots):
                self.side_copy(chunk - 2, step).wait_send()

        for step in range(1, place.spots):
            there = lax.rem(place.spot + step, place.spots)
            total = self.stage[slot, :, there, place.core].astype(jnp.float32) + self.core_in[
                chunk, :, there
            ].astype(jnp.float32)
            self.side[slot, :, step - 1] = total.astype(jnp.bfloat16)
            self.side_copy(chunk, step).start()

    def third(self, chunk):
        place = self.place
        slot = lax.rem(chunk, 2)
        total = self.stage[slot, :, place.spot, place.core].astype(jnp.float32) + self.core_in[
            chunk, :, place.spot
        ].astype(jnp.float32)
        for step in range(1, place.spots):
            self.side_copy(chunk, step).wait_recv()
            total = total + self.side_in[chunk, :, step - 1].astype(jnp.float32)
        return total

    def finish(self):
        for chunk in range(max(self.chunks - 2, 0), self.chunks):
            self.core_copy(chunk).wait_send()
            for step in range(1, self.place.spots):
                self.side_copy(chunk, step).wait_send()


def when(condition, action, *args):
    pl.when(condition)(functools.partial(action, *args))


def spread_kernel(over_expert, source, target, *sems):
    place = Place()
    spread = Spread(place, source, target, sems, over_expert)
    place.meet(over_expert)
    spread.start()

    def step(turn, carry):
        when(turn < spread.chunks, spread.first, turn)
        when(turn >= 1, spread.second, turn - 1)
        return carry

    lax.fori_loop(0, spread.chunks + 1, step, 0)

    def last(turn, carry):
        spread.third(turn)
        spread.finish(turn)
        return carry

    lax.fori_loop(0, spread.chunks, last, 0)


def spread_rows(rows, over_expert, collective):
    chunks, count, width = rows.shape
    parts = lax.axis_size("tensor")
    full = pl.pallas_call(
        functools.partial(spread_kernel, over_expert),
        out_shape=jax.ShapeDtypeStruct((1, chunks, count, width * parts), rows.dtype),
        in_specs=[pl.BlockSpec(memory_space=pl.ANY)],
        out_specs=pl.BlockSpec(memory_space=pl.ANY),
        scratch_shapes=Spread.scratch(chunks, parts // 2),
        compiler_params=pltpu.CompilerParams(collective_id=collective, has_side_effects=True),
    )(rows[None])
    return full.reshape(chunks * count, width * parts)


def collect_kernel(make, operand_count, *refs):
    place = Place()
    operands = refs[:operand_count]
    result = refs[operand_count]
    collect = Collect(place, refs[operand_count + 1 :])
    place.meet(False)

    def one(chunk):
        collect.free_stage(chunk)
        slot = lax.rem(chunk, 2)
        width = result.shape[2]
        for spot in range(place.spots):
            for core in range(2):
                first = (spot * 2 + core) * width
                part = make(operands, chunk, first, width)
                collect.stage[slot, 0, spot, core] = part.astype(jnp.bfloat16)
        collect.first(chunk)

    def close(chunk):
        result[chunk] = collect.third(chunk)[0]

    def step(turn, carry):
        when(turn >= 2, close, turn - 2)
        when((turn >= 1) & (turn <= collect.chunks), collect.second, turn - 1)
        when(turn < collect.chunks, one, turn)
        return carry

    lax.fori_loop(0, collect.chunks + 2, step, 0)
    collect.finish()


def collect_rows(make, operands, chunks, rows, width, collective):
    parts = lax.axis_size("tensor")
    out = pl.pallas_call(
        functools.partial(collect_kernel, make, len(operands)),
        out_shape=jax.ShapeDtypeStruct((chunks, rows, width), jnp.float32),
        in_specs=[pl.BlockSpec(memory_space=pltpu.VMEM)] * len(operands),
        out_specs=pl.BlockSpec(memory_space=pltpu.VMEM),
        scratch_shapes=Collect.scratch(chunks, 1, parts // 2, rows, width),
        compiler_params=pltpu.CompilerParams(
            collective_id=collective, has_side_effects=True, vmem_limit_bytes=48 * MIB
        ),
    )(*operands)
    return out.reshape(chunks * rows, width)


def make_attended(span, operands, chunk, first, width):
    heads, gates, weight = operands
    total = None
    for expert in range(gates.shape[2]):
        term = gates[chunk, :, expert : expert + 1] * jnp.dot(
            heads[chunk, :, expert * span : (expert + 1) * span],
            weight[expert * span : (expert + 1) * span, first : first + width],
            preferred_element_type=jnp.float32,
        )
        total = term if total is None else total + term
    return total


def make_projected(operands, chunk, first, width):
    grads, weights = operands[:3], operands[3:]
    total = None
    for grad, weight in zip(grads, weights):
        term = dot_nt(grad[chunk], weight[first : first + width, :])
        total = term if total is None else total + term
    return total


def experts_kernel(sharers, *refs):
    (
        source, gate_hbm, up_hbm, down_hbm,
        inbox, middle_out, gate_out, up_out, returned,
        gate_w, up_w, down_w, rows, middle, gate_g, up_g, closing,
        load_sem, store_sem, back_send, back_land,
    ) = refs[:21]
    place = Place()
    spread = Spread(place, source, inbox, refs[21:27], True, sharers)
    collect = Collect(place, refs[27:])
    chunks = spread.chunks
    width = source.shape[3]
    units = gate_w.shape[1]
    tile = 704 if units % 704 == 0 else units
    loads = [
        pltpu.make_async_copy(held, kept, load_sem.at[number])
        for number, (held, kept) in enumerate(
            ((gate_hbm, gate_w), (up_hbm, up_w), (down_hbm, down_w))
        )
    ]
    for load in loads:
        load.start()
    place.meet(True)
    spread.start()

    def stores(owner):
        return [
            pltpu.make_async_copy(held, out.at[owner], store_sem.at[number])
            for number, (held, out) in enumerate(
                ((middle, middle_out), (gate_g, gate_out), (up_g, up_out))
            )
        ]

    def work(chunk):
        owner = spread.owner(chunk)
        slot = lax.rem(chunk, 2)
        spread.third(chunk)
        fetch = pltpu.make_async_copy(inbox.at[:, owner], rows, load_sem.at[3])
        fetch.start()

        @pl.when(chunk == 0)
        def _():
            for load in loads:
                load.wait()

        @pl.when(chunk > 0)
        def _():
            for store in stores(spread.owner(chunk - 1)):
                store.wait()

        collect.free_stage(chunk)
        fetch.wait()
        for first in range(0, units, tile):
            here = slice(first, first + tile)
            gate = jnp.dot(rows[0], gate_w[:, here], preferred_element_type=jnp.float32)
            up = jnp.dot(rows[0], up_w[:, here], preferred_element_type=jnp.float32)
            sig = jax.nn.sigmoid(gate)
            act = gate * sig
            middle[:, here] = (act * up).astype(jnp.bfloat16)
            grad = dot_nt(rows[1], down_w[here, :])
            gate_g[:, here] = (grad * up * sig * (1.0 + gate * (1.0 - sig))).astype(jnp.bfloat16)
            up_g[:, here] = (grad * act).astype(jnp.bfloat16)
        for store in stores(owner):
            store.start()
        for spot in range(place.spots):
            for core in range(2):
                first = (spot * 2 + core) * width
                here = slice(first, first + width)
                collect.stage[slot, 0, spot, core] = jnp.dot(
                    middle[...], down_w[:, here], preferred_element_type=jnp.float32
                ).astype(jnp.bfloat16)
                collect.stage[slot, 1, spot, core] = (
                    dot_nt(gate_g[...], gate_w[here, :]) + dot_nt(up_g[...], up_w[here, :])
                ).astype(jnp.bfloat16)
        collect.first(chunk)

    def back_copy(chunk):
        owner = spread.owner(chunk)
        return remote(
            closing.at[lax.rem(chunk, 2)],
            returned.at[:, place.expert],
            back_send.at[chunk],
            back_land.at[chunk],
            place.device(owner, place.tensor),
        )

    def close(chunk):
        slot = lax.rem(chunk, 2)
        total = collect.third(chunk)

        @pl.when(chunk >= 3)
        def _():
            back_copy(chunk - 2).wait_send()

        closing[slot] = total.astype(jnp.bfloat16)

        @pl.when(chunk > 0)
        def _():
            back_copy(chunk).start()

        @pl.when(chunk == 0)
        def _():
            own = pltpu.make_async_copy(
                closing.at[slot], returned.at[:, place.expert], back_send.at[chunk]
            )
            own.start()
            own.wait()

    def step(turn, carry):
        now = turn - 2
        when(turn < chunks, spread.first, turn)
        when((turn >= 1) & (turn <= chunks), spread.second, turn - 1)
        when(now >= 2, close, now - 2)
        when((now >= 1) & (now <= chunks), collect.second, now - 1)
        when((now >= 0) & (now < chunks), work, now)
        return carry

    lax.fori_loop(0, chunks + 4, step, 0)

    def last(turn, carry):
        spread.finish(turn)

        @pl.when(turn > 0)
        def _():
            owner = spread.owner(turn)
            remote(
                closing.at[0],
                returned.at[:, owner],
                back_send.at[turn],
                back_land.at[turn],
                place.device(owner, place.tensor),
            ).wait_recv()

        return carry

    lax.fori_loop(0, chunks, last, 0)
    for store in stores(spread.owner(chunks - 1)):
        store.wait()
    for chunk in range(max(chunks - 2, 1), chunks):
        back_copy(chunk).wait_send()
    collect.finish()


def experts(source, gate_w, up_w, down_w, sharers, collective):
    kinds, _, capacity, width = source.shape
    groups, parts = lax.axis_size("expert"), lax.axis_size("tensor")
    spots = parts // 2
    model_width, units = gate_w.shape
    low = jnp.bfloat16
    anywhere = pl.BlockSpec(memory_space=pl.ANY)
    hidden_rows = jax.ShapeDtypeStruct((groups, capacity, units), low)
    return pl.pallas_call(
        functools.partial(experts_kernel, sharers),
        out_shape=(
            jax.ShapeDtypeStruct((kinds, groups, capacity, model_width), low),
            hidden_rows,
            hidden_rows,
            hidden_rows,
            jax.ShapeDtypeStruct((kinds, groups, capacity, width), low),
        ),
        in_specs=[anywhere] * 4,
        out_specs=(anywhere,) * 5,
        scratch_shapes=[
            pltpu.VMEM((model_width, units), low),
            pltpu.VMEM((model_width, units), low),
            pltpu.VMEM((units, model_width), low),
            pltpu.VMEM((kinds, capacity, model_width), low),
            pltpu.VMEM((capacity, units), low),
            pltpu.VMEM((capacity, units), low),
            pltpu.VMEM((capacity, units), low),
            pltpu.VMEM((2, kinds, capacity, width), low),
            pltpu.SemaphoreType.DMA((4,)),
            pltpu.SemaphoreType.DMA((3,)),
            pltpu.SemaphoreType.DMA((groups,)),
            pltpu.SemaphoreType.DMA((groups,)),
        ]
        + Spread.scratch(groups, spots)
        + Collect.scratch(groups, kinds, spots, capacity, width),
        compiler_params=pltpu.CompilerParams(
            collective_id=collective, has_side_effects=True, vmem_limit_bytes=60 * MIB
        ),
    )(source, gate_w, up_w, down_w)


def to_expert(rows, group_count):
    count, width = rows.shape
    return lax.all_to_all(
        rows.reshape(group_count, count // group_count, width),
        "expert",
        split_axis=0,
        concat_axis=0,
        tiled=True,
    ).reshape(count, width)


def gather_tensor(rows):
    return lax.all_gather(rows, "tensor", axis=0)


def body(
    tokens,
    out_grad,
    attn_gain,
    attn_router,
    w_query,
    w_key,
    w_value,
    w_out,
    mlp_gain,
    mlp_router,
    w_gate,
    w_up,
    w_down,
    deal,
    seq_lengths,
    attn_routes,
    mlp_routes,
    slot_order,
):
    tok_rows, model_width = tokens.shape
    group_count = lax.axis_size("expert")
    part_count = lax.axis_size("tensor")
    group_index = lax.axis_index("expert")
    part_index = lax.axis_index("tensor")
    bucket_rows = tok_rows // group_count
    col_width = model_width // part_count
    col_first = part_index * col_width
    low = jnp.bfloat16

    def own_cols(values):
        return lax.dynamic_slice_in_dim(values, col_first, col_width, values.ndim - 1)

    deal_rank = deal // tok_rows * bucket_rows + (deal % tok_rows - group_index * bucket_rows)
    row_ids = jnp.arange(tok_rows, dtype=jnp.int32)
    deal_mask = (row_ids[:, None] == deal_rank[None, :]).astype(low)
    dealt = jnp.dot(deal_mask, own_cols(tokens), preferred_element_type=jnp.float32).astype(low)
    resid_low = spread_rows(dealt.reshape(group_count, bucket_rows, col_width), True, 0)
    grad_cols_low = to_expert(
        jnp.dot(deal_mask, own_cols(out_grad), preferred_element_type=jnp.float32).astype(low),
        group_count,
    )
    grad_cols = grad_cols_low.astype(jnp.float32)
    resid_in = resid_low.astype(jnp.float32)
    resid_cols = own_cols(resid_low).astype(jnp.float32)
    gain_one, gain_two = own_cols(attn_gain), own_cols(mlp_gain)
    router_one = lax.dynamic_slice_in_dim(attn_router, col_first, col_width, 0)
    router_two = lax.dynamic_slice_in_dim(mlp_router, col_first, col_width, 0)
    expert_count = mlp_router.shape[1]
    sharers = group_count // expert_count
    capacity = 5 * tok_rows // (2 * expert_count)
    target, position, kept = slot_table(mlp_routes, slot_order[0], capacity)
    slots = expert_count * capacity
    destination = jnp.where(kept, target * capacity + position, slots).reshape(tok_rows, 2)
    slot_ids = jnp.arange(slots, dtype=jnp.int32)
    chosen = [destination[:, way] for way in range(2)]
    to_slot = (
        (slot_ids[:, None] == chosen[0][None, :]) | (slot_ids[:, None] == chosen[1][None, :])
    ).astype(low)
    slot_grads = jnp.dot(to_slot, grad_cols_low, preferred_element_type=jnp.float32)

    segment, cosine, sine = rotary_tables(seq_lengths[0], tok_rows)
    scale = 1.0 / math.sqrt(HEAD)
    local_heads = w_query.shape[1] // HEAD
    local_experts = local_heads // QH
    span = QH * HEAD
    factor_one, scaled_one, normed_one = norm_stats(resid_in, attn_gain)
    normed_low = normed_one.astype(low)
    attn_logits = jnp.dot(normed_one, attn_router, precision=PRECISE)
    attn_gates, attn_mask = pair_gates(attn_logits, attn_routes)
    gate_table = jnp.sum(attn_gates[:, :, None] * attn_mask, axis=1)
    gate_local = lax.dynamic_slice_in_dim(gate_table, part_index * local_experts, local_experts, 1)
    query_pre = jnp.dot(normed_low, w_query, preferred_element_type=jnp.float32).reshape(
        tok_rows, local_heads, HEAD
    )
    key_pre = jnp.dot(normed_low, w_key, preferred_element_type=jnp.float32).reshape(
        tok_rows, local_heads, HEAD
    )
    values = (
        jnp.dot(normed_low, w_value, preferred_element_type=jnp.float32)
        .astype(low)
        .reshape(tok_rows, local_heads, HEAD)
    )
    query = (query_pre * cosine + half_turn(query_pre) * sine).astype(low)
    keys = (key_pre * cosine + half_turn(key_pre) * sine).astype(low)
    scores = block_scores(query, keys, segment, 0, tok_rows, scale)
    top_score = jnp.max(scores, axis=-1, keepdims=True)
    expo = jnp.exp(scores - top_score)
    totals = jnp.sum(expo, axis=-1, keepdims=True)
    probs = (expo / totals).astype(low)
    head_blocks = jnp.einsum("hqk,khd->qhd", probs, values, preferred_element_type=jnp.float32)
    log_total = top_score + jnp.log(totals)
    heads_low = head_blocks.astype(low).reshape(tok_rows, local_heads * HEAD)
    pieces, piece_rows = 4, tok_rows // 4
    attn_cols = collect_rows(
        functools.partial(make_attended, span),
        (
            heads_low.reshape(pieces, piece_rows, local_heads * HEAD),
            gate_local.reshape(pieces, piece_rows, local_experts),
            w_out,
        ),
        pieces,
        piece_rows,
        col_width,
        1,
    )
    hidden = resid_cols + attn_cols
    weighed = hidden * gain_two
    stats = jnp.concatenate(
        [
            jnp.sum(hidden * hidden, axis=1)[None, :],
            jnp.dot(weighed, router_two, precision=PRECISE).T,
        ],
        axis=0,
    )
    stats = jnp.sum(gather_tensor(stats), axis=0)
    factor_two = lax.rsqrt(stats[0] / model_width + EPSILON)[:, None]
    mlp_logits = stats[1:].T * factor_two
    scaled_two = hidden * factor_two
    normed_two = scaled_two * gain_two
    mlp_gates, mlp_mask = pair_gates(mlp_logits, mlp_routes)
    slot_rows = jnp.dot(
        to_slot, normed_two.astype(low), preferred_element_type=jnp.float32
    ).astype(low)
    slot_gates = sum(
        jnp.sum(
            jnp.where(slot_ids[:, None] == chosen[way][None, :], mlp_gates[:, way][None, :], 0.0),
            axis=1,
        )
        for way in range(2)
    )
    slot_grads = (slot_gates[:, None] * slot_grads).astype(low)
    inbox, middle, gate_grad, up_grad, returned = experts(
        jnp.stack([slot_rows, slot_grads]).reshape(2, expert_count, capacity, col_width),
        w_gate[0],
        w_up[0],
        w_down[0],
        sharers,
        2,
    )
    if sharers > 1:
        returned = (
            jnp.sum(
                returned.reshape(2, expert_count, sharers, capacity, col_width).astype(jnp.float32),
                axis=2,
            )
        ).astype(low)
    made, row_grads = returned.reshape(2, slots, col_width)
    from_slot = [(chosen[way][:, None] == slot_ids[None, :]).astype(low) for way in range(2)]
    pair_values = jnp.stack(
        [
            jnp.dot(from_slot[way], made, preferred_element_type=jnp.float32)
            for way in range(2)
        ],
        axis=1,
    )
    row_grad_sum = jnp.dot(
        from_slot[0] + from_slot[1], row_grads, preferred_element_type=jnp.float32
    )
    mixed_cols = hidden + jnp.sum(mlp_gates[:, :, None] * pair_values, axis=1)
    back_mixed = to_expert(mixed_cols.astype(low), group_count)
    weighed_two = scaled_two * gain_two
    stats = jnp.stack(
        [
            jnp.sum(pair_values[:, 0] * grad_cols, axis=1),
            jnp.sum(pair_values[:, 1] * grad_cols, axis=1),
            jnp.sum(row_grad_sum * weighed_two, axis=1),
        ]
    )
    stats = jnp.sum(gather_tensor(stats), axis=0)
    mlp_logit_grad = pair_back(mlp_gates, mlp_mask, stats[:2].T)
    norm_two_grad = row_grad_sum + jnp.dot(mlp_logit_grad, router_two.T, precision=PRECISE)
    mlp_router_grad = jnp.dot(normed_two.T, mlp_logit_grad, precision=PRECISE)
    mlp_gain_grad = jnp.sum(norm_two_grad * scaled_two, axis=0)
    mean_two = (stats[2] + jnp.sum(mlp_logit_grad * mlp_logits, axis=1)) / model_width
    hidden_grad = grad_cols + factor_two * (norm_two_grad * gain_two - scaled_two * mean_two[:, None])
    hidden_grad_low = spread_rows(
        hidden_grad.astype(low).reshape(pieces, piece_rows, col_width), False, 3
    )
    gate_wide = jnp.repeat(gate_local, span, axis=1)
    heads_float = heads_low.astype(jnp.float32)
    out_w_grad = jnp.einsum(
        "tc,td->cd",
        (heads_float * gate_wide).astype(low),
        hidden_grad_low,
        preferred_element_type=jnp.float32,
    )
    heads_plain = jnp.einsum(
        "td,cd->tc", hidden_grad_low, w_out, preferred_element_type=jnp.float32
    )
    local_gate_grad = jnp.sum(
        (heads_plain * heads_float).reshape(tok_rows, local_experts, span), axis=2
    )
    heads_grad = (heads_plain * gate_wide).astype(low).reshape(tok_rows, local_heads, HEAD)
    scores = block_scores(query, keys, segment, 0, tok_rows, scale)
    probs = jnp.exp(scores - log_total)
    value_grad = jnp.einsum(
        "hqk,qhd->khd", probs.astype(low), heads_grad, preferred_element_type=jnp.float32
    )
    prob_grad = jnp.einsum("qhd,khd->hqk", heads_grad, values, preferred_element_type=jnp.float32)
    score_grad = (
        probs * (prob_grad - jnp.sum(probs * prob_grad, axis=-1, keepdims=True))
    ).astype(low)
    query_grad = (
        jnp.einsum("hqk,khd->qhd", score_grad, keys, preferred_element_type=jnp.float32) * scale
    )
    key_grad = (
        jnp.einsum("hqk,qhd->khd", score_grad, query, preferred_element_type=jnp.float32) * scale
    )
    width = local_heads * HEAD
    query_pre_grad = undo_turn(query_grad, cosine, sine).astype(low).reshape(tok_rows, width)
    key_pre_grad = undo_turn(key_grad, cosine, sine).astype(low).reshape(tok_rows, width)
    value_pre_grad = value_grad.astype(low).reshape(tok_rows, width)
    weight_grads = [
        jnp.einsum("td,tc->dc", normed_low, grad, preferred_element_type=jnp.float32)
        for grad in (query_pre_grad, key_pre_grad, value_pre_grad)
    ]
    norm_one_cols = collect_rows(
        make_projected,
        tuple(
            grad.reshape(pieces, piece_rows, width)
            for grad in (query_pre_grad, key_pre_grad, value_pre_grad)
        )
        + (w_query, w_key, w_value),
        pieces,
        piece_rows,
        col_width,
        4,
    )
    scaled_cols = resid_cols * factor_one
    normed_cols = scaled_cols * gain_one
    stats = jnp.concatenate(
        [jnp.sum(norm_one_cols * normed_cols, axis=1)[None, :], local_gate_grad.T], axis=0
    )
    stats = gather_tensor(stats)
    gate_grads = stats[:, 1:].reshape(part_count * local_experts, tok_rows).T
    attn_pair_grad = jnp.sum(attn_mask * gate_grads[:, None, :], axis=2)
    attn_logit_grad = pair_back(attn_gates, attn_mask, attn_pair_grad)
    norm_one_grad = norm_one_cols + jnp.dot(attn_logit_grad, router_one.T, precision=PRECISE)
    attn_router_grad = jnp.dot(normed_cols.T, attn_logit_grad, precision=PRECISE)
    attn_gain_grad = jnp.sum(norm_one_grad * scaled_cols, axis=0)
    mean_one = (
        jnp.sum(stats[:, 0], axis=0) + jnp.sum(attn_logit_grad * attn_logits, axis=1)
    ) / model_width
    input_cols = hidden_grad + factor_one * (
        norm_one_grad * gain_one - scaled_cols * mean_one[:, None]
    )
    back_grad = to_expert(input_cols.astype(low), group_count)
    mixed, tokens_grad = (
        jnp.einsum("ri,rc->ic", deal_mask, back, preferred_element_type=jnp.float32).astype(low)
        for back in (back_mixed, back_grad)
    )
    out_w_grad = lax.psum(out_w_grad.astype(low), "expert").astype(jnp.float32)
    weight_grads = [
        grad.astype(jnp.float32)
        for grad in lax.psum(tuple(grad.astype(low) for grad in weight_grads), "expert")
    ]
    small = jnp.concatenate(
        [attn_gain_grad[None], attn_router_grad.T, mlp_gain_grad[None], mlp_router_grad.T], axis=0
    )
    small = gather_tensor(lax.psum(small, "expert"))
    small = small.transpose(1, 0, 2).reshape(-1, model_width)
    experts_of = attn_router.shape[1]
    rows = inbox.reshape(2, -1, model_width)
    units = middle.shape[2]
    gate_w_grad, up_w_grad = (
        jnp.einsum("sd,sf->df", rows[0], grad.reshape(-1, units), preferred_element_type=jnp.float32)
        for grad in (gate_grad, up_grad)
    )
    down_grad = jnp.einsum(
        "sf,sd->fd", middle.reshape(-1, units), rows[1], preferred_element_type=jnp.float32
    )
    return (
        mixed,
        tokens_grad,
        small[0],
        small[1 : 1 + experts_of].T,
        weight_grads[0],
        weight_grads[1],
        weight_grads[2],
        out_w_grad,
        small[1 + experts_of],
        small[2 + experts_of :].T,
        gate_w_grad[None],
        up_w_grad[None],
        down_grad[None],
    )


def solution(mesh):
    placed = (
        P("expert", None),
        P("expert", None),
        P(),
        P(),
        P(None, "tensor"),
        P(None, "tensor"),
        P(None, "tensor"),
        P("tensor", None),
        P(),
        P(),
        P("expert", None, "tensor"),
        P("expert", None, "tensor"),
        P("expert", "tensor", None),
        P("expert"),
        P("expert", None),
        P("expert", None),
        P("expert", None),
        P("expert", None),
    )
    return jax.shard_map(
        body,
        mesh=mesh,
        in_specs=placed,
        out_specs=(
            P("expert", "tensor"),
            P("expert", "tensor"),
            P(),
            P(),
            P(None, "tensor"),
            P(None, "tensor"),
            P(None, "tensor"),
            P("tensor", None),
            P(),
            P(),
            P("expert", None, "tensor"),
            P("expert", None, "tensor"),
            P("expert", "tensor", None),
        ),
        check_vma=False,
    )
```

time: 1610 us -> 921 us (0.57)
  waiting for transfers between devices: 956 us -> 152 us
  Pallas kernels: 0 us -> 368 us
  matrix products: 286 us -> 157 us
  local copies, waits for them, and re-layouts: 158 us -> 66.6 us
  blocking collectives: 19.4 us -> 81.7 us
  other arithmetic: 115 us -> 53 us
  starting transfers between devices: 53 us -> 17.2 us
    all_to_all x8 -> x3, waiting for transfers between devices: 375 us -> 0.01 us  [to_expert(): lax.all_to_all(rows.reshape(group_count, count // group_count, width), 'e...]
    pallas_call x0 -> x5, Pallas kernels: none -> 368 us  [the longest x1 249 us: experts(): pl.pallas_call(functools.partial(experts_kernel, sharers), out_shape=(jax...]
    psum x4 -> x1, waiting for transfers between devices: 425 us -> 152 us  [body(): lax.psum(tuple((grad.astype(low) for grad in weight_grads)), 'expert')]
    reduce_scatter x2 -> x0, waiting for transfers between devices: 156 us -> none  [return_rows(): lax.psum_scatter(partial_rows, 'tensor', scatter_dimension=1, tiled=True)]
    dot_general x28 -> x24, matrix products: 256 us -> 134 us  [the longest x2 37.3 us: body(): jnp.einsum('sd,sf->df', rows[0], grad.reshape(-1, units), preferred_eleme...]
    gather x11 -> x0, local copies, waits for them, and re-layouts: 90.4 us -> none  [the longest x1 18.6 us: body(): grads_ext[owner_token]]
    psum x1, blocking collectives: 14.2 us -> 60 us  [body(): small = gather_tensor(lax.psum(small, 'expert'))]
    all_to_all x8 -> x3, starting transfers between devices: 52.5 us -> 17.2 us  [to_expert(): lax.all_to_all(rows.reshape(group_count, count // group_count, width), 'e...]
  transfers between devices with their start and end apart: 15 -> 4, of which waited for: 10 -> 1; matrix products, arithmetic and copies ran while one was open for 24% -> 18% of each run, Pallas kernels for 0% -> 7%
where the time goes in v1:
time: 921 us; the launch traced here: 910 us
  Pallas kernels  368 us (40%)
  matrix products  157 us (17%)
  waiting for transfers between devices  152 us (17%)
  blocking collectives  81.7 us (9%)
  local copies, waits for them, and re-layouts  66.6 us (7%)
  other arithmetic  53 us (6%)
  starting transfers between devices  17.2 us (2%)
  between operations  15.5 us (2%)
    pallas_call x1, Pallas kernels, experts(): pl.pallas_call(functools.partial(experts_kernel, sharers), out_shape=(jax...  249 us
    psum x1, waiting for transfers between devices, body(): lax.psum(tuple((grad.astype(low) for grad in weight_grads)), 'expert')  152 us
    pallas_call x2, Pallas kernels, spread_rows(): pl.pallas_call(functools.partial(spread_kernel, over_expert), out_shape=j...  63 us
    psum x1, blocking collectives, body(): small = gather_tensor(lax.psum(small, 'expert'))  60 us
    pallas_call x2, Pallas kernels, collect_rows(): pl.pallas_call(functools.partial(collect_kernel, make, len(operands)), ou...  56.3 us
    dot_general x2, matrix products, body(): jnp.einsum('sd,sf->df', rows[0], grad.reshape(-1, units), preferred_eleme...  37.3 us
    all_gather x4, blocking collectives, gather_tensor(): return lax.all_gather(rows, 'tensor', axis=0)  21.7 us
    dot_general x1, matrix products, body(): jnp.einsum('sf,sd->fd', middle.reshape(-1, units), rows[1], preferred_ele...  19 us
  transfers between devices with their start and end apart: 4, of which 1 were waited for; matrix products, arithmetic and copies ran while one was open for 18% of the time, Pallas kernels for 7%

profile of v1, /device:TPU:20, one launch (start us, length us, event | category | flops | bytes accessed | tf_op | source)
XLA Modules:
  0.0 910.4 jit_solution(4840695097328188155)
XLA Ops:
  10.8 6.1 all-to-all-start
  18.9 2.8 fusion.77
  21.7 36.5 %shard_map.273 = bf16[1,8,96,2048]{3,2,1,0:T(8,128)(2,1)} custom-call(bf16[1,8,96,512]{3,2,1,0:T(8,128)(2,1)} %bitcast.201), custom_call_target="tpu_custom_call" | custom-call | tf_op jit(solution)/shard_map/pallas_call | solution.py:408
  58.2 2.7 fusion.2
  61.1 3.1 fusion.4
  74.2 4.1 copy.210
  78.3 2.6 copy.209
  82.1 7.7 fusion.5
  90.1 5.5 fusion.81
  96.8 4.5 fusion.132
  109.5 2.9 fusion.130
  117.8 25.5 %shard_map.274 = f32[4,192,512]{2,1,0:T(8,128)S(1)} custom-call(bf16[4,192,512]{2,1,0:T(8,128)(2,1)S(1)} %reshape_reshape.12.refs_0_, f32[4,192,2]{2,1,0:T(8,128)S(1)} %bitcast.159, bf16[512,2048]{1,0:T(8,128)(2,1)S(1)} %copy-done.7), custom_call_target="tpu_custom_call" | custom-call | tf_op jit(solution)/shard_map/pallas_call | solution.py:452
  144.4 3.1 copy.176
  151.4 5.6 all-gather.3
  161.0 3.2 fusion.29
  165.6 3.4 multiply_convert_fusion.1
  171.3 248.7 %shard_map.275 = (bf16[2,8,240,2048]{3,2,1,0:T(8,128)(2,1)}, bf16[8,240,1408]{2,1,0:T(8,128)(2,1)}, bf16[8,240,1408]{2,1,0:T(8,128)(2,1)}, bf16[8,240,1408]{2,1,0:T(8,128)(2,1)}, bf16[2,8,240,512]{3,2,1,0:T(8,128)(2,1)}) custom-call(bf16[2,8,240,512]{3,2,1,0:T(8,128)(2,1)} %pad_maximum_fusion.refs_0_, bf16[2048,1408]{1,0:T(8,128)(2,1)} %bitcast.171, ...), custom_call_target="tpu_custom_call" | custom-call | tf_op jit(solution)/shard_map/pallas_call | solution.py:638
  422.6 3.7 multiply_reduce_fusion.2
  428.4 3.4 fusion.61
  431.9 5.2 all-gather.4
  437.3 5.0 fusion.124
  444.6 26.5 %shard_map.276 = bf16[1,4,192,2048]{3,2,1,0:T(8,128)(2,1)} custom-call(bf16[1,4,192,512]{3,2,1,0:T(8,128)(2,1)} %bitcast.183), custom_call_target="tpu_custom_call" | custom-call | tf_op jit(solution)/shard_map/pallas_call | solution.py:408
  471.1 4.5 bitcast_reduce_fusion
  475.8 6.4 fusion.74
  482.3 4.8 multiply_reduce_fusion
  489.8 10.3 %multiply_convert_fusion = bf16[4,768,768]{1,2,0:T(8,128)(2,1)} fusion(f32[4,768,768]{1,2,0:T(8,128)} %get-tuple-element.75, f32[4,768,768]{1,2,0:T(8,128)} %copy-done.8, f32[4,768]{1,0:T(4,128)S(1)} %get-tuple-element.74, f32[4,768]{1,0:T(4,128)S(1)} %log_add_fusion), kind=kLoop, calls=%fused_computation | loop fusion | flops 9437184 | bytes 23617536 | tf_op jit(solution)/shard_map/convert_element_type | solution.py:888
  500.1 3.5 fusion.133
  517.8 30.8 %shard_map.277 = f32[4,192,512]{2,1,0:T(8,128)S(1)} custom-call(bf16[4,192,512]{2,1,0:T(8,128)(2,1)S(1)} %reshape_reshape.13.refs_0_, bf16[4,192,512]{2,1,0:T(8,128)(2,1)S(1)} %copy-done.6, bf16[4,192,512]{2,1,0:T(8,128)(2,1)S(1)} %copy-done.5, bf16[2048,512]{1,0:T(8,128)(2,1)S(1)} %copy-done.2, bf16[2048,512]{1,0:T(8,128)(2,1)} %refs_4_.1, ...), custom_call_target="tpu_custom_call" | custom-call | tf_op jit(solution)/shard_map/pallas_call | solution.py:452
  552.1 5.2 all-gather.5
  557.4 5.0 convolution_convert_fusion
  565.9 4.4 multiply_reduce_fusion.1
  572.7 5.1 all-to-all-start.2
  577.9 5.2 convolution_convert_fusion.1
  583.1 3.2 convolution_convert_fusion.3
  586.3 3.2 convolution_convert_fusion.2
  589.6 11.6 %fusion.125 = (bf16[1,8,240,2048]{3,2,1,0:T(8,128)(2,1)}, bf16[1,8,240,2048]{3,2,1,0:T(8,128)(2,1)}) fusion(bf16[2,8,240,2048]{3,2,1,0:T(8,128)(2,1)} %get-tuple-element.19), kind=kLoop, calls=%fused_computation.218 | loop fusion | bytes 31457280 | tf_op jit(solution)/shard_map/slice | solution.py:956
  601.2 18.7 %convolution_bitcast_fusion = f32[1,2048,1408]{2,1,0:T(8,128)} fusion(bf16[1920,2048]{1,0:T(8,128)(2,1)} %bitcast.167, bf16[1920,1408]{1,0:T(8,128)(2,1)} %bitcast.215), kind=kOutput, calls=%fused_computation.7 | convolution fusion | flops 11072962560 | bytes 24805376 | tf_op jit(solution)/shard_map/sd,sf->df/dot_general | solution.py:952
  621.1 18.7 %convolution_bitcast_fusion.1 = f32[1,2048,1408]{2,1,0:T(8,128)} fusion(bf16[1920,2048]{1,0:T(8,128)(2,1)} %bitcast.168, bf16[1920,1408]{1,0:T(8,128)(2,1)} %bitcast.214), kind=kOutput, calls=%fused_computation.8 | convolution fusion | flops 11072962560 | bytes 24805376 | tf_op jit(solution)/shard_map/sd,sf->df/dot_general | solution.py:952
  639.7 19.0 %convolution_bitcast_fusion.2 = f32[1,1408,2048]{2,1,0:T(8,128)} fusion(bf16[1920,1408]{1,0:T(8,128)(2,1)} %bitcast.213, bf16[1920,2048]{1,0:T(8,128)(2,1)} %bitcast.166), kind=kOutput, calls=%fused_computation.9 | convolution fusion | flops 11072962560 | bytes 24805376 | tf_op jit(solution)/shard_map/sf,sd->fd/dot_general | solution.py:955
  658.7 6.0 all-to-all-start.1
  667.6 60.0 %psum.35 = f32[1,18,512]{2,1,0:T(8,128)S(1)} all-reduce(f32[1,18,512]{2,1,0:T(8,128)S(1)} %maximum_bitcast_fusion.1), channel_id=1, replica_groups=mesh['expert'=8,'tensor'=4] {'expert'}, use_global_device_ids=true, to_apply=%region_36.37 | all-reduce | flops 9216 | bytes 73728 | tf_op jit(solution)/shard_map/psum | solution.py:946
  727.6 5.6 all_gather.31
  734.4 2.9 fusion.80
  739.0 151.7 %all-reduce.3.cloned.1.call-done = (bf16[2048,512]{1,0:T(8,128)(2,1)}, bf16[2048,512]{1,0:T(8,128)(2,1)}, bf16[2048,512]{1,0:T(8,128)(2,1)}, bf16[512,2048]{1,0:T(8,128)(2,1)}) async-done(((bf16[2048,512]{1,0:T(8,128)(2,1)}, bf16[2048,512]{1,0:T(8,128)(2,1)}, bf16[2048,512]{1,0:T(8,128)(2,1)}, bf16[512,2048]{1,0:T(8,128)(2,1)}), (bf16[2048,512]{1,0:T(8,128)(2,1)}, bf16[2048,512]{1,0:T(8,128)(2,1)}, ...) | async-done | bytes 8388624 | tf_op jit(solution)/shard_map/psum | solution.py:941
  890.7 4.3 convert_element_type.213
  895.0 2.6 convert_element_type.215
  897.6 2.6 convert_element_type.217
  900.3 2.5 convert_element_type.223
  (244 shorter events, 85.3 us)
Async XLA Ops:
  9.1 8.3 copy-start.50
  10.8 153.5 %all-to-all-start = ((bf16[8,96,512]{2,1,0:T(8,128)(2,1)}), bf16[8,96,512]{2,1,0:T(8,128)(2,1)}, u32[]{:S(2)}, u32[]{:S(2)}) async-start(bf16[8,96,512]{2,1,0:T(8,128)(2,1)} %bitcast.198), calls=%async_computation | async-start | bytes 1572864 | tf_op jit(solution)/shard_map/all_to_all | solution.py:673
  58.2 2.8 copy-start.14
  61.1 21.0 %copy-start.54 = (f32[768]{0:T(1024)}, f32[768]{0:T(1024)S(1)}, u32[]{:S(2)}) copy-start(f32[768]{0:T(1024)S(1)} %rsqrt.23) | copy-start | bytes 9220
  64.2 7.5 copy-start.62
  66.5 370.8 %copy-start.52 = (f32[512]{0:T(512)}, f32[512]{0:T(512)S(1)}, u32[]{:S(2)}) copy-start(f32[512]{0:T(512)S(1)} %dynamic_slice.28) | copy-start | bytes 6148
  74.2 4.1 copy-start.2
  78.3 3.8 copy-start.58
  78.3 3.8 copy-start.59
  82.1 7.7 copy-start.46
  89.8 5.8 copy-start.48
  96.8 4.5 copy-start.27
  96.8 4.5 copy-start.35
  104.9 2.8 copy-start.21
  104.9 2.8 copy-start.23
  107.7 4.6 copy-start.8
  144.4 3.1 copy-start.15
  147.5 2.8 copy-start.57
  149.2 7.8 copy-start.51
  157.1 3.9 copy-start.11
  165.6 271.6 %copy-start.19 = (bf16[768,512]{0,1:T(8,128)(2,1)}, bf16[768,512]{0,1:T(8,128)(2,1)S(1)}, u32[]{:S(2)}) copy-start(bf16[768,512]{0,1:T(8,128)(2,1)S(1)} %copy.181) | copy-start | bytes 2359300
  165.6 3.4 copy-start.36
  428.4 3.4 copy-start.41
  444.6 26.5 %copy-start.44 = (bf16[768,4,128]{0,2,1:T(8,128)(2,1)S(1)}, bf16[768,4,128]{0,2,1:T(8,128)(2,1)}, u32[]{:S(2)}) copy-start(bf16[768,4,128]{0,2,1:T(8,128)(2,1)} %get-tuple-element.78) | copy-start | bytes 2359300
  471.1 11.1 %slice-start = ((s8[9437184]{0:T(1024)(128)(4,1)}), s8[4194304]{0:T(1024)(128)(4,1)S(1)}, s32[]{:S(2)}) async-start(s8[9437184]{0:T(1024)(128)(4,1)} %bitcast.160), calls=%async_computation.4 | async-start | bytes 8388608
  471.1 11.1 %slice-start.1 = ((s8[9437184]{0:T(1024)(128)(4,1)}), s8[4194304]{0:T(1024)(128)(4,1)S(1)}, s32[]{:S(2)}) async-start(s8[9437184]{0:T(1024)(128)(4,1)} %bitcast.160), calls=%async_computation.5 | async-start | bytes 8388608
  475.8 6.5 slice-start.2
  475.8 6.5 copy-start.43
  500.1 4.0 copy-start.9
  500.1 4.2 copy-start.22
  500.1 4.3 copy-start.38
  549.8 7.6 copy-start.45
  557.4 5.1 copy-start.47
  557.4 5.2 copy-start.49
  562.6 3.3 copy-start.24
  562.7 3.3 copy-start.53
  570.3 7.5 copy-start.25
  572.7 86.0 %all-to-all-start.2 = ((bf16[8,96,512]{2,1,0:T(8,128)(2,1)}), bf16[8,96,512]{2,1,0:T(8,128)(2,1)}, u32[]{:S(2)}, u32[]{:S(2)}) async-start(bf16[8,96,512]{2,1,0:T(8,128)(2,1)} %bitcast.47), calls=%async_computation.2 | async-start | bytes 1572864 | tf_op jit(solution)/shard_map/all_to_all | solution.py:673
  577.8 312.8 %all-reduce.3.cloned.1.call-start = ((), (), s32[]{:S(2)}) async-start(), calls=%async_computation.3 | async-start | bytes 16777216 | tf_op jit(solution)/shard_map/psum | solution.py:941
  577.8 5.2 copy-start.28
  577.8 5.2 copy-start.30
  583.1 3.2 copy-start.29
  601.2 18.7 %copy-start.26 = (bf16[768,512]{0,1:T(8,128)(2,1)S(1)}, bf16[768,512]{0,1:T(8,128)(2,1)}, u32[]{:S(2)}) copy-start(bf16[768,512]{0,1:T(8,128)(2,1)} %get-tuple-element.42) | copy-start | bytes 2359300
  639.7 24.9 %copy-start.18 = (bf16[768,512]{0,1:T(8,128)(2,1)S(1)}, bf16[768,512]{0,1:T(8,128)(2,1)}, u32[]{:S(2)}) copy-start(bf16[768,512]{0,1:T(8,128)(2,1)} %copy.211) | copy-start | bytes 2359300
  658.7 78.6 %all-to-all-start.1 = ((bf16[8,96,512]{2,1,0:T(8,128)(2,1)}), bf16[8,96,512]{2,1,0:T(8,128)(2,1)S(1)}, u32[]{:S(2)}, u32[]{:S(2)}) async-start(bf16[8,96,512]{2,1,0:T(8,128)(2,1)} %bitcast.29), calls=%async_computation.1 | async-start | bytes 1572864 | tf_op jit(solution)/shard_map/all_to_all | solution.py:673
  664.7 69.8 %copy-start.61 = (s32[768]{0:T(1024)S(1)}, s32[768]{0:T(1024)}, u32[]{:S(2)}) copy-start(s32[768]{0:T(1024)} %copy-done.60) | copy-start | bytes 9220
  890.7 4.4 copy-start.34
  900.3 2.9 copy-start.1
  (22 other events, 37.5 us)
Sparse Core Ops, SparseCore 0:
  601.3 289.2 all-reduce.2

commit v2 on v1

--- a/solution.py
+++ b/solution.py
@@ -113,10 +113,13 @@
     def before(self, step):
         return lax.rem(self.spot + self.spots - step, self.spots) * 2 + self.core
 
-    def meet(self, over_expert):
-        peers = [self.device(self.expert, self.spot * 2 + 1 - self.core)]
-        for step in range(1, self.spots):
-            peers.append(self.device(self.expert, self.across(step)))
+    def meet(self, over_expert, whole_tensor=False):
+        if whole_tensor:
+            peers = [self.device(self.expert, self.along(step)) for step in range(1, self.parts)]
+        else:
+            peers = [self.device(self.expert, self.spot * 2 + 1 - self.core)]
+            for step in range(1, self.spots):
+                peers.append(self.device(self.expert, self.across(step)))
         if over_expert:
             for step in range(1, self.groups):
                 peers.append(self.device(flip(self.expert, step, self.groups), self.tensor))
@@ -124,6 +127,15 @@
         for peer in peers:
             pl.semaphore_signal(barrier, inc=1, device_id=peer, device_id_type=MESH)
         pl.semaphore_wait(barrier, len(peers))
+
+    def along(self, step):
+        return lax.rem(self.tensor + step, self.parts)
+
+
+def lasting(microseconds):
+    return pl.CostEstimate(
+        flops=0, bytes_accessed=int(microseconds * 3_000_000), transcendentals=0
+    )
 
 
 def remote(source, target, send, receive, device):
@@ -157,9 +169,14 @@
         self.chunks = target.shape[1]
 
     def owner(self, chunk):
-        if self.over_expert:
-            return flip(self.place.expert, chunk, self.place.groups)
-        return chunk
+        if not self.over_expert:
+            return chunk
+        half, odd, pair = self.place.groups // 2, lax.rem(chunk, 2), lax.div(chunk, 2)
+        even_way = jnp.minimum(chunk, 1) * half + pair
+        odd_way = pair + (1 - jnp.minimum(pair, 1)) * half
+        return flip(
+            self.place.expert, odd * odd_way + (1 - odd) * even_way, self.place.groups
+        )
 
     def spot_of(self, owner, tensor):
         first = pl.multiple_of(tensor * self.width, 128)
@@ -402,7 +419,7 @@
     lax.fori_loop(0, spread.chunks, last, 0)
 
 
-def spread_rows(rows, over_expert, collective):
+def spread_rows(rows, over_expert, collective, microseconds):
     chunks, count, width = rows.shape
     parts = lax.axis_size("tensor")
     full = pl.pallas_call(
@@ -412,6 +429,7 @@
         out_specs=pl.BlockSpec(memory_space=pl.ANY),
         scratch_shapes=Spread.scratch(chunks, parts // 2),
         compiler_params=pltpu.CompilerParams(collective_id=collective, has_side_effects=True),
+        cost_estimate=lasting(microseconds),
     )(rows[None])
     return full.reshape(chunks * count, width * parts)
 
@@ -458,6 +476,7 @@
         compiler_params=pltpu.CompilerParams(
             collective_id=collective, has_side_effects=True, vmem_limit_bytes=48 * MIB
         ),
+        cost_estimate=lasting(26),
     )(*operands)
     return out.reshape(chunks * rows, width)
 
@@ -475,29 +494,22 @@
     return total
 
 
-def make_projected(operands, chunk, first, width):
-    grads, weights = operands[:3], operands[3:]
-    total = None
-    for grad, weight in zip(grads, weights):
-        term = dot_nt(grad[chunk], weight[first : first + width, :])
-        total = term if total is None else total + term
-    return total
-
-
-def experts_kernel(sharers, *refs):
+def experts_kernel(sharers, halves, piece_count, *refs):
+    (source, gates, gate_hbm, up_hbm, down_hbm), refs = refs[:5], refs[5:]
+    pieces, refs = refs[:piece_count], refs[piece_count:]
     (
-        source, gate_hbm, up_hbm, down_hbm,
-        inbox, middle_out, gate_out, up_out, returned,
-        gate_w, up_w, down_w, rows, middle, gate_g, up_g, closing,
-        load_sem, store_sem, back_send, back_land,
-    ) = refs[:21]
+        inbox, grads_out, middle_out, gate_out, up_out, returned,
+        gate_w, up_w, down_w, rows, grads, middle, gate_g, up_g, closing, gates_in,
+        load_sem, piece_sem, store_sem, back_send, back_land, mark_send, mark_land,
+    ) = refs[:23]
     place = Place()
-    spread = Spread(place, source, inbox, refs[21:27], True, sharers)
-    collect = Collect(place, refs[27:])
+    spread = Spread(place, source, inbox, refs[23:29], True, sharers)
+    collect = Collect(place, refs[29:])
     chunks = spread.chunks
     width = source.shape[3]
     units = gate_w.shape[1]
     tile = 704 if units % 704 == 0 else units
+    capacity = rows.shape[0]
     loads = [
         pltpu.make_async_copy(held, kept, load_sem.at[number])
         for number, (held, kept) in enumerate(
@@ -507,22 +519,67 @@
     for load in loads:
         load.start()
     place.meet(True)
+
+    def mark_copy(chunk):
+        peer = spread.owner(chunk)
+        return remote(
+            gates.at[lax.div(peer, sharers)],
+            gates_in.at[place.expert],
+            mark_send.at[chunk],
+            mark_land.at[chunk],
+            place.device(peer, place.tensor),
+        )
+
+    def mark_landed(chunk):
+        peer = spread.owner(chunk)
+        return remote(
+            gates.at[lax.div(peer, sharers)],
+            gates_in.at[peer],
+            mark_send.at[chunk],
+            mark_land.at[chunk],
+            place.device(peer, place.tensor),
+        )
+
     spread.start()
+    for chunk in range(1, chunks):
+        mark_copy(chunk).start()
+    own_mark = pltpu.make_async_copy(
+        gates.at[lax.div(place.expert, sharers)], gates_in.at[place.expert], mark_send.at[0]
+    )
+    own_mark.start()
+    own_mark.wait()
 
     def stores(owner):
         return [
             pltpu.make_async_copy(held, out.at[owner], store_sem.at[number])
             for number, (held, out) in enumerate(
-                ((middle, middle_out), (gate_g, gate_out), (up_g, up_out))
+                ((middle, middle_out), (gate_g, gate_out), (up_g, up_out), (grads, grads_out))
             )
         ]
+
+    def fetches(owner):
+        copies = [pltpu.make_async_copy(inbox.at[0, owner], rows, load_sem.at[3])]
+        number = 0
+        for first, count in halves:
+            for step in range(place.spots):
+                for other in range(2):
+                    tensor = place.before(step)
+                    if other:
+                        tensor = tensor + 1 - 2 * place.core
+                    column = pl.multiple_of(tensor * width, 128)
+                    copies.append(
+                        pltpu.make_async_copy(
+                            pieces[number].at[owner],
+                            grads.at[pl.ds(first, count), pl.ds(column, width)],
+                            piece_sem.at[number],
+                        )
+                    )
+                    number += 1
+        return copies
 
     def work(chunk):
         owner = spread.owner(chunk)
         slot = lax.rem(chunk, 2)
-        spread.third(chunk)
-        fetch = pltpu.make_async_copy(inbox.at[:, owner], rows, load_sem.at[3])
-        fetch.start()
 
         @pl.when(chunk == 0)
         def _():
@@ -533,17 +590,30 @@
         def _():
             for store in stores(spread.owner(chunk - 1)):
                 store.wait()
-
+            mark_landed(chunk).wait_recv()
+
+        spread.third(chunk)
+        copies = fetches(owner)
+        for fetch in copies:
+            fetch.start()
         collect.free_stage(chunk)
-        fetch.wait()
+        for fetch in copies:
+            fetch.wait()
+        wide = gates_in.shape[2]
+        line = jnp.broadcast_to(gates_in[owner][:1], (capacity, wide))
+        here = lax.broadcasted_iota(jnp.int32, (capacity, wide), 0) == lax.broadcasted_iota(
+            jnp.int32, (capacity, wide), 1
+        )
+        gate_column = jnp.sum(jnp.where(here, line, 0.0), axis=1, keepdims=True)
+        grads[...] = (grads[...].astype(jnp.float32) * gate_column).astype(jnp.bfloat16)
         for first in range(0, units, tile):
             here = slice(first, first + tile)
-            gate = jnp.dot(rows[0], gate_w[:, here], preferred_element_type=jnp.float32)
-            up = jnp.dot(rows[0], up_w[:, here], preferred_element_type=jnp.float32)
+            gate = jnp.dot(rows[...], gate_w[:, here], preferred_element_type=jnp.float32)
+            up = jnp.dot(rows[...], up_w[:, here], preferred_element_type=jnp.float32)
             sig = jax.nn.sigmoid(gate)
             act = gate * sig
             middle[:, here] = (act * up).astype(jnp.bfloat16)
-            grad = dot_nt(rows[1], down_w[here, :])
+            grad = dot_nt(grads[...], down_w[here, :])
             gate_g[:, here] = (grad * up * sig * (1.0 + gate * (1.0 - sig))).astype(jnp.bfloat16)
             up_g[:, here] = (grad * act).astype(jnp.bfloat16)
         for store in stores(owner):
@@ -609,6 +679,7 @@
         @pl.when(turn > 0)
         def _():
             owner = spread.owner(turn)
+            mark_copy(turn).wait_send()
             remote(
                 closing.at[0],
                 returned.at[:, owner],
@@ -627,8 +698,8 @@
     collect.finish()
 
 
-def experts(source, gate_w, up_w, down_w, sharers, collective):
-    kinds, _, capacity, width = source.shape
+def experts(source, gates, gate_w, up_w, down_w, pieces, halves, sharers, collective):
+    _, capacity, width = source.shape
     groups, parts = lax.axis_size("expert"), lax.axis_size("tensor")
     spots = parts // 2
     model_width, units = gate_w.shape
@@ -636,36 +707,375 @@
     anywhere = pl.BlockSpec(memory_space=pl.ANY)
     hidden_rows = jax.ShapeDtypeStruct((groups, capacity, units), low)
     return pl.pallas_call(
-        functools.partial(experts_kernel, sharers),
+        functools.partial(experts_kernel, sharers, halves, len(pieces)),
         out_shape=(
-            jax.ShapeDtypeStruct((kinds, groups, capacity, model_width), low),
+            jax.ShapeDtypeStruct((1, groups, capacity, model_width), low),
+            jax.ShapeDtypeStruct((groups, capacity, model_width), low),
             hidden_rows,
             hidden_rows,
             hidden_rows,
-            jax.ShapeDtypeStruct((kinds, groups, capacity, width), low),
+            jax.ShapeDtypeStruct((2, groups, capacity, width), low),
         ),
-        in_specs=[anywhere] * 4,
-        out_specs=(anywhere,) * 5,
+        in_specs=[anywhere] * (5 + len(pieces)),
+        out_specs=(anywhere,) * 6,
         scratch_shapes=[
             pltpu.VMEM((model_width, units), low),
             pltpu.VMEM((model_width, units), low),
             pltpu.VMEM((units, model_width), low),
-            pltpu.VMEM((kinds, capacity, model_width), low),
+            pltpu.VMEM((capacity, model_width), low),
+            pltpu.VMEM((capacity, model_width), low),
             pltpu.VMEM((capacity, units), low),
             pltpu.VMEM((capacity, units), low),
             pltpu.VMEM((capacity, units), low),
-            pltpu.VMEM((2, kinds, capacity, width), low),
+            pltpu.VMEM((2, 2, capacity, width), low),
+            pltpu.VMEM((groups,) + gates.shape[1:], jnp.float32),
             pltpu.SemaphoreType.DMA((4,)),
-            pltpu.SemaphoreType.DMA((3,)),
+            pltpu.SemaphoreType.DMA((len(pieces),)),
+            pltpu.SemaphoreType.DMA((4,)),
+            pltpu.SemaphoreType.DMA((groups,)),
+            pltpu.SemaphoreType.DMA((groups,)),
             pltpu.SemaphoreType.DMA((groups,)),
             pltpu.SemaphoreType.DMA((groups,)),
         ]
         + Spread.scratch(groups, spots)
-        + Collect.scratch(groups, kinds, spots, capacity, width),
+        + Collect.scratch(groups, 2, spots, capacity, width),
         compiler_params=pltpu.CompilerParams(
             collective_id=collective, has_side_effects=True, vmem_limit_bytes=60 * MIB
         ),
-    )(source, gate_w, up_w, down_w)
+        cost_estimate=lasting(180),
+    )(source[None], gates, gate_w, up_w, down_w, *pieces)
+
+
+def tensor_pieces(rows):
+    parts = lax.axis_size("tensor")
+    spots = parts // 2
+    swap = [(index, index ^ 1) for index in range(parts)]
+    pieces = []
+    for step in range(spots):
+        came = rows
+        if step:
+            came = lax.ppermute(
+                rows, "tensor", [(index, (index + 2 * step) % parts) for index in range(parts)]
+            )
+        pieces.append(came)
+    return [piece for came in pieces for piece in (came, lax.ppermute(came, "tensor", swap))]
+
+
+def closing_kernel(count, *refs):
+    normed_t, gain, marks, hidden, scaled, routed, small_in = refs[:7]
+    grads, weights, refs = refs[7 : 7 + count], refs[7 + count : 7 + 2 * count], refs[7 + 2 * count :]
+    refs = refs[len(refs) - (count + 2 + 20 + 8) :]
+    (
+        hold, partial, stat_own, stat_in, ready, gathered, small_own, small_got, small_sum,
+        ring_send, ring_land, stat_send, stat_land, back_send, back_land,
+        small_send, small_land, last_send, last_land, own_sem,
+    ) = refs[count + 2 : count + 22]
+    summed, back, small_out = refs[:count], refs[count], refs[count + 1]
+    place = Place()
+    collect = Collect(place, refs[count + 22 :])
+    groups, parts = place.groups, place.parts
+    pieces, _, rows = collect.core_in.shape[0], None, collect.core_in.shape[3]
+    width = hidden.shape[1]
+    block = hold.shape[3]
+    bucket = back.shape[1]
+    each = rows // bucket
+    place.meet(True, True)
+
+    parity, half = lax.rem(place.expert, 2), lax.div(place.expert, 2)
+    at = half + parity * (groups - 1 - 2 * half)
+
+    def member(spot):
+        spot = lax.rem(spot + groups, groups)
+        high = lax.div(spot, groups // 2)
+        return (1 - high) * 2 * spot + high * (2 * (groups - 1 - spot) + 1)
+
+    ways = ((0, 1), (1, -1))
+
+    def first_row(way, sign, step):
+        spot = lax.rem(at - sign * step + 2 * groups, groups)
+        return pl.multiple_of((way * groups + spot) * block, block)
+
+    def ring_copy(step, way, sign, number, source, target):
+        return remote(
+            source,
+            target,
+            ring_send.at[step, way, number],
+            ring_land.at[step, way, number],
+            place.device(member(at + sign), place.tensor),
+        )
+
+    def slot(step, way, number):
+        return hold.at[step, way, number]
+
+    def spot_out(step, way, sign, number):
+        return summed[number].at[pl.ds(first_row(way, sign, step), block)]
+
+    def ring(step):
+        for number in range(count):
+            for way, sign in ways:
+
+                @pl.when((step >= 1) & (step < groups))
+                def _():
+                    held = slot(step, way, number)
+                    ring_copy(step - 1, way, sign, number, held, held).wait_recv()
+
+                @pl.when(step >= groups)
+                def _():
+                    held = spot_out(step, way, sign, number)
+                    ring_copy(step - 1, way, sign, number, held, held).wait_recv()
+
+                @pl.when(step < groups)
+                def _():
+                    first = first_row(way, sign, step)
+                    own = jnp.dot(
+                        normed_t[pl.ds(first, block), :],
+                        grads[number][...],
+                        preferred_element_type=jnp.float32,
+                    )
+
+                    @pl.when(step == 0)
+                    def _():
+                        hold[0, way, number] = own.astype(jnp.bfloat16)
+
+                    @pl.when(step > 0)
+                    def _():
+                        hold[step, way, number] = (
+                            own + hold[step, way, number].astype(jnp.float32)
+                        ).astype(jnp.bfloat16)
+
+                @pl.when(step < groups - 1)
+                def _():
+                    ring_copy(
+                        step, way, sign, number, slot(step, way, number), slot(step + 1, way, number)
+                    ).start()
+
+                @pl.when(step == groups - 1)
+                def _():
+                    held, there = slot(step, way, number), spot_out(step, way, sign, number)
+                    ring_copy(step, way, sign, number, held, there).start()
+                    pltpu.make_async_copy(held, there, own_sem.at[way, number]).start()
+
+                @pl.when((step >= groups) & (step < 2 * groups - 2))
+                def _():
+                    held = spot_out(step, way, sign, number)
+                    ring_copy(step, way, sign, number, held, held).start()
+
+    def ring_finish(step, carry):
+        for number in range(count):
+            for way, sign in ways:
+                held = slot(0, way, number)
+                ring_copy(step, way, sign, number, held, held).wait_send()
+        return carry
+
+    def band(piece):
+        return pl.ds(pl.multiple_of(piece * rows, rows), rows)
+
+    def project(piece):
+        collect.free_stage(piece)
+        side = lax.rem(piece, 2)
+        for spot in range(place.spots):
+            for core in range(2):
+                first = (spot * 2 + core) * width
+                part = None
+                for grad, weight in zip(grads, weights):
+                    term = dot_nt(grad[band(piece), :], weight[first : first + width, :])
+                    part = term if part is None else part + term
+                collect.stage[side, 0, spot, core] = part.astype(jnp.bfloat16)
+        collect.first(piece)
+
+    def stat_copy(piece, step):
+        return remote(
+            stat_own.at[piece],
+            stat_in.at[piece, step - 1],
+            stat_send.at[piece, step - 1],
+            stat_land.at[piece, step - 1],
+            place.device(place.expert, place.along(step)),
+        )
+
+    def measure(piece):
+        total = collect.third(piece)[0]
+        partial[piece] = total
+        inner = jnp.sum(total * scaled[band(piece), :] * gain[...], axis=1, keepdims=True)
+        stat_own[piece] = jnp.broadcast_to(inner, (rows, 128))
+        for step in range(1, parts):
+            stat_copy(piece, step).start()
+
+    def back_copy(target, piece, number):
+        return remote(
+            ready.at[piece, pl.ds(number * bucket, bucket)],
+            back.at[place.expert],
+            back_send.at[target],
+            back_land.at[place.expert],
+            place.device(target, place.tensor),
+        )
+
+    def conclude(piece):
+        inner = stat_own[piece]
+        for step in range(1, parts):
+            stat_copy(piece, step).wait_recv()
+            inner = inner + stat_in[piece, step - 1]
+        mean = (inner[:, :1] + marks[band(piece), 1:2]) / (width * parts)
+        grad = partial[piece] + routed[band(piece), :]
+        part = scaled[band(piece), :]
+        gathered[...] += jnp.sum(grad * part, axis=0, keepdims=True)
+        result = hidden[band(piece), :] + marks[band(piece), 0:1] * (grad * gain[...] - part * mean)
+        ready[piece] = result.astype(jnp.bfloat16)
+        for number in range(each):
+            target = piece * each + number
+
+            @pl.when(target != place.expert)
+            def _():
+                back_copy(target, piece, number).start()
+
+            @pl.when(target == place.expert)
+            def _():
+                own = pltpu.make_async_copy(
+                    ready.at[piece, pl.ds(number * bucket, bucket)],
+                    back.at[place.expert],
+                    own_sem.at[0, count],
+                )
+                own.start()
+                own.wait()
+
+    def small_copy(step):
+        return remote(
+            small_own,
+            small_got.at[step - 1],
+            small_send.at[step - 1],
+            small_land.at[step - 1],
+            place.device(flip(place.expert, step, groups), place.tensor),
+        )
+
+    def last_copy(step, origin):
+        return remote(
+            small_sum,
+            small_out.at[origin],
+            last_send.at[step - 1],
+            last_land.at[step - 1],
+            place.device(place.expert, place.along(step)),
+        )
+
+    own_small = pltpu.make_async_copy(small_sum, small_out.at[place.tensor], own_sem.at[1, count])
+
+    def small_first():
+        small_own[...] = small_in[...]
+        small_own[0:1, :] = gathered[...]
+        for step in range(1, groups):
+            small_copy(step).start()
+
+    def small_second():
+        total = small_own[...]
+        for step in range(1, groups):
+            small_copy(step).wait_recv()
+            total = total + small_got[step - 1]
+        small_sum[...] = total
+        own_small.start()
+        for step in range(1, parts):
+            last_copy(step, place.tensor).start()
+
+    gathered[...] = jnp.zeros_like(gathered)
+    turns = max(2 * groups - 1, pieces + 5)
+
+    def turn_step(turn, carry):
+        when(turn < 2 * groups - 1, ring, turn)
+        when((turn >= 3) & (turn < pieces + 3), conclude, turn - 3)
+        when((turn >= 2) & (turn < pieces + 2), measure, turn - 2)
+        when((turn >= 1) & (turn < pieces + 1), collect.second, turn - 1)
+        when(turn < pieces, project, turn)
+        when(turn == pieces + 3, small_first)
+        when(turn == pieces + 4, small_second)
+        return carry
+
+    lax.fori_loop(0, turns, turn_step, 0)
+    lax.fori_loop(0, 2 * groups - 2, ring_finish, 0)
+    for number in range(count):
+        for way, sign in ways:
+            pltpu.make_async_copy(
+                slot(groups - 1, way, number),
+                spot_out(groups - 1, way, sign, number),
+                own_sem.at[way, number],
+            ).wait()
+    collect.finish()
+    for step in range(1, groups):
+        small_copy(step).wait_send()
+    own_small.wait()
+    for step in range(1, parts):
+        origin = lax.rem(place.tensor + parts - step, parts)
+        last_copy(step, place.tensor).wait_send()
+        last_copy(step, origin).wait_recv()
+
+    def settle(piece, carry):
+        for step in range(1, parts):
+            stat_copy(piece, step).wait_send()
+        for number in range(each):
+            target = piece * each + number
+
+            @pl.when(target != place.expert)
+            def _():
+                back_copy(target, piece, number).wait_send()
+                remote(
+                    ready.at[piece, pl.ds(number * bucket, bucket)],
+                    back.at[target],
+                    back_send.at[target],
+                    back_land.at[target],
+                    place.device(target, place.tensor),
+                ).wait_recv()
+
+        return carry
+
+    lax.fori_loop(0, pieces, settle, 0)
+
+
+def closing(normed_t, gain, marks, hidden, scaled, routed, small, grads, weights, after, pieces, collective):
+    groups, parts = lax.axis_size("expert"), lax.axis_size("tensor")
+    spots = parts // 2
+    model_width, tokens = normed_t.shape
+    columns = grads[0].shape[1]
+    width = hidden.shape[1]
+    count = len(grads)
+    rows = tokens // pieces
+    block = model_width // (2 * groups)
+    low, full = jnp.bfloat16, jnp.float32
+    inside = pl.BlockSpec(memory_space=pltpu.VMEM)
+    anywhere = pl.BlockSpec(memory_space=pl.ANY)
+    dma = pltpu.SemaphoreType.DMA
+    return pl.pallas_call(
+        functools.partial(closing_kernel, count),
+        out_shape=(
+            *(jax.ShapeDtypeStruct((model_width, columns), low) for _ in range(count)),
+            jax.ShapeDtypeStruct((groups, tokens // groups, width), low),
+            jax.ShapeDtypeStruct((parts,) + small.shape, full),
+        ),
+        in_specs=[inside] * (7 + 2 * count) + [anywhere] * len(after),
+        out_specs=(anywhere,) * (count + 2),
+        scratch_shapes=[
+            pltpu.VMEM((groups, 2, count, block, columns), low),
+            pltpu.VMEM((pieces, rows, width), full),
+            pltpu.VMEM((pieces, rows, 128), full),
+            pltpu.VMEM((pieces, parts - 1, rows, 128), full),
+            pltpu.VMEM((pieces, rows, width), low),
+            pltpu.VMEM((1, width), full),
+            pltpu.VMEM(small.shape, full),
+            pltpu.VMEM((groups - 1,) + small.shape, full),
+            pltpu.VMEM(small.shape, full),
+            dma((2 * groups - 2, 2, count)),
+            dma((2 * groups - 2, 2, count)),
+            dma((pieces, parts - 1)),
+            dma((pieces, parts - 1)),
+            dma((groups,)),
+            dma((groups,)),
+            dma((groups - 1,)),
+            dma((groups - 1,)),
+            dma((parts - 1,)),
+            dma((parts - 1,)),
+            dma((2, count + 1)),
+        ]
+        + Collect.scratch(pieces, 1, spots, rows, width),
+        compiler_params=pltpu.CompilerParams(
+            collective_id=collective, has_side_effects=True, vmem_limit_bytes=56 * MIB
+        ),
+        cost_estimate=lasting(140),
+    )(normed_t, gain, marks, hidden, scaled, routed, small, *grads, *weights, *after)
 
 
 def to_expert(rows, group_count):
@@ -677,6 +1087,27 @@
         concat_axis=0,
         tiled=True,
     ).reshape(count, width)
+
+
+def side_by_side(pieces):
+    parts = len(pieces)
+    spots = parts // 2
+    index = lax.axis_index("tensor")
+    spot, core = index // 2, index % 2
+    pairs = []
+    for step in range(spots):
+        same, other = pieces[2 * step], pieces[2 * step + 1]
+        pairs.append(
+            (jnp.where(core == 0, same, other), jnp.where(core == 0, other, same))
+        )
+    ordered = []
+    for here in range(spots):
+        for side in range(2):
+            value = pairs[0][side]
+            for step in range(1, spots):
+                value = jnp.where((spot - here) % spots == step, pairs[step][side], value)
+            ordered.append(value)
+    return jnp.concatenate(ordered, axis=1)
 
 
 def gather_tensor(rows):
@@ -720,14 +1151,13 @@
     row_ids = jnp.arange(tok_rows, dtype=jnp.int32)
     deal_mask = (row_ids[:, None] == deal_rank[None, :]).astype(low)
     dealt = jnp.dot(deal_mask, own_cols(tokens), preferred_element_type=jnp.float32).astype(low)
-    resid_low = spread_rows(dealt.reshape(group_count, bucket_rows, col_width), True, 0)
-    grad_cols_low = to_expert(
-        jnp.dot(deal_mask, own_cols(out_grad), preferred_element_type=jnp.float32).astype(low),
-        group_count,
-    )
+    resid_low = spread_rows(dealt.reshape(group_count, bucket_rows, col_width), True, 0, 30)
+    dealt_grads = jnp.dot(
+        deal_mask, own_cols(out_grad), preferred_element_type=jnp.float32
+    ).astype(low)
+    dealt_grads, resid_low = lax.optimization_barrier((dealt_grads, resid_low))
+    grad_cols_low = to_expert(dealt_grads, group_count)
     grad_cols = grad_cols_low.astype(jnp.float32)
-    resid_in = resid_low.astype(jnp.float32)
-    resid_cols = own_cols(resid_low).astype(jnp.float32)
     gain_one, gain_two = own_cols(attn_gain), own_cols(mlp_gain)
     router_one = lax.dynamic_slice_in_dim(attn_router, col_first, col_width, 0)
     router_two = lax.dynamic_slice_in_dim(mlp_router, col_first, col_width, 0)
@@ -742,8 +1172,17 @@
     to_slot = (
         (slot_ids[:, None] == chosen[0][None, :]) | (slot_ids[:, None] == chosen[1][None, :])
     ).astype(low)
-    slot_grads = jnp.dot(to_slot, grad_cols_low, preferred_element_type=jnp.float32)
-
+    slot_grads = jnp.dot(to_slot, grad_cols_low, preferred_element_type=jnp.float32).astype(low)
+    slot_grads = slot_grads.reshape(expert_count, capacity, col_width)
+    slot_grads, resid_low = lax.optimization_barrier((slot_grads, resid_low))
+    halves = ((0, capacity),)
+    grad_pieces = []
+    for first, count in halves:
+        block = jnp.repeat(slot_grads[:, first : first + count], sharers, axis=0)
+        grad_pieces.append(to_expert(block.reshape(group_count * count, col_width), group_count))
+
+    resid_in = resid_low.astype(jnp.float32)
+    resid_cols = own_cols(resid_low).astype(jnp.float32)
     segment, cosine, sine = rotary_tables(seq_lengths[0], tok_rows)
     scale = 1.0 / math.sqrt(HEAD)
     local_heads = w_query.shape[1] // HEAD
@@ -789,6 +1228,12 @@
         col_width,
         1,
     )
+    *grad_pieces, attn_cols = lax.optimization_barrier((*grad_pieces, attn_cols))
+    grad_pieces = [
+        piece
+        for (_, count), rows in zip(halves, grad_pieces)
+        for piece in tensor_pieces(rows.reshape(group_count, count, col_width))
+    ]
     hidden = resid_cols + attn_cols
     weighed = hidden * gain_two
     stats = jnp.concatenate(
@@ -814,12 +1259,16 @@
         )
         for way in range(2)
     )
-    slot_grads = (slot_gates[:, None] * slot_grads).astype(low)
-    inbox, middle, gate_grad, up_grad, returned = experts(
-        jnp.stack([slot_rows, slot_grads]).reshape(2, expert_count, capacity, col_width),
+    gate_lines = jnp.pad(slot_gates.reshape(expert_count, capacity), ((0, 0), (0, -capacity % 128)))
+    gate_lines = jnp.broadcast_to(gate_lines[:, None, :], (expert_count, 8, gate_lines.shape[1]))
+    inbox, slot_grads, middle, gate_grad, up_grad, returned = experts(
+        slot_rows.reshape(expert_count, capacity, col_width),
+        gate_lines,
         w_gate[0],
         w_up[0],
         w_down[0],
+        grad_pieces,
+        halves,
         sharers,
         2,
     )
@@ -859,9 +1308,7 @@
     mlp_gain_grad = jnp.sum(norm_two_grad * scaled_two, axis=0)
     mean_two = (stats[2] + jnp.sum(mlp_logit_grad * mlp_logits, axis=1)) / model_width
     hidden_grad = grad_cols + factor_two * (norm_two_grad * gain_two - scaled_two * mean_two[:, None])
-    hidden_grad_low = spread_rows(
-        hidden_grad.astype(low).reshape(pieces, piece_rows, col_width), False, 3
-    )
+    hidden_grad_low = side_by_side(tensor_pieces(hidden_grad.astype(low)))
     gate_wide = jnp.repeat(gate_local, span, axis=1)
     heads_float = heads_low.astype(jnp.float32)
     out_w_grad = jnp.einsum(
@@ -870,11 +1317,20 @@
         hidden_grad_low,
         preferred_element_type=jnp.float32,
     )
+    out_w_grad, middle, up_grad, hidden_grad_low = lax.optimization_barrier(
+        (out_w_grad.astype(low), middle, up_grad, hidden_grad_low)
+    )
+    out_w_grad = lax.psum(out_w_grad, "expert").astype(jnp.float32)
     heads_plain = jnp.einsum(
         "td,cd->tc", hidden_grad_low, w_out, preferred_element_type=jnp.float32
     )
-    local_gate_grad = jnp.sum(
-        (heads_plain * heads_float).reshape(tok_rows, local_experts, span), axis=2
+    gate_products = heads_plain * heads_float
+    local_gate_grad = jnp.stack(
+        [
+            jnp.sum(gate_products[:, expert * span : (expert + 1) * span], axis=1)
+            for expert in range(local_experts)
+        ],
+        axis=1,
     )
     heads_grad = (heads_plain * gate_wide).astype(low).reshape(tok_rows, local_heads, HEAD)
     scores = block_scores(query, keys, segment, 0, tok_rows, scale)
@@ -896,65 +1352,58 @@
     query_pre_grad = undo_turn(query_grad, cosine, sine).astype(low).reshape(tok_rows, width)
     key_pre_grad = undo_turn(key_grad, cosine, sine).astype(low).reshape(tok_rows, width)
     value_pre_grad = value_grad.astype(low).reshape(tok_rows, width)
-    weight_grads = [
-        jnp.einsum("td,tc->dc", normed_low, grad, preferred_element_type=jnp.float32)
-        for grad in (query_pre_grad, key_pre_grad, value_pre_grad)
-    ]
-    norm_one_cols = collect_rows(
-        make_projected,
-        tuple(
-            grad.reshape(pieces, piece_rows, width)
-            for grad in (query_pre_grad, key_pre_grad, value_pre_grad)
-        )
-        + (w_query, w_key, w_value),
-        pieces,
-        piece_rows,
-        col_width,
-        4,
-    )
+    gate_grads = gather_tensor(local_gate_grad.T)
+    gate_grads = gate_grads.reshape(part_count * local_experts, tok_rows).T
+    attn_pair_grad = jnp.sum(attn_mask * gate_grads[:, None, :], axis=2)
+    attn_logit_grad = pair_back(attn_gates, attn_mask, attn_pair_grad)
     scaled_cols = resid_cols * factor_one
     normed_cols = scaled_cols * gain_one
-    stats = jnp.concatenate(
-        [jnp.sum(norm_one_cols * normed_cols, axis=1)[None, :], local_gate_grad.T], axis=0
-    )
-    stats = gather_tensor(stats)
-    gate_grads = stats[:, 1:].reshape(part_count * local_experts, tok_rows).T
-    attn_pair_grad = jnp.sum(attn_mask * gate_grads[:, None, :], axis=2)
-    attn_logit_grad = pair_back(attn_gates, attn_mask, attn_pair_grad)
-    norm_one_grad = norm_one_cols + jnp.dot(attn_logit_grad, router_one.T, precision=PRECISE)
     attn_router_grad = jnp.dot(normed_cols.T, attn_logit_grad, precision=PRECISE)
-    attn_gain_grad = jnp.sum(norm_one_grad * scaled_cols, axis=0)
-    mean_one = (
-        jnp.sum(stats[:, 0], axis=0) + jnp.sum(attn_logit_grad * attn_logits, axis=1)
-    ) / model_width
-    input_cols = hidden_grad + factor_one * (
-        norm_one_grad * gain_one - scaled_cols * mean_one[:, None]
-    )
-    back_grad = to_expert(input_cols.astype(low), group_count)
+    small = jnp.concatenate(
+        [
+            jnp.zeros((1, col_width), jnp.float32),
+            attn_router_grad.T,
+            mlp_gain_grad[None],
+            mlp_router_grad.T,
+        ],
+        axis=0,
+    )
+    small = jnp.pad(small, ((0, -small.shape[0] % 8), (0, 0)))
+    marks = jnp.stack(
+        [factor_one[:, 0], jnp.sum(attn_logit_grad * attn_logits, axis=1)], axis=1
+    )
+    rows = inbox.reshape(-1, model_width)
+    grad_rows = slot_grads.reshape(-1, model_width)
+    units = middle.shape[2]
+    gate_w_grad, up_w_grad = (
+        jnp.einsum("sd,sf->df", rows, grad.reshape(-1, units), preferred_element_type=jnp.float32)
+        for grad in (gate_grad, up_grad)
+    )
+    down_grad = jnp.einsum(
+        "sf,sd->fd", middle.reshape(-1, units), grad_rows, preferred_element_type=jnp.float32
+    )
+    *weight_grads, back_grad, small = closing(
+        normed_low.T,
+        gain_one[None],
+        jnp.pad(marks, ((0, 0), (0, 126))),
+        hidden_grad,
+        scaled_cols,
+        jnp.dot(attn_logit_grad, router_one.T, precision=PRECISE),
+        small,
+        (query_pre_grad, key_pre_grad, value_pre_grad),
+        (w_query, w_key, w_value),
+        (gate_w_grad, up_w_grad, down_grad),
+        pieces,
+        3,
+    )
+    back_grad = back_grad.reshape(tok_rows, col_width)
+    weight_grads = [grad.astype(jnp.float32) for grad in weight_grads]
     mixed, tokens_grad = (
         jnp.einsum("ri,rc->ic", deal_mask, back, preferred_element_type=jnp.float32).astype(low)
         for back in (back_mixed, back_grad)
     )
-    out_w_grad = lax.psum(out_w_grad.astype(low), "expert").astype(jnp.float32)
-    weight_grads = [
-        grad.astype(jnp.float32)
-        for grad in lax.psum(tuple(grad.astype(low) for grad in weight_grads), "expert")
-    ]
-    small = jnp.concatenate(
-        [attn_gain_grad[None], attn_router_grad.T, mlp_gain_grad[None], mlp_router_grad.T], axis=0
-    )
-    small = gather_tensor(lax.psum(small, "expert"))
     small = small.transpose(1, 0, 2).reshape(-1, model_width)
     experts_of = attn_router.shape[1]
-    rows = inbox.reshape(2, -1, model_width)
-    units = middle.shape[2]
-    gate_w_grad, up_w_grad = (
-        jnp.einsum("sd,sf->df", rows[0], grad.reshape(-1, units), preferred_element_type=jnp.float32)
-        for grad in (gate_grad, up_grad)
-    )
-    down_grad = jnp.einsum(
-        "sf,sd->fd", middle.reshape(-1, units), rows[1], preferred_element_type=jnp.float32
-    )
     return (
         mixed,
         tokens_grad,
@@ -965,7 +1414,7 @@
         weight_grads[2],
         out_w_grad,
         small[1 + experts_of],
-        small[2 + experts_of :].T,
+        small[2 + experts_of : 2 + experts_of + expert_count].T,
         gate_w_grad[None],
         up_w_grad[None],
         down_grad[None],

time: 921 us -> 791 us (0.86)
  waiting for transfers between devices: 152 us -> 54 us
  Pallas kernels: 368 us -> 437 us
  blocking collectives: 81.7 us -> 16.2 us
  local copies, waits for them, and re-layouts: 66.6 us -> 40.3 us
  matrix products: 157 us -> 140 us
    psum x1, waiting for transfers between devices: 152 us -> 0.01 us  [body(): out_w_grad = lax.psum(out_w_grad, 'expert').astype(jnp.float32)]
    pallas_call x1 -> x2, Pallas kernels: 249 us -> 380 us  [the longest x1 194 us: closing(): pl.pallas_call(functools.partial(closing_kernel, count), out_shape=(*(jax...]
    psum x1 -> x0, blocking collectives: 60 us -> none  [body(): small = gather_tensor(lax.psum(small, 'expert'))]
    ppermute x0 -> x6, waiting for transfers between devices: none -> 44 us  [the longest x2 44 us: tensor_pieces(): lax.ppermute(rows, 'tensor', [(index, (index + 2 * step) % parts) for ind...]
    pallas_call x2 -> x1, Pallas kernels: 63 us -> 31.2 us  [spread_rows(): pl.pallas_call(functools.partial(spread_kernel, over_expert), out_shape=j...]
    pallas_call x2 -> x1, Pallas kernels: 56.3 us -> 26.7 us  [collect_rows(): pl.pallas_call(functools.partial(collect_kernel, make, len(operands)), ou...]
    dot_general x6 -> x3, matrix products: 68 us -> 55.3 us  [the longest x2 36.3 us: body(): jnp.einsum('sd,sf->df', rows, grad.reshape(-1, units), preferred_element_...]
    slice x3 -> x1, local copies, waits for them, and re-layouts: 12.3 us -> 0.66 us  [body(): small[2 + experts_of:2 + experts_of + expert_count]]
  transfers between devices with their start and end apart: 4 -> 10, of which waited for: 1 -> 3; matrix products, arithmetic and copies ran while one was open for 18% -> 15% of each run, Pallas kernels for 7% -> 28%
where the time goes in v2:
time: 791 us; the launch traced here: 785 us
  Pallas kernels  437 us (55%)
  matrix products  140 us (18%)
  other arithmetic  56.3 us (7%)
  waiting for transfers between devices  54 us (7%)
  local copies, waits for them, and re-layouts  40.3 us (5%)
  starting transfers between devices  25.3 us (3%)
  blocking collectives  16.2 us (2%)
  between operations  15.5 us (2%)
    pallas_call x1, Pallas kernels, closing(): pl.pallas_call(functools.partial(closing_kernel, count), out_shape=(*(jax...  194 us
    pallas_call x1, Pallas kernels, experts(): pl.pallas_call(functools.partial(experts_kernel, sharers, halves, len(pie...  186 us
    ppermute x2, waiting for transfers between devices, tensor_pieces(): lax.ppermute(rows, 'tensor', [(index, (index + 2 * step) % parts) for ind...  44 us
    dot_general x2, matrix products, body(): jnp.einsum('sd,sf->df', rows, grad.reshape(-1, units), preferred_element_...  36.3 us
    pallas_call x1, Pallas kernels, spread_rows(): pl.pallas_call(functools.partial(spread_kernel, over_expert), out_shape=j...  31.2 us
    pallas_call x1, Pallas kernels, collect_rows(): pl.pallas_call(functools.partial(collect_kernel, make, len(operands)), ou...  26.7 us
    all_to_all x3, starting transfers between devices, to_expert(): lax.all_to_all(rows.reshape(group_count, count // group_count, width), 'e...  23.9 us
    dot_general x1, matrix products, body(): jnp.einsum('sf,sd->fd', middle.reshape(-1, units), grad_rows, preferred_e...  19.1 us
  transfers between devices with their start and end apart: 10, of which 3 were waited for; matrix products, arithmetic and copies ran while one was open for 15% of the time, Pallas kernels for 28%

profile of v2, /device:TPU:20, one launch (start us, length us, event | category | flops | bytes accessed | tf_op | source)
XLA Modules:
  0.0 784.7 jit_solution(11208866450397185512)
XLA Ops:
  10.8 2.8 fusion.65
  13.6 31.2 %shard_map.273 = bf16[1,8,96,2048]{3,2,1,0:T(8,128)(2,1)} custom-call(bf16[1,8,96,512]{3,2,1,0:T(8,128)(2,1)} %bitcast.175), custom_call_target="tpu_custom_call" | custom-call | bytes 90000000 | tf_op jit(solution)/shard_map/pallas_call | solution.py:425
  44.8 10.4 %all-to-all-start = ((bf16[8,96,512]{2,1,0:T(8,128)(2,1)}), bf16[8,96,512]{2,1,0:T(8,128)(2,1)S(1)}, u32[]{:S(2)}, u32[]{:S(2)}) async-start(bf16[8,96,512]{2,1,0:T(8,128)(2,1)} %bitcast.2), calls=%async_computation | async-start | bytes 1572864 | tf_op jit(solution)/shard_map/all_to_all | solution.py:1083
  59.1 2.3 broadcast_multiply_fusion.1
  62.6 10.0 %all-to-all-done = bf16[8,96,512]{2,1,0:T(8,128)(2,1)S(1)} async-done(((bf16[8,96,512]{2,1,0:T(8,128)(2,1)}), bf16[8,96,512]{2,1,0:T(8,128)(2,1)S(1)}, u32[]{:S(2)}, u32[]{:S(2)}) %all-to-all-start) | async-done | bytes 786464 | tf_op jit(solution)/shard_map/all_to_all | solution.py:1083
  73.4 3.1 fusion.23
  76.5 8.4 %all-to-all-start.1 = ((bf16[8,240,512]{2,1,0:T(8,128)(2,1)}), bf16[8,240,512]{2,1,0:T(8,128)(2,1)}, u32[]{:S(2)}, u32[]{:S(2)}) async-start(bf16[8,240,512]{2,1,0:T(8,128)(2,1)} %bitcast.167), calls=%async_computation.1 | async-start | bytes 3932160 | tf_op jit(solution)/shard_map/all_to_all | solution.py:1083
  104.6 7.8 fusion.4
  112.8 26.7 %shard_map.274 = f32[4,192,512]{2,1,0:T(8,128)S(1)} custom-call(bf16[4,192,512]{2,1,0:T(8,128)(2,1)S(1)} %reshape_reshape.3.refs_0_, f32[4,192,2]{2,1,0:T(8,128)S(1)} %bitcast.138, bf16[512,2048]{1,0:T(8,128)(2,1)S(1)} %copy-done.2), custom_call_target="tpu_custom_call" | custom-call | bytes 78000000 | tf_op jit(solution)/shard_map/pallas_call | solution.py:470
  144.7 3.1 multiply_reduce_fusion.3
  147.8 36.5 %collective-permute-done.1.refs_7_ = bf16[8,240,512]{2,1,0:T(8,128)(2,1)} collective-permute-done((bf16[8,240,512]{2,1,0:T(8,128)(2,1)}, bf16[8,240,512]{2,1,0:T(8,128)(2,1)}, u32[]{:S(2)}, u32[]{:S(2)}) %collective-permute-start.1) | collective-permute-done | bytes 1966112 | tf_op jit(solution)/shard_map/ppermute | solution.py:757
  185.7 5.7 all-gather.3
  193.2 4.6 fusion.26
  198.4 186.0 %shard_map.275 = (bf16[1,8,240,2048]{3,2,1,0:T(8,128)(2,1)}, bf16[8,240,2048]{2,1,0:T(8,128)(2,1)}, bf16[8,240,1408]{2,1,0:T(8,128)(2,1)}, bf16[8,240,1408]{2,1,...) custom-call(bf16[1,8,240,512]{3,2,1,0:T(8,128)(2,1)} %bitcast.168, ...), custom_call_target="tpu_custom_call" | custom-call | bytes 540000000 | tf_op jit(solution)/shard_map/pallas_call | solution.py:709
  384.4 2.4 fusion.114
  386.8 3.3 fusion.10
  390.1 3.3 fusion.8
  393.4 3.3 multiply_reduce_fusion.2
  396.7 3.1 copy.149
  399.8 3.0 copy.150
  402.8 2.3 fusion.46
  405.2 5.2 all-gather.4
  410.6 3.5 fusion.20
  414.1 3.0 copy.148
  417.1 6.2 fusion.113
  423.3 2.4 fusion.107
  425.8 4.6 copy.162.refs_0_
  430.8 5.1 all-to-all-start.2
  435.9 7.5 collective-permute-done.3
  443.4 18.8 %fusion.119.refs_13_ = f32[2048,1408]{1,0:T(8,128)} fusion(bf16[1920,2048]{1,0:T(8,128)(2,1)} %bitcast.186, bf16[1920,1408]{1,0:T(8,128)(2,1)} %bitcast.191), kind=kOutput, calls=%fused_computation.211 | convolution fusion | flops 11072962560 | bytes 24805376 | tf_op jit(solution)/shard_map/sd,sf->df/dot_general | solution.py:1379
  469.0 3.8 convolution_convert_fusion
  472.8 3.9 fusion.49
  476.9 5.3 all-gather.5
  486.3 7.2 multiply_reduce_fusion
  493.4 10.2 %multiply_convert_fusion = bf16[4,768,768]{1,2,0:T(8,128)(2,1)} fusion(f32[4,768,768]{1,2,0:T(8,128)} %get-tuple-element.105, f32[4,768,768]{1,2,0:T(8,128)} %copy-done.4, f32[4,768]{1,0:T(4,128)S(1)} %get-tuple-element.104, f32[4,768]{1,0:T(4,128)S(1)} %log_add_fusion), kind=kLoop, calls=%fused_computation | loop fusion | flops 9437184 | bytes 23617536 | tf_op jit(solution)/shard_map/convert_element_type | solution.py:1344
  503.7 3.5 fusion.118
  507.9 3.2 bitcast_multiply_fusion.2
  512.4 17.4 %fusion.120.refs_14_ = f32[2048,1408]{1,0:T(8,128)} fusion(bf16[1920,2048]{1,0:T(8,128)(2,1)S(1)} %bitcast.189, bf16[1920,1408]{1,0:T(8,128)(2,1)} %bitcast.190), kind=kOutput, calls=%fused_computation.212 | convolution fusion | flops 11072962560 | bytes 24805376 | tf_op jit(solution)/shard_map/sd,sf->df/dot_general | solution.py:1379
  529.9 19.1 %fusion.121 = f32[1408,2048,1]{1,0,2:T(8,128)} fusion(bf16[8,240,1408]{2,1,0:T(8,128)(2,1)} %get-tuple-element.47, bf16[8,240,2048]{2,1,0:T(8,128)(2,1)} %get-tuple-element.48), kind=kOutput, calls=%fused_computation.213 | convolution fusion | flops 11072962560 | bytes 24805376 | tf_op jit(solution)/shard_map/sf,sd->fd/dot_general | solution.py:1382
  552.5 2.3 copy.172.refs_7_
  554.8 2.3 copy.173.refs_8_
  557.2 5.4 fusion.61
  563.8 3.3 fusion.86.refs_5_
  567.1 193.6 %shard_map.276 = (bf16[2048,512]{1,0:T(8,128)(2,1)}, bf16[2048,512]{1,0:T(8,128)(2,1)}, bf16[2048,512]{1,0:T(8,128)(2,1)}, bf16[8,96,512]{2,1,0:T(8,128)(2,1)}, f32[4,24,512]{2,1,0:T(8,128)}) custom-call(bf16[2048,768]{1,0:T(8,128)(2,1)} %copy.162.refs_0_, f32[1,512]{1,0:T(1,128)} %bitcast.181, f32[768,128]{1,0:T(8,128)} %pad.13.refs_2_, ...), custom_call_target="tpu_custom_call" | custom-call | bytes 420000000 | tf_op jit(solution)/shard_map/pallas_call | solution.py:1042
  760.7 4.3 convert_element_type.166
  765.0 2.6 convert_element_type.167
  767.6 2.6 convert_element_type.168
  773.2 4.1 convert_element_type.169
  (228 shorter events, 59.4 us)
Async XLA Ops:
  8.1 5.5 copy-start.50
  13.6 41.6 %copy-start.35 = (s32[768,2]{0,1:T(2,128)S(1)}, s32[768,2]{0,1:T(2,128)}, u32[]{:S(2)}) copy-start(s32[768,2]{0,1:T(2,128)} %param.34) | copy-start | bytes 18436
  13.6 41.8 %copy-start.48 = (s32[1,1536]{1,0:T(1,128)S(1)}, s32[1,1536]{1,0:T(1,128)}, u32[]{:S(2)}) copy-start(s32[1,1536]{1,0:T(1,128)} %param.35) | copy-start | bytes 18436
  13.6 42.1 %copy-start.53 = (s32[1,3]{1,0:T(1,128)S(1)}, s32[1,3]{1,0:T(1,128)}, u32[]{:S(2)}) copy-start(s32[1,3]{1,0:T(1,128)} %param.32) | copy-start | bytes 40
  44.8 27.7 %all-to-all-start = ((bf16[8,96,512]{2,1,0:T(8,128)(2,1)}), bf16[8,96,512]{2,1,0:T(8,128)(2,1)S(1)}, u32[]{:S(2)}, u32[]{:S(2)}) async-start(bf16[8,96,512]{2,1,0:T(8,128)(2,1)} %bitcast.2), calls=%async_computation | async-start | bytes 1572864 | tf_op jit(solution)/shard_map/all_to_all | solution.py:1083
  59.0 13.5 %copy-start.40 = (s32[768]{0:T(1024)}, s32[768]{0:T(1024)S(1)}, u32[]{:S(2)}) copy-start(s32[768]{0:T(1024)S(1)} %get-tuple-element.59) | copy-start | bytes 9220
  59.0 13.5 %copy-start.42 = (s32[768]{0:T(1024)}, s32[768]{0:T(1024)S(1)}, u32[]{:S(2)}) copy-start(s32[768]{0:T(1024)S(1)} %get-tuple-element.60) | copy-start | bytes 9220
  76.5 8.4 %copy-start.6 = (bf16[1,8,96,2048]{3,2,1,0:T(8,128)(2,1)S(1)}, bf16[1,8,96,2048]{3,2,1,0:T(8,128)(2,1)}, u32[]{:S(2)}) copy-start(bf16[1,8,96,2048]{3,2,1,0:T(8,128)(2,1)} %shard_map.273) | copy-start | bytes 9437188
  76.5 9.1 %copy-start.44 = (f32[2048]{0:T(1024)S(1)}, f32[2048]{0:T(1024)}, u32[]{:S(2)}) copy-start(f32[2048]{0:T(1024)} %param.20) | copy-start | bytes 24580
  76.5 64.2 %all-to-all-start.1 = ((bf16[8,240,512]{2,1,0:T(8,128)(2,1)}), bf16[8,240,512]{2,1,0:T(8,128)(2,1)}, u32[]{:S(2)}, u32[]{:S(2)}) async-start(bf16[8,240,512]{2,1,0:T(8,128)(2,1)} %bitcast.167), calls=%async_computation.1 | async-start | bytes 3932160 | tf_op jit(solution)/shard_map/all_to_all | solution.py:1083
  96.2 5.3 copy-start.4
  96.2 3.2 copy-start.24
  96.2 3.1 copy-start.45
  104.6 7.8 copy-start.34
  104.6 8.2 %copy-start.2 = (bf16[512,2048]{1,0:T(8,128)(2,1)S(1)}, bf16[512,2048]{1,0:T(8,128)(2,1)}, u32[]{:S(2)}) copy-start(bf16[512,2048]{1,0:T(8,128)(2,1)} %refs_2_.1) | copy-start | bytes 6291460
  112.5 29.2 %copy-start.46 = (f32[2048]{0:T(1024)S(1)}, f32[2048]{0:T(1024)}, u32[]{:S(2)}) copy-start(f32[2048]{0:T(1024)} %param.20) | copy-start | bytes 24580
  140.7 43.7 %collective-permute-start.1 = (bf16[8,240,512]{2,1,0:T(8,128)(2,1)}, bf16[8,240,512]{2,1,0:T(8,128)(2,1)}, u32[]{:S(2)}, u32[]{:S(2)}) collective-permute-start(bf16[8,240,512]{2,1,0:T(8,128)(2,1)} %bitcast.22.refs_5_), channel_id=1, source_target_pairs={{0,2},{1,3},{2,0},{3,1},{4,6},{5,7},{6,4},{7,5},{8,10},{9,11},{10,... | collective-permute-start | bytes 5898248 | tf_op jit(solution)/shard_map/ppermute | solution.py:757
  141.7 341.7 %copy-start.47 = (f32[512]{0:T(512)}, f32[512]{0:T(512)S(1)}, u32[]{:S(2)}) copy-start(f32[512]{0:T(512)S(1)} %dynamic_slice.30) | copy-start | bytes 6148
  144.6 39.7 %copy-start.39 = (f32[2048,8]{0,1:T(8,128)S(1)}, f32[2048,8]{0,1:T(8,128)}, u32[]{:S(2)}) copy-start(f32[2048,8]{0,1:T(8,128)} %param.27) | copy-start | bytes 196612
  144.6 46.8 %copy-start.36 = (s32[768,2]{0,1:T(2,128)S(1)}, s32[768,2]{0,1:T(2,128)}, u32[]{:S(2)}) copy-start(s32[768,2]{0,1:T(2,128)} %param.34) | copy-start | bytes 18436
  144.6 47.0 %copy-start.41 = (s32[768]{0:T(1024)S(1)}, s32[768]{0:T(1024)}, u32[]{:S(2)}) copy-start(s32[768]{0:T(1024)} %copy-done.40) | copy-start | bytes 9220
  144.6 47.0 %copy-start.43 = (s32[768]{0:T(1024)S(1)}, s32[768]{0:T(1024)}, u32[]{:S(2)}) copy-start(s32[768]{0:T(1024)} %copy-done.42) | copy-start | bytes 9220
  144.7 53.1 %collective-permute-start = (bf16[8,240,512]{2,1,0:T(8,128)(2,1)}, bf16[8,240,512]{2,1,0:T(8,128)(2,1)}, u32[]{:S(2)}, u32[]{:S(2)}) collective-permute-start(bf16[8,240,512]{2,1,0:T(8,128)(2,1)} %bitcast.22.refs_5_), channel_id=1, source_target_pairs={{0,1},{1,0},{2,3},{3,2},{4,5},{5,4},{6,7},{7,6},{8,9},{9,8},{10,11... | collective-permute-start | bytes 5898248 | tf_op jit(solution)/shard_map/ppermute | solution.py:761
  147.8 36.5 %copy-start.8 = (f32[768,512]{1,0:T(8,128)}, f32[768,512]{1,0:T(8,128)S(1)}, u32[]{:S(2)}) copy-start(f32[768,512]{1,0:T(8,128)S(1)} %get-tuple-element.66) | copy-start | bytes 4718596
  184.3 13.4 %collective-permute-start.2 = (bf16[8,240,512]{2,1,0:T(8,128)(2,1)}, bf16[8,240,512]{2,1,0:T(8,128)(2,1)}, u32[]{:S(2)}, u32[]{:S(2)}) collective-permute-start(bf16[8,240,512]{2,1,0:T(8,128)(2,1)} %collective-permute-done.1.refs_7_), channel_id=1, source_target_pairs={{0,1},{1,0},{2,3},{3,2},{4,5},{5,4},{6,7},{7,6},{8,9},{9,8},{10,11... | collective-permute-start | bytes 5898248 | tf_op jit(solution)/shard_map/ppermute | solution.py:761
  390.1 3.3 copy-start.9
  396.7 6.1 copy-start.16
  417.1 6.3 copy-start.7
  423.3 20.1 %collective-permute-start.3 = (bf16[768,512]{1,0:T(8,128)(2,1)}, bf16[768,512]{1,0:T(8,128)(2,1)}, u32[]{:S(2)}, u32[]{:S(2)}) collective-permute-start(bf16[768,512]{1,0:T(8,128)(2,1)} %get-tuple-element.63), channel_id=1, source_target_pairs={{0,2},{1,3},{2,0},{3,1},{4,6},{5,7},{6,4},{7,5},{8,10},{9,11},{10,... | collective-permute-start | bytes 2359304 | tf_op jit(solution)/shard_map/ppermute | solution.py:757
  425.8 4.6 copy-start.38
  430.4 34.5 %collective-permute-start.5 = (bf16[768,512]{1,0:T(8,128)(2,1)}, bf16[768,512]{1,0:T(8,128)(2,1)}, u32[]{:S(2)}, u32[]{:S(2)}) collective-permute-start(bf16[768,512]{1,0:T(8,128)(2,1)} %get-tuple-element.63), channel_id=1, source_target_pairs={{0,1},{1,0},{2,3},{3,2},{4,5},{5,4},{6,7},{7,6},{8,9},{9,8},{10,11... | collective-permute-start | bytes 2359304 | tf_op jit(solution)/shard_map/ppermute | solution.py:761
  430.8 32.5 %all-to-all-start.2 = ((bf16[8,96,512]{2,1,0:T(8,128)(2,1)}), bf16[8,96,512]{2,1,0:T(8,128)(2,1)S(1)}, u32[]{:S(2)}, u32[]{:S(2)}) async-start(bf16[8,96,512]{2,1,0:T(8,128)(2,1)} %bitcast.26), calls=%async_computation.2 | async-start | bytes 1572864 | tf_op jit(solution)/shard_map/all_to_all | solution.py:1083
  435.9 337.3 %all-reduce.5.cloned.1.call-start = ((), (), s32[]{:S(2)}) async-start(), calls=%async_computation.3 | async-start | bytes 4194304 | tf_op jit(solution)/shard_map/psum | solution.py:1323
  443.4 21.6 %collective-permute-start.4 = (bf16[768,512]{1,0:T(8,128)(2,1)}, bf16[768,512]{1,0:T(8,128)(2,1)}, u32[]{:S(2)}, u32[]{:S(2)}) collective-permute-start(bf16[768,512]{1,0:T(8,128)(2,1)} %collective-permute-done.3), channel_id=1, source_target_pairs={{0,1},{1,0},{2,3},{3,2},{4,5},{5,4},{6,7},{7,6},{8,9},{9,8},{10,11... | collective-permute-start | bytes 2359304 | tf_op jit(solution)/shard_map/ppermute | solution.py:761
  443.4 18.9 %copy-start.10 = (f32[768,512]{1,0:T(8,128)S(1)}, f32[768,512]{1,0:T(8,128)}, u32[]{:S(2)}) copy-start(f32[768,512]{1,0:T(8,128)} %copy-done.8) | copy-start | bytes 4718596
  443.4 19.9 %copy-start.51 = (s32[768]{0:T(1024)S(1)}, s32[768]{0:T(1024)}, u32[]{:S(2)}) copy-start(s32[768]{0:T(1024)} %copy-done.50) | copy-start | bytes 9220
  476.7 9.6 %copy-start.31 = (bf16[768,512]{0,1:T(8,128)(2,1)S(1)}, bf16[768,512]{0,1:T(8,128)(2,1)}, u32[]{:S(2)}) copy-start(bf16[768,512]{0,1:T(8,128)(2,1)} %copy-done.30) | copy-start | bytes 2359300
  503.7 4.0 copy-start.5
  503.7 4.2 copy-start.12
  503.7 4.3 copy-start.28
  503.7 8.7 %slice-start = ((s8[7864320]{0:T(1024)(128)(4,1)}), s8[4194304]{0:T(1024)(128)(4,1)S(1)}, s32[]{:S(2)}) async-start(s8[7864320]{0:T(1024)(128)(4,1)} %bitcast.187), calls=%async_computation.4 | async-start | bytes 8388608
  507.9 4.5 slice-start.1
  529.9 19.1 %copy-start.17 = (f32[768,4,128]{0,2,1:T(8,128)S(1)}, f32[768,4,128]{0,2,1:T(8,128)}, u32[]{:S(2)}) copy-start(f32[768,4,128]{0,2,1:T(8,128)} %get-tuple-element.91) | copy-start | bytes 4718596
  529.9 19.3 %copy-start.27 = (f32[768,128]{0,1:T(8,128)S(1)}, f32[768,128]{0,1:T(8,128)}, u32[]{:S(2)}) copy-start(f32[768,128]{0,1:T(8,128)} %get-tuple-element.96) | copy-start | bytes 1179652
  760.7 4.4 copy-start.23
  767.6 2.6 copy-start.33
  767.6 3.9 copy-start.52
  771.5 5.8 copy-start.1
  (18 other events, 29.5 us)
Sparse Core Ops, SparseCore 0:
  530.0 127.2 all-reduce.4

commit v3 on v2

--- a/solution.py
+++ b/solution.py
@@ -12,18 +12,9 @@
 QH = 2
 
 
-PRECISE = lax.Precision.HIGHEST
+PRECISE = lax.Precision.HIGH
 EPSILON = 1e-06
 MASKED = -1e30
-
-
-def half_turn(values):
-    middle = values.shape[-1] // 2
-    return jnp.concatenate([-values[..., middle:], values[..., :middle]], axis=-1)
-
-
-def undo_turn(values, cosine, sine):
-    return values * cosine - half_turn(values * sine)
 
 
 def rotary_tables(lengths, tok_rows):
@@ -37,7 +28,7 @@
     frequency = jnp.exp(-math.log(10000.0) * jnp.arange(0, HEAD, 2, dtype=jnp.float32) / HEAD)
     angles = offsets[:, None] * frequency[None, :]
     angles = jnp.concatenate([angles, angles], axis=1)
-    return (segment, jnp.cos(angles)[:, None, :], jnp.sin(angles)[:, None, :])
+    return (segment, jnp.cos(angles), jnp.sin(angles))
 
 
 def pair_gates(logits, routes):
@@ -61,23 +52,11 @@
     return (target, position, position < capacity)
 
 
-def norm_stats(values, gain):
-    factor = lax.rsqrt(jnp.mean(values * values, axis=1, keepdims=True) + EPSILON)
-    scaled = values * factor
-    return (factor, scaled, scaled * gain)
-
-
-def block_scores(query, keys, segment, start, block_rows, scale):
-    places = jnp.arange(keys.shape[0], dtype=jnp.int32)
-    allowed = (segment[start : start + block_rows, None] == segment[None, :]) & (
-        places[:, None] >= places[None, :]
-    )
-    raw = jnp.einsum("qhd,khd->hqk", query, keys, preferred_element_type=jnp.float32) * scale
-    return jnp.where(allowed[None], raw, MASKED)
-
-
 MESH = pl.DeviceIdType.MESH
 MIB = 1 << 20
+AHEAD_DEAL = 2
+AHEAD = 2
+EARLY = 2
 
 
 def flip(number, other, count):
@@ -161,15 +140,16 @@
             pltpu.SemaphoreType.DMA((chunks, spots)),
         ]
 
-    def __init__(self, place, source, target, sems, over_expert, sharers=1):
+    def __init__(self, place, source, target, sems, over_expert, sharers=1, by_group=None):
         self.place, self.source, self.target = place, source, target
+        self.by_group = over_expert if by_group is None else by_group
         self.first_send, self.first_land, self.side_send, self.side_land, self.core_send, self.core_land = sems
         self.over_expert, self.sharers = over_expert, sharers
         self.width = source.shape[3]
         self.chunks = target.shape[1]
 
     def owner(self, chunk):
-        if not self.over_expert:
+        if not self.by_group:
             return chunk
         half, odd, pair = self.place.groups // 2, lax.rem(chunk, 2), lax.div(chunk, 2)
         even_way = jnp.minimum(chunk, 1) * half + pair
@@ -187,20 +167,24 @@
             return self.source.at[:, owner]
         return self.source.at[:, lax.div(owner, self.sharers)]
 
-    def start(self):
+    def send(self, chunk):
+        place = self.place
+        peer = self.owner(chunk)
+        remote(
+            self.block(peer),
+            self.spot_of(place.expert, place.tensor),
+            self.first_send.at[chunk],
+            self.first_land.at[chunk],
+            place.device(peer, place.tensor),
+        ).start()
+
+    def start(self, ahead):
         place = self.place
         own = self.owner(0)
         if not self.over_expert:
             return
-        for chunk in range(1, self.chunks):
-            peer = self.owner(chunk)
-            remote(
-                self.block(peer),
-                self.spot_of(place.expert, place.tensor),
-                self.first_send.at[chunk],
-                self.first_land.at[chunk],
-                place.device(peer, place.tensor),
-            ).start()
+        for chunk in range(1, min(ahead + 1, self.chunks)):
+            self.send(chunk)
         copy = pltpu.make_async_copy(
             self.block(own), self.spot_of(own, place.tensor), self.first_send.at[0]
         )
@@ -267,6 +251,9 @@
         place = self.place
         owner = self.owner(chunk)
         flipped = 1 - 2 * place.core
+        if not self.over_expert:
+            mine = self.spot_of(owner, place.tensor)
+            pltpu.make_async_copy(self.block(owner), mine, self.first_send.at[chunk]).wait()
         for step in range(place.spots):
             came = self.spot_of(owner, place.before(step) + flipped)
             remote(
@@ -294,8 +281,6 @@
                     device,
                 ).wait_send()
 
-        else:
-            pltpu.make_async_copy(self.block(owner), mine, self.first_send.at[chunk]).wait()
         for step in range(1, place.spots):
             remote(
                 mine,
@@ -312,10 +297,10 @@
 
 class Collect:
     @staticmethod
-    def scratch(chunks, kinds, spots, rows, width):
+    def scratch(chunks, kinds, spots, rows, width, slots=2):
         return [
-            pltpu.VMEM((2, kinds, spots, 2, rows, width), jnp.bfloat16),
-            pltpu.VMEM((2, kinds, max(spots - 1, 1), rows, width), jnp.bfloat16),
+            pltpu.VMEM((slots, kinds, spots, 2, rows, width), jnp.bfloat16),
+            pltpu.VMEM((slots, kinds, max(spots - 1, 1), rows, width), jnp.bfloat16),
             pltpu.VMEM((chunks, kinds, spots, rows, width), jnp.bfloat16),
             pltpu.VMEM((chunks, kinds, max(spots - 1, 1), rows, width), jnp.bfloat16),
             pltpu.SemaphoreType.DMA((chunks,)),
@@ -329,11 +314,12 @@
         self.stage, self.side, self.core_in, self.side_in = refs[:4]
         self.core_send, self.core_land, self.side_send, self.side_land = refs[4:]
         self.chunks = self.core_in.shape[0]
+        self.slots = self.stage.shape[0]
 
     def core_copy(self, chunk):
         place = self.place
         return remote(
-            self.stage.at[lax.rem(chunk, 2), :, :, 1 - place.core],
+            self.stage.at[lax.rem(chunk, self.slots), :, :, 1 - place.core],
             self.core_in.at[chunk],
             self.core_send.at[chunk],
             self.core_land.at[chunk],
@@ -343,7 +329,7 @@
     def side_copy(self, chunk, step):
         place = self.place
         return remote(
-            self.side.at[lax.rem(chunk, 2), :, step - 1],
+            self.side.at[lax.rem(chunk, self.slots), :, step - 1],
             self.side_in.at[chunk, :, step - 1],
             self.side_send.at[chunk, step - 1],
             self.side_land.at[chunk, step - 1],
@@ -351,22 +337,22 @@
         )
 
     def free_stage(self, chunk):
-        @pl.when(chunk >= 2)
+        @pl.when(chunk >= self.slots)
         def _():
-            self.core_copy(chunk - 2).wait_send()
+            self.core_copy(chunk - self.slots).wait_send()
 
     def first(self, chunk):
         self.core_copy(chunk).start()
 
     def second(self, chunk):
         place = self.place
-        slot = lax.rem(chunk, 2)
+        slot = lax.rem(chunk, self.slots)
         self.core_copy(chunk).wait_recv()
 
-        @pl.when(chunk >= 2)
+        @pl.when(chunk >= self.slots)
         def _():
             for step in range(1, place.spots):
-                self.side_copy(chunk - 2, step).wait_send()
+                self.side_copy(chunk - self.slots, step).wait_send()
 
         for step in range(1, place.spots):
             there = lax.rem(place.spot + step, place.spots)
@@ -378,7 +364,7 @@
 
     def third(self, chunk):
         place = self.place
-        slot = lax.rem(chunk, 2)
+        slot = lax.rem(chunk, self.slots)
         total = self.stage[slot, :, place.spot, place.core].astype(jnp.float32) + self.core_in[
             chunk, :, place.spot
         ].astype(jnp.float32)
@@ -388,7 +374,7 @@
         return total
 
     def finish(self):
-        for chunk in range(max(self.chunks - 2, 0), self.chunks):
+        for chunk in range(max(self.chunks - self.slots, 0), self.chunks):
             self.core_copy(chunk).wait_send()
             for step in range(1, self.place.spots):
                 self.side_copy(chunk, step).wait_send()
@@ -402,10 +388,12 @@
     place = Place()
     spread = Spread(place, source, target, sems, over_expert)
     place.meet(over_expert)
-    spread.start()
+    spread.start(AHEAD_DEAL)
 
     def step(turn, carry):
         when(turn < spread.chunks, spread.first, turn)
+        if over_expert:
+            when(turn + 1 + AHEAD_DEAL < spread.chunks, spread.send, turn + 1 + AHEAD_DEAL)
         when(turn >= 1, spread.second, turn - 1)
         return carry
 
@@ -494,17 +482,17 @@
     return total
 
 
-def experts_kernel(sharers, halves, piece_count, *refs):
-    (source, gates, gate_hbm, up_hbm, down_hbm), refs = refs[:5], refs[5:]
-    pieces, refs = refs[:piece_count], refs[piece_count:]
+def experts_kernel(sharers, *refs):
     (
-        inbox, grads_out, middle_out, gate_out, up_out, returned,
+        source, source_grads, gates, gate_hbm, up_hbm, down_hbm,
+        inbox, inbox_grads, grads_out, middle_out, gate_out, up_out, returned,
         gate_w, up_w, down_w, rows, grads, middle, gate_g, up_g, closing, gates_in,
-        load_sem, piece_sem, store_sem, back_send, back_land, mark_send, mark_land,
-    ) = refs[:23]
+        load_sem, store_sem, back_send, back_land, mark_send, mark_land,
+    ) = refs[:29]
     place = Place()
-    spread = Spread(place, source, inbox, refs[23:29], True, sharers)
-    collect = Collect(place, refs[29:])
+    spread = Spread(place, source, inbox, refs[29:35], True, sharers)
+    spread_grads = Spread(place, source_grads, inbox_grads, refs[35:41], False, by_group=True)
+    collect = Collect(place, refs[41:])
     chunks = spread.chunks
     width = source.shape[3]
     units = gate_w.shape[1]
@@ -540,7 +528,7 @@
             place.device(peer, place.tensor),
         )
 
-    spread.start()
+    spread.start(AHEAD)
     for chunk in range(1, chunks):
         mark_copy(chunk).start()
     own_mark = pltpu.make_async_copy(
@@ -548,6 +536,8 @@
     )
     own_mark.start()
     own_mark.wait()
+    for chunk in range(EARLY):
+        spread_grads.first(chunk)
 
     def stores(owner):
         return [
@@ -558,28 +548,13 @@
         ]
 
     def fetches(owner):
-        copies = [pltpu.make_async_copy(inbox.at[0, owner], rows, load_sem.at[3])]
-        number = 0
-        for first, count in halves:
-            for step in range(place.spots):
-                for other in range(2):
-                    tensor = place.before(step)
-                    if other:
-                        tensor = tensor + 1 - 2 * place.core
-                    column = pl.multiple_of(tensor * width, 128)
-                    copies.append(
-                        pltpu.make_async_copy(
-                            pieces[number].at[owner],
-                            grads.at[pl.ds(first, count), pl.ds(column, width)],
-                            piece_sem.at[number],
-                        )
-                    )
-                    number += 1
-        return copies
+        return [
+            pltpu.make_async_copy(inbox.at[0, owner], rows, load_sem.at[3]),
+            pltpu.make_async_copy(inbox_grads.at[0, owner], grads, load_sem.at[4]),
+        ]
 
     def work(chunk):
         owner = spread.owner(chunk)
-        slot = lax.rem(chunk, 2)
 
         @pl.when(chunk == 0)
         def _():
@@ -593,10 +568,10 @@
             mark_landed(chunk).wait_recv()
 
         spread.third(chunk)
+        spread_grads.third(chunk)
         copies = fetches(owner)
         for fetch in copies:
             fetch.start()
-        collect.free_stage(chunk)
         for fetch in copies:
             fetch.wait()
         wide = gates_in.shape[2]
@@ -618,46 +593,60 @@
             up_g[:, here] = (grad * act).astype(jnp.bfloat16)
         for store in stores(owner):
             store.start()
+        made, fed = 2 * chunk, 2 * chunk + 1
+        when(chunk >= 1, collect.second, made - 1)
+        when(chunk >= 1, close, made - 2)
+        collect.free_stage(made)
         for spot in range(place.spots):
             for core in range(2):
                 first = (spot * 2 + core) * width
                 here = slice(first, first + width)
-                collect.stage[slot, 0, spot, core] = jnp.dot(
+                collect.stage[lax.rem(made, 4), 0, spot, core] = jnp.dot(
                     middle[...], down_w[:, here], preferred_element_type=jnp.float32
                 ).astype(jnp.bfloat16)
-                collect.stage[slot, 1, spot, core] = (
+        collect.first(made)
+        collect.free_stage(fed)
+        for spot in range(place.spots):
+            for core in range(2):
+                first = (spot * 2 + core) * width
+                here = slice(first, first + width)
+                collect.stage[lax.rem(fed, 4), 0, spot, core] = (
                     dot_nt(gate_g[...], gate_w[here, :]) + dot_nt(up_g[...], up_w[here, :])
                 ).astype(jnp.bfloat16)
-        collect.first(chunk)
-
-    def back_copy(chunk):
-        owner = spread.owner(chunk)
+        collect.first(fed)
+        collect.second(made)
+        when(chunk >= 1, close, made - 1)
+
+    def back_copy(item, owner=None):
+        peer = spread.owner(lax.div(item, 2))
         return remote(
-            closing.at[lax.rem(chunk, 2)],
-            returned.at[:, place.expert],
-            back_send.at[chunk],
-            back_land.at[chunk],
-            place.device(owner, place.tensor),
-        )
-
-    def close(chunk):
-        slot = lax.rem(chunk, 2)
-        total = collect.third(chunk)
-
-        @pl.when(chunk >= 3)
+            closing.at[lax.rem(item, 4)],
+            returned.at[lax.rem(item, 2), place.expert if owner is None else owner],
+            back_send.at[item],
+            back_land.at[item],
+            place.device(peer, place.tensor),
+        )
+
+    def close(item):
+        slot = lax.rem(item, 4)
+        total = collect.third(item)[0]
+
+        @pl.when(item >= 6)
         def _():
-            back_copy(chunk - 2).wait_send()
+            back_copy(item - 4).wait_send()
 
         closing[slot] = total.astype(jnp.bfloat16)
 
-        @pl.when(chunk > 0)
+        @pl.when(item >= 2)
         def _():
-            back_copy(chunk).start()
-
-        @pl.when(chunk == 0)
+            back_copy(item).start()
+
+        @pl.when(item < 2)
         def _():
             own = pltpu.make_async_copy(
-                closing.at[slot], returned.at[:, place.expert], back_send.at[chunk]
+                closing.at[slot],
+                returned.at[lax.rem(item, 2), place.expert],
+                back_send.at[item],
             )
             own.start()
             own.wait()
@@ -665,40 +654,40 @@
     def step(turn, carry):
         now = turn - 2
         when(turn < chunks, spread.first, turn)
+        when(turn + 1 + AHEAD < chunks, spread.send, turn + 1 + AHEAD)
         when((turn >= 1) & (turn <= chunks), spread.second, turn - 1)
-        when(now >= 2, close, now - 2)
-        when((now >= 1) & (now <= chunks), collect.second, now - 1)
-        when((now >= 0) & (now < chunks), work, now)
+        when(turn + EARLY < chunks, spread_grads.first, turn + EARLY)
+        when((turn >= 1) & (turn <= chunks), spread_grads.second, turn - 1)
+        when(now >= 0, work, now)
         return carry
 
-    lax.fori_loop(0, chunks + 4, step, 0)
+    lax.fori_loop(0, chunks + 2, step, 0)
+    items = 2 * chunks
+    collect.second(items - 1)
+    close(items - 2)
+    close(items - 1)
 
     def last(turn, carry):
         spread.finish(turn)
+        spread_grads.finish(turn)
 
         @pl.when(turn > 0)
         def _():
-            owner = spread.owner(turn)
             mark_copy(turn).wait_send()
-            remote(
-                closing.at[0],
-                returned.at[:, owner],
-                back_send.at[turn],
-                back_land.at[turn],
-                place.device(owner, place.tensor),
-            ).wait_recv()
+            for item in (2 * turn, 2 * turn + 1):
+                back_copy(item, spread.owner(turn)).wait_recv()
 
         return carry
 
     lax.fori_loop(0, chunks, last, 0)
     for store in stores(spread.owner(chunks - 1)):
         store.wait()
-    for chunk in range(max(chunks - 2, 1), chunks):
-        back_copy(chunk).wait_send()
+    for item in range(max(items - 4, 2), items):
+        back_copy(item).wait_send()
     collect.finish()
 
 
-def experts(source, gates, gate_w, up_w, down_w, pieces, halves, sharers, collective):
+def experts(source, source_grads, gates, gate_w, up_w, down_w, sharers, collective):
     _, capacity, width = source.shape
     groups, parts = lax.axis_size("expert"), lax.axis_size("tensor")
     spots = parts // 2
@@ -707,8 +696,9 @@
     anywhere = pl.BlockSpec(memory_space=pl.ANY)
     hidden_rows = jax.ShapeDtypeStruct((groups, capacity, units), low)
     return pl.pallas_call(
-        functools.partial(experts_kernel, sharers, halves, len(pieces)),
+        functools.partial(experts_kernel, sharers),
         out_shape=(
+            jax.ShapeDtypeStruct((1, groups, capacity, model_width), low),
             jax.ShapeDtypeStruct((1, groups, capacity, model_width), low),
             jax.ShapeDtypeStruct((groups, capacity, model_width), low),
             hidden_rows,
@@ -716,8 +706,8 @@
             hidden_rows,
             jax.ShapeDtypeStruct((2, groups, capacity, width), low),
         ),
-        in_specs=[anywhere] * (5 + len(pieces)),
-        out_specs=(anywhere,) * 6,
+        in_specs=[anywhere] * 6,
+        out_specs=(anywhere,) * 7,
         scratch_shapes=[
             pltpu.VMEM((model_width, units), low),
             pltpu.VMEM((model_width, units), low),
@@ -727,38 +717,37 @@
             pltpu.VMEM((capacity, units), low),
             pltpu.VMEM((capacity, units), low),
             pltpu.VMEM((capacity, units), low),
-            pltpu.VMEM((2, 2, capacity, width), low),
+            pltpu.VMEM((4, capacity, width), low),
             pltpu.VMEM((groups,) + gates.shape[1:], jnp.float32),
+            pltpu.SemaphoreType.DMA((5,)),
             pltpu.SemaphoreType.DMA((4,)),
-            pltpu.SemaphoreType.DMA((len(pieces),)),
-            pltpu.SemaphoreType.DMA((4,)),
-            pltpu.SemaphoreType.DMA((groups,)),
-            pltpu.SemaphoreType.DMA((groups,)),
+            pltpu.SemaphoreType.DMA((2 * groups,)),
+            pltpu.SemaphoreType.DMA((2 * groups,)),
             pltpu.SemaphoreType.DMA((groups,)),
             pltpu.SemaphoreType.DMA((groups,)),
         ]
         + Spread.scratch(groups, spots)
-        + Collect.scratch(groups, 2, spots, capacity, width),
+        + Spread.scratch(groups, spots)
+        + Collect.scratch(2 * groups, 1, spots, capacity, width, 4),
         compiler_params=pltpu.CompilerParams(
             collective_id=collective, has_side_effects=True, vmem_limit_bytes=60 * MIB
         ),
         cost_estimate=lasting(180),
-    )(source[None], gates, gate_w, up_w, down_w, *pieces)
-
-
-def tensor_pieces(rows):
+    )(source[None], source_grads[None], gates, gate_w, up_w, down_w)
+
+
+def across_spots(rows):
     parts = lax.axis_size("tensor")
-    spots = parts // 2
-    swap = [(index, index ^ 1) for index in range(parts)]
-    pieces = []
-    for step in range(spots):
-        came = rows
-        if step:
-            came = lax.ppermute(
-                rows, "tensor", [(index, (index + 2 * step) % parts) for index in range(parts)]
-            )
-        pieces.append(came)
-    return [piece for came in pieces for piece in (came, lax.ppermute(came, "tensor", swap))]
+    pairs = [
+        [(index, (index + 2 * step) % parts) for index in range(parts)]
+        for step in range(parts // 2)
+    ]
+    return [rows] + [lax.ppermute(rows, "tensor", pair) for pair in pairs[1:]]
+
+
+def across_cores(pieces):
+    swap = [(index, index ^ 1) for index in range(lax.axis_size("tensor"))]
+    return [part for piece in pieces for part in (piece, lax.ppermute(piece, "tensor", swap))]
 
 
 def closing_kernel(count, *refs):
@@ -1078,6 +1067,185 @@
     )(normed_t, gain, marks, hidden, scaled, routed, small, *grads, *weights, *after)
 
 
+def dot_tn(left, right):
+    return lax.dot_general(
+        left, right, (((0,), (0,)), ((), ())), preferred_element_type=jnp.float32
+    )
+
+
+def bands(tokens):
+    size = 256 if tokens % 256 == 0 else tokens
+    return [(first, size) for first in range(0, tokens, size)]
+
+
+def masked_scores(query, keys, segment_column, segment_row, first, size, column):
+    last = first + size
+    rows = slice(first, last)
+    scores = dot_nt(query[rows, column], keys[:last, column]) * (1.0 / math.sqrt(HEAD))
+    place = lax.broadcasted_iota(jnp.int32, (size, last), 0) + first
+    other = lax.broadcasted_iota(jnp.int32, (size, last), 1)
+    allowed = (segment_column[rows, :] == segment_row[:, :last]) & (place >= other)
+    return jnp.where(allowed, scores, MASKED)
+
+
+def attend_kernel(
+    resid, gain, router, w_query, w_key, w_value, cosine, sine, segment_column, segment_row,
+    normed, normed_t, factor, logits, query, keys, values, heads, log_total,
+):
+    tokens, columns = query.shape
+    low = jnp.bfloat16
+    for first, size in bands(tokens):
+        rows = slice(first, first + size)
+        value = resid[rows, :].astype(jnp.float32)
+        scale = lax.rsqrt(jnp.mean(value * value, axis=1, keepdims=True) + EPSILON)
+        value = value * scale * gain[...]
+        high = value.astype(low)
+        rest = (value - high.astype(jnp.float32)).astype(low)
+        factor[rows, :] = scale
+        normed[rows, :] = high
+        normed_t[:, rows] = high.T
+        logits[rows, :] = jnp.dot(
+            high, router[...], preferred_element_type=jnp.float32
+        ) + jnp.dot(rest, router[...], preferred_element_type=jnp.float32)
+        values[rows, :] = jnp.dot(
+            high, w_value[...], preferred_element_type=jnp.float32
+        ).astype(low)
+        for weight, out in ((w_query, query), (w_key, keys)):
+            flat = jnp.dot(high, weight[...], preferred_element_type=jnp.float32)
+            for head in range(columns // HEAD):
+                column = slice(head * HEAD, (head + 1) * HEAD)
+                part = flat[:, column]
+                turned = pltpu.roll(part, HEAD // 2, 1)
+                out[rows, column] = (part * cosine[rows, :] + turned * sine[rows, :]).astype(low)
+    for head in range(columns // HEAD):
+        column = slice(head * HEAD, (head + 1) * HEAD)
+        for first, size in bands(tokens):
+            last = first + size
+            rows = slice(first, last)
+            scores = masked_scores(query, keys, segment_column, segment_row, first, size, column)
+            top = jnp.max(scores, axis=1, keepdims=True)
+            expo = jnp.exp(scores - top)
+            total = jnp.sum(expo, axis=1, keepdims=True)
+            probs = (expo / total).astype(low)
+            heads[rows, column] = jnp.dot(
+                probs, values[:last, column], preferred_element_type=jnp.float32
+            ).astype(low)
+            log_total[rows, head : head + 1] = top + jnp.log(total)
+
+
+def attend(resid, gain, router, weights, cosine, sine, segment):
+    tokens, model_width = resid.shape
+    columns = weights[0].shape[1]
+    low, full = jnp.bfloat16, jnp.float32
+    block = jax.ShapeDtypeStruct((tokens, columns), low)
+    inside = pl.BlockSpec(memory_space=pltpu.VMEM)
+    return pl.pallas_call(
+        attend_kernel,
+        out_shape=(
+            jax.ShapeDtypeStruct((tokens, model_width), low),
+            jax.ShapeDtypeStruct((model_width, tokens), low),
+            jax.ShapeDtypeStruct((tokens, 1), full),
+            jax.ShapeDtypeStruct((tokens, router.shape[1]), full),
+            block,
+            block,
+            block,
+            block,
+            jax.ShapeDtypeStruct((tokens, columns // HEAD), full),
+        ),
+        in_specs=[inside] * 10,
+        out_specs=(inside,) * 9,
+        compiler_params=pltpu.CompilerParams(vmem_limit_bytes=56 * MIB),
+        cost_estimate=lasting(20),
+    )(resid, gain, router, *weights, cosine, sine, segment[:, None], segment[None, :])
+
+
+def attend_back_kernel(
+    grads, w_out, gates, heads, query, keys, values, log_total, cosine, sine,
+    segment_column, segment_row,
+    query_grad, key_grad, value_grad, gate_grad, weight_grad,
+    heads_grad, gated, key_sum, value_sum,
+):
+    tokens, columns = query.shape
+    low = jnp.bfloat16
+    span = columns // gates.shape[1]
+    scale = 1.0 / math.sqrt(HEAD)
+    for first, size in bands(tokens):
+        rows = slice(first, first + size)
+        plain = dot_nt(grads[rows, :], w_out[...])
+        for expert in range(gates.shape[1]):
+            column = slice(expert * span, (expert + 1) * span)
+            gate = gates[rows, expert : expert + 1]
+            head = heads[rows, column].astype(jnp.float32)
+            gate_grad[rows, expert : expert + 1] = jnp.sum(
+                plain[:, column] * head, axis=1, keepdims=True
+            )
+            heads_grad[rows, column] = (plain[:, column] * gate).astype(low)
+            gated[rows, column] = (head * gate).astype(low)
+    weight_grad[...] = dot_tn(gated[...], grads[...]).astype(low)
+
+    def unturn(value, rows):
+        turned = pltpu.roll(value * sine[rows, :], HEAD // 2, 1)
+        return value * cosine[rows, :] + turned
+
+    for head in range(columns // HEAD):
+        column = slice(head * HEAD, (head + 1) * HEAD)
+        for first, size in bands(tokens):
+            last = first + size
+            rows = slice(first, last)
+            scores = masked_scores(query, keys, segment_column, segment_row, first, size, column)
+            probs = jnp.exp(scores - log_total[rows, head : head + 1])
+            value_part = dot_tn(probs.astype(low), heads_grad[rows, column])
+            prob_grad = dot_nt(heads_grad[rows, column], values[:last, column])
+            score_grad = (
+                probs * (prob_grad - jnp.sum(probs * prob_grad, axis=1, keepdims=True))
+            ).astype(low)
+            query_grad[rows, column] = unturn(
+                jnp.dot(score_grad, keys[:last, column], preferred_element_type=jnp.float32)
+                * scale,
+                rows,
+            ).astype(low)
+            key_part = dot_tn(score_grad, query[rows, column])
+            if first:
+                value_sum[:first, :] += value_part[:first]
+                key_sum[:first, :] += key_part[:first]
+            value_sum[rows, :] = value_part[first:]
+            key_sum[rows, :] = key_part[first:]
+        whole = slice(0, tokens)
+        key_grad[:, column] = unturn(key_sum[...] * scale, whole).astype(low)
+        value_grad[:, column] = value_sum[...].astype(low)
+
+
+def attend_back(grads, w_out, gates, heads, query, keys, values, log_total, cosine, sine, segment):
+    tokens, model_width = grads.shape
+    columns = query.shape[1]
+    low, full = jnp.bfloat16, jnp.float32
+    block = jax.ShapeDtypeStruct((tokens, columns), low)
+    inside = pl.BlockSpec(memory_space=pltpu.VMEM)
+    return pl.pallas_call(
+        attend_back_kernel,
+        out_shape=(
+            block,
+            block,
+            block,
+            jax.ShapeDtypeStruct(gates.shape, full),
+            jax.ShapeDtypeStruct(w_out.shape, low),
+        ),
+        in_specs=[inside] * 12,
+        out_specs=(inside,) * 5,
+        scratch_shapes=[
+            pltpu.VMEM((tokens, columns), low),
+            pltpu.VMEM((tokens, columns), low),
+            pltpu.VMEM((tokens, HEAD), full),
+            pltpu.VMEM((tokens, HEAD), full),
+        ],
+        compiler_params=pltpu.CompilerParams(vmem_limit_bytes=56 * MIB),
+        cost_estimate=lasting(25),
+    )(
+        grads, w_out, gates, heads, query, keys, values, log_total, cosine, sine,
+        segment[:, None], segment[None, :],
+    )
+
+
 def to_expert(rows, group_count):
     count, width = rows.shape
     return lax.all_to_all(
@@ -1157,7 +1325,6 @@
     ).astype(low)
     dealt_grads, resid_low = lax.optimization_barrier((dealt_grads, resid_low))
     grad_cols_low = to_expert(dealt_grads, group_count)
-    grad_cols = grad_cols_low.astype(jnp.float32)
     gain_one, gain_two = own_cols(attn_gain), own_cols(mlp_gain)
     router_one = lax.dynamic_slice_in_dim(attn_router, col_first, col_width, 0)
     router_two = lax.dynamic_slice_in_dim(mlp_router, col_first, col_width, 0)
@@ -1172,49 +1339,36 @@
     to_slot = (
         (slot_ids[:, None] == chosen[0][None, :]) | (slot_ids[:, None] == chosen[1][None, :])
     ).astype(low)
-    slot_grads = jnp.dot(to_slot, grad_cols_low, preferred_element_type=jnp.float32).astype(low)
-    slot_grads = slot_grads.reshape(expert_count, capacity, col_width)
-    slot_grads, resid_low = lax.optimization_barrier((slot_grads, resid_low))
-    halves = ((0, capacity),)
-    grad_pieces = []
-    for first, count in halves:
-        block = jnp.repeat(slot_grads[:, first : first + count], sharers, axis=0)
-        grad_pieces.append(to_expert(block.reshape(group_count * count, col_width), group_count))
-
-    resid_in = resid_low.astype(jnp.float32)
     resid_cols = own_cols(resid_low).astype(jnp.float32)
     segment, cosine, sine = rotary_tables(seq_lengths[0], tok_rows)
-    scale = 1.0 / math.sqrt(HEAD)
+    sign = jnp.where(jnp.arange(HEAD) < HEAD // 2, -1.0, 1.0)
     local_heads = w_query.shape[1] // HEAD
     local_experts = local_heads // QH
     span = QH * HEAD
-    factor_one, scaled_one, normed_one = norm_stats(resid_in, attn_gain)
-    normed_low = normed_one.astype(low)
-    attn_logits = jnp.dot(normed_one, attn_router, precision=PRECISE)
+    experts_of = attn_router.shape[1]
+    router_high = lax.reduce_precision(attn_router, 8, 7)
+    router_parts = jnp.concatenate([router_high, attn_router - router_high], axis=1).astype(low)
+    router_parts = jnp.pad(router_parts, ((0, 0), (0, -router_parts.shape[1] % 128)))
+    normed_low, normed_t, factor_one, logit_parts, query, keys, values, heads_low, log_total = (
+        attend(
+            resid_low,
+            attn_gain[None],
+            router_parts,
+            (w_query, w_key, w_value),
+            cosine,
+            sine * sign,
+            segment,
+        )
+    )
+    attn_logits = logit_parts[:, :experts_of] + logit_parts[:, experts_of : 2 * experts_of]
     attn_gates, attn_mask = pair_gates(attn_logits, attn_routes)
     gate_table = jnp.sum(attn_gates[:, :, None] * attn_mask, axis=1)
     gate_local = lax.dynamic_slice_in_dim(gate_table, part_index * local_experts, local_experts, 1)
-    query_pre = jnp.dot(normed_low, w_query, preferred_element_type=jnp.float32).reshape(
-        tok_rows, local_heads, HEAD
-    )
-    key_pre = jnp.dot(normed_low, w_key, preferred_element_type=jnp.float32).reshape(
-        tok_rows, local_heads, HEAD
-    )
-    values = (
-        jnp.dot(normed_low, w_value, preferred_element_type=jnp.float32)
-        .astype(low)
-        .reshape(tok_rows, local_heads, HEAD)
-    )
-    query = (query_pre * cosine + half_turn(query_pre) * sine).astype(low)
-    keys = (key_pre * cosine + half_turn(key_pre) * sine).astype(low)
-    scores = block_scores(query, keys, segment, 0, tok_rows, scale)
-    top_score = jnp.max(scores, axis=-1, keepdims=True)
-    expo = jnp.exp(scores - top_score)
-    totals = jnp.sum(expo, axis=-1, keepdims=True)
-    probs = (expo / totals).astype(low)
-    head_blocks = jnp.einsum("hqk,khd->qhd", probs, values, preferred_element_type=jnp.float32)
-    log_total = top_score + jnp.log(totals)
-    heads_low = head_blocks.astype(low).reshape(tok_rows, local_heads * HEAD)
+    grad_cols_low, heads_low = lax.optimization_barrier((grad_cols_low, heads_low))
+    grad_cols = grad_cols_low.astype(jnp.float32)
+    slot_grads = jnp.dot(to_slot, grad_cols_low, preferred_element_type=jnp.float32).astype(low)
+    slot_grads = jnp.repeat(slot_grads.reshape(expert_count, capacity, col_width), sharers, axis=0)
+    slot_grads = to_expert(slot_grads.reshape(group_count * capacity, col_width), group_count)
     pieces, piece_rows = 4, tok_rows // 4
     attn_cols = collect_rows(
         functools.partial(make_attended, span),
@@ -1228,12 +1382,6 @@
         col_width,
         1,
     )
-    *grad_pieces, attn_cols = lax.optimization_barrier((*grad_pieces, attn_cols))
-    grad_pieces = [
-        piece
-        for (_, count), rows in zip(halves, grad_pieces)
-        for piece in tensor_pieces(rows.reshape(group_count, count, col_width))
-    ]
     hidden = resid_cols + attn_cols
     weighed = hidden * gain_two
     stats = jnp.concatenate(
@@ -1261,14 +1409,13 @@
     )
     gate_lines = jnp.pad(slot_gates.reshape(expert_count, capacity), ((0, 0), (0, -capacity % 128)))
     gate_lines = jnp.broadcast_to(gate_lines[:, None, :], (expert_count, 8, gate_lines.shape[1]))
-    inbox, slot_grads, middle, gate_grad, up_grad, returned = experts(
+    inbox, _, slot_grads, middle, gate_grad, up_grad, returned = experts(
         slot_rows.reshape(expert_count, capacity, col_width),
+        slot_grads.reshape(group_count, capacity, col_width),
         gate_lines,
         w_gate[0],
         w_up[0],
         w_down[0],
-        grad_pieces,
-        halves,
         sharers,
         2,
     )
@@ -1308,50 +1455,32 @@
     mlp_gain_grad = jnp.sum(norm_two_grad * scaled_two, axis=0)
     mean_two = (stats[2] + jnp.sum(mlp_logit_grad * mlp_logits, axis=1)) / model_width
     hidden_grad = grad_cols + factor_two * (norm_two_grad * gain_two - scaled_two * mean_two[:, None])
-    hidden_grad_low = side_by_side(tensor_pieces(hidden_grad.astype(low)))
-    gate_wide = jnp.repeat(gate_local, span, axis=1)
-    heads_float = heads_low.astype(jnp.float32)
-    out_w_grad = jnp.einsum(
-        "tc,td->cd",
-        (heads_float * gate_wide).astype(low),
+    rows = inbox.reshape(-1, model_width)
+    grad_rows = slot_grads.reshape(-1, model_width)
+    units = middle.shape[2]
+
+    def rows_product(left, right):
+        return jnp.einsum("sa,sb->ab", left, right, preferred_element_type=jnp.float32)
+
+    hidden_pieces = across_spots(hidden_grad.astype(low))
+    gate_w_grad = rows_product(rows, gate_grad.reshape(-1, units))
+    *hidden_pieces, gate_w_grad = lax.optimization_barrier((*hidden_pieces, gate_w_grad))
+    hidden_grad_low = side_by_side(across_cores(hidden_pieces))
+    query_pre_grad, key_pre_grad, value_pre_grad, local_gate_grad, out_w_grad = attend_back(
         hidden_grad_low,
-        preferred_element_type=jnp.float32,
-    )
-    out_w_grad, middle, up_grad, hidden_grad_low = lax.optimization_barrier(
-        (out_w_grad.astype(low), middle, up_grad, hidden_grad_low)
-    )
+        w_out,
+        gate_local,
+        heads_low,
+        query,
+        keys,
+        values,
+        log_total,
+        cosine,
+        sine * sign,
+        segment,
+    )
+    out_w_grad, middle, up_grad = lax.optimization_barrier((out_w_grad, middle, up_grad))
     out_w_grad = lax.psum(out_w_grad, "expert").astype(jnp.float32)
-    heads_plain = jnp.einsum(
-        "td,cd->tc", hidden_grad_low, w_out, preferred_element_type=jnp.float32
-    )
-    gate_products = heads_plain * heads_float
-    local_gate_grad = jnp.stack(
-        [
-            jnp.sum(gate_products[:, expert * span : (expert + 1) * span], axis=1)
-            for expert in range(local_experts)
-        ],
-        axis=1,
-    )
-    heads_grad = (heads_plain * gate_wide).astype(low).reshape(tok_rows, local_heads, HEAD)
-    scores = block_scores(query, keys, segment, 0, tok_rows, scale)
-    probs = jnp.exp(scores - log_total)
-    value_grad = jnp.einsum(
-        "hqk,qhd->khd", probs.astype(low), heads_grad, preferred_element_type=jnp.float32
-    )
-    prob_grad = jnp.einsum("qhd,khd->hqk", heads_grad, values, preferred_element_type=jnp.float32)
-    score_grad = (
-        probs * (prob_grad - jnp.sum(probs * prob_grad, axis=-1, keepdims=True))
-    ).astype(low)
-    query_grad = (
-        jnp.einsum("hqk,khd->qhd", score_grad, keys, preferred_element_type=jnp.float32) * scale
-    )
-    key_grad = (
-        jnp.einsum("hqk,qhd->khd", score_grad, query, preferred_element_type=jnp.float32) * scale
-    )
-    width = local_heads * HEAD
-    query_pre_grad = undo_turn(query_grad, cosine, sine).astype(low).reshape(tok_rows, width)
-    key_pre_grad = undo_turn(key_grad, cosine, sine).astype(low).reshape(tok_rows, width)
-    value_pre_grad = value_grad.astype(low).reshape(tok_rows, width)
     gate_grads = gather_tensor(local_gate_grad.T)
     gate_grads = gate_grads.reshape(part_count * local_experts, tok_rows).T
     attn_pair_grad = jnp.sum(attn_mask * gate_grads[:, None, :], axis=2)
@@ -1372,18 +1501,10 @@
     marks = jnp.stack(
         [factor_one[:, 0], jnp.sum(attn_logit_grad * attn_logits, axis=1)], axis=1
     )
-    rows = inbox.reshape(-1, model_width)
-    grad_rows = slot_grads.reshape(-1, model_width)
-    units = middle.shape[2]
-    gate_w_grad, up_w_grad = (
-        jnp.einsum("sd,sf->df", rows, grad.reshape(-1, units), preferred_element_type=jnp.float32)
-        for grad in (gate_grad, up_grad)
-    )
-    down_grad = jnp.einsum(
-        "sf,sd->fd", middle.reshape(-1, units), grad_rows, preferred_element_type=jnp.float32
-    )
+    up_w_grad = rows_product(rows, up_grad.reshape(-1, units))
+    down_grad = rows_product(middle.reshape(-1, units), grad_rows)
     *weight_grads, back_grad, small = closing(
-        normed_low.T,
+        normed_t,
         gain_one[None],
         jnp.pad(marks, ((0, 0), (0, 126))),
         hidden_grad,
@@ -1403,7 +1524,6 @@
         for back in (back_mixed, back_grad)
     )
     small = small.transpose(1, 0, 2).reshape(-1, model_width)
-    experts_of = attn_router.shape[1]
     return (
         mixed,
         tokens_grad,

time: 791 us -> 709 us (0.90)
  Pallas kernels: 437 us -> 500 us
  waiting for transfers between devices: 54 us -> 0.03 us
  matrix products: 140 us -> 91.4 us
  other arithmetic: 56.3 us -> 36.9 us
  local copies, waits for them, and re-layouts: 40.3 us -> 23.3 us
    pallas_call x1 -> x3, Pallas kernels: 186 us -> 245 us  [the longest x1 206 us: experts(): pl.pallas_call(functools.partial(experts_kernel, sharers), out_shape=(jax...]
    dot_general x15 -> x3, matrix products: 100 us -> 56.2 us  [rows_product(): jnp.einsum('sa,sb->ab', left, right, preferred_element_type=jnp.float32)]
    ppermute x6 -> x3, waiting for transfers between devices: 44 us -> 0.01 us  [the longest x2 0.01 us: across_cores(): lax.ppermute(piece, 'tensor', swap)]
    convert_element_type x4 -> x0, other arithmetic: 14.7 us -> none  [the longest x1 10.2 us: body(): score_grad = (probs * (prob_grad - jnp.sum(probs * prob_grad, axis=-1, ke...]
    all_to_all x3, waiting for transfers between devices: 9.96 us -> 0.01 us  [to_expert(): lax.all_to_all(rows.reshape(group_count, count // group_count, width), 'e...]
    unnamed x114 -> x74, local copies, waits for them, and re-layouts: 11.4 us -> 2.72 us
  transfers between devices with their start and end apart: 10 -> 7, of which waited for: 3 -> 0; matrix products, arithmetic and copies ran while one was open for 15% -> 12% of each run, Pallas kernels for 28% -> 35%
where the time goes in v3:
time: 709 us; the launch traced here: 704 us
  Pallas kernels  500 us (71%)
  matrix products  91.4 us (13%)
  other arithmetic  36.9 us (5%)
  local copies, waits for them, and re-layouts  23.3 us (3%)
  starting transfers between devices  21 us (3%)
  blocking collectives  16 us (2%)
  between operations  15 us (2%)
    pallas_call x1, Pallas kernels, experts(): pl.pallas_call(functools.partial(experts_kernel, sharers), out_shape=(jax...  206 us
    pallas_call x1, Pallas kernels, closing(): pl.pallas_call(functools.partial(closing_kernel, count), out_shape=(*(jax...  196 us
    dot_general x3, matrix products, rows_product(): jnp.einsum('sa,sb->ab', left, right, preferred_element_type=jnp.float32)  56.2 us
    pallas_call x1, Pallas kernels, spread_rows(): pl.pallas_call(functools.partial(spread_kernel, over_expert), out_shape=j...  31.2 us
    pallas_call x1, Pallas kernels, collect_rows(): pl.pallas_call(functools.partial(collect_kernel, make, len(operands)), ou...  28.1 us
    pallas_call x1, Pallas kernels, attend(): pl.pallas_call(attend_kernel, out_shape=(jax.ShapeDtypeStruct((tokens, mo...  21.6 us
    all_to_all x3, starting transfers between devices, to_expert(): lax.all_to_all(rows.reshape(group_count, count // group_count, width), 'e...  19.6 us
    pallas_call x1, Pallas kernels, attend_back(): pl.pallas_call(attend_back_kernel, out_shape=(block, block, block, jax.Sh...  17.5 us
  transfers between devices with their start and end apart: 7, of which 0 were waited for; matrix products, arithmetic and copies ran while one was open for 12% of the time, Pallas kernels for 35%

profile of v3, /device:TPU:20, one launch (start us, length us, event | category | flops | bytes accessed | tf_op | source)
XLA Modules:
  0.0 703.7 jit_solution(322100208251475190)
XLA Ops:
  8.1 1.0 copy-done
  9.1 1.7 fusion.38
  10.8 2.8 fusion.39
  13.6 31.2 %shard_map.273 = bf16[1,8,96,2048]{3,2,1,0:T(8,128)(2,1)} custom-call(bf16[1,8,96,512]{3,2,1,0:T(8,128)(2,1)} %bitcast.105), custom_call_target="tpu_custom_call" | custom-call | bytes 90000000 | tf_op jit(solution)/shard_map/pallas_call | solution.py:413
  44.8 8.0 %all-to-all-start = ((bf16[8,96,512]{2,1,0:T(8,128)(2,1)}), bf16[8,96,512]{2,1,0:T(8,128)(2,1)S(1)}, u32[]{:S(2)}, u32[]{:S(2)}) async-start(bf16[8,96,512]{2,1,0:T(8,128)(2,1)} %bitcast.2), calls=%async_computation | async-start | bytes 1572864 | tf_op jit(solution)/shard_map/all_to_all | solution.py:1251
  55.6 2.0 convert_reduce_fusion
  59.1 2.8 sine_multiply_fusion
  61.9 21.6 %shard_map.274 = (bf16[768,2048]{1,0:T(8,128)(2,1)}, bf16[2048,768]{1,0:T(8,128)(2,1)}, f32[768,1]{1,0:T(8,128)}, f32[768,128]{1,0:T(8,128)}, bf16[768,512]{1,0:...) custom-call(bf16[768,2048]{1,0:T(8,128)(2,1)} %bitcast.86, ...), custom_call_target="tpu_custom_call" | custom-call | bytes 60000000 | tf_op jit(solution)/shard_map/pallas_call | solution.py:1142
  84.0 3.1 fusion.13
  87.1 6.1 all-to-all-start.1
  94.2 1.1 copy.104
  96.4 1.2 reduce.9
  97.6 28.1 %shard_map.275 = f32[4,192,512]{2,1,0:T(8,128)S(1)} custom-call(bf16[4,192,512]{2,1,0:T(8,128)(2,1)S(1)} %bitcast.85, f32[4,192,2]{2,1,0:T(8,128)S(1)} %bitcast.84, bf16[512,2048]{1,0:T(8,128)(2,1)S(1)} %copy-done.2), custom_call_target="tpu_custom_call" | custom-call | bytes 78000000 | tf_op jit(solution)/shard_map/pallas_call | solution.py:458
  125.7 2.8 multiply_reduce_fusion.2
  128.5 1.4 fusion.36
  130.0 5.6 all-gather.3
  135.8 1.4 select_reduce_fusion
  137.4 3.2 fusion.10
  141.2 205.8 %shard_map.276 = (bf16[1,8,240,2048]{3,2,1,0:T(8,128)(2,1)}, bf16[1,8,240,2048]{3,2,1,0:T(8,128)(2,1)}, bf16[8,240,2048]{2,1,0:T(8,128)(2,1)}, bf16[8,240,1408]{...) custom-call(bf16[1,8,240,512]{3,2,1,0:T(8,128)(2,1)} %bitcast.104, ...), custom_call_target="tpu_custom_call" | custom-call | bytes 540000000 | tf_op jit(solution)/shard_map/pallas_call | solution.py:698
  347.0 2.4 fusion.82
  349.4 2.2 fusion.4
  351.6 3.3 fusion.1
  355.0 3.3 multiply_reduce_fusion.1
  358.3 1.6 copy.110
  359.9 3.1 copy.111
  363.0 2.3 fusion.32
  365.4 5.2 all-gather.4
  370.8 3.5 fusion.9
  374.2 3.0 copy.109
  377.2 4.6 fusion.81
  381.9 5.5 all-to-all-start.2
  388.2 18.6 %fusion.85.refs_13_ = f32[2048,1408]{1,0:T(8,128)} fusion(bf16[1920,2048]{1,0:T(8,128)(2,1)} %bitcast.118, bf16[1920,1408]{1,0:T(8,128)(2,1)} %bitcast.121), kind=kOutput, calls=%fused_computation.157 | convolution fusion | flops 11072962560 | bytes 24805376 | tf_op jit(solution)/shard_map/sa,sb->ab/dot_general | solution.py:1463
  408.9 2.9 fusion.40
  411.9 1.9 broadcast_select_fusion.7
  413.8 2.1 pad_maximum_fusion.grads
  415.9 17.5 %shard_map.277 = (bf16[768,512]{1,0:T(8,128)(2,1)}, bf16[768,512]{1,0:T(8,128)(2,1)}, bf16[768,512]{1,0:T(8,128)(2,1)}, f32[768,2]{1,0:T(8,128)}, bf16[512,2048]{1,0:T(8,128)(2,1)}) custom-call(bf16[768,2048]{1,0:T(8,128)(2,1)} %pad_maximum_fusion.grads, bf16[512,2048]{1,0:T(8,128)(2,1)} %w_out.1, f32[768,2]{1,0:T(8,128)} %copy-done.3, ...), custom_call_target="tpu_custom_call" | custom-call | bytes 75000000 | tf_op jit(solution)/shard_map/pallas_call | solution.py:1224
  433.4 1.1 copy.113
  434.5 5.2 all-gather.5
  439.7 18.8 %fusion.86.refs_14_ = f32[2048,1408]{1,0:T(8,128)} fusion(bf16[1920,2048]{1,0:T(8,128)(2,1)} %bitcast.119, bf16[1920,1408]{1,0:T(8,128)(2,1)} %bitcast.120), kind=kOutput, calls=%fused_computation.158 | convolution fusion | flops 11072962560 | bytes 24805376 | tf_op jit(solution)/shard_map/sa,sb->ab/dot_general | solution.py:1463
  458.6 18.7 %fusion.87 = f32[1408,2048,1]{1,0,2:T(8,128)} fusion(bf16[8,240,1408]{2,1,0:T(8,128)(2,1)} %get-tuple-element.73, bf16[8,240,2048]{2,1,0:T(8,128)(2,1)} %get-tuple-element.74), kind=kOutput, calls=%fused_computation.159 | convolution fusion | flops 11072962560 | bytes 24805376 | tf_op jit(solution)/shard_map/sa,sb->ab/dot_general | solution.py:1463
  478.9 1.8 fusion.34
  481.4 2.7 fusion.60.refs_5_
  484.1 195.8 %shard_map.278 = (bf16[2048,512]{1,0:T(8,128)(2,1)}, bf16[2048,512]{1,0:T(8,128)(2,1)}, bf16[2048,512]{1,0:T(8,128)(2,1)}, bf16[8,96,512]{2,1,0:T(8,128)(2,1)}, f32[4,24,512]{2,1,0:T(8,128)}) custom-call(bf16[2048,768]{1,0:T(8,128)(2,1)} %get-tuple-element.54.refs_0_, f32[1,512]{1,0:T(1,128)} %bitcast.113, f32[768,128]{1,0:T(8,128)} %pad.18.refs_2_, ...), custom_call_target="tpu_custom_call" | custom-call | bytes 420000000 | tf_op jit(solution)/shard_map/pallas_call | solution.py:1031
  679.8 4.3 convert_element_type.93
  684.2 2.6 convert_element_type.94
  686.8 2.6 convert_element_type.95
  690.7 1.7 fusion.41
  692.4 4.1 convert_element_type.96
  (157 shorter events, 15.2 us)
Async XLA Ops:
  7.2 1.9 copy-start
  8.1 5.5 copy-start.31
  13.6 39.2 %copy-start.34 = (s32[1,3]{1,0:T(1,128)S(1)}, s32[1,3]{1,0:T(1,128)}, u32[]{:S(2)}) copy-start(s32[1,3]{1,0:T(1,128)} %param.32) | copy-start | bytes 40
  13.6 41.0 %copy-start.19 = (s32[768,2]{0,1:T(2,128)S(1)}, s32[768,2]{0,1:T(2,128)}, u32[]{:S(2)}) copy-start(s32[768,2]{0,1:T(2,128)} %param.34) | copy-start | bytes 18436
  44.8 10.0 %copy-start.16 = (f32[2048,8]{0,1:T(8,128)S(1)}, f32[2048,8]{0,1:T(8,128)}, u32[]{:S(2)}) copy-start(f32[2048,8]{0,1:T(8,128)} %param.21) | copy-start | bytes 196612
  44.8 10.5 %copy-start.30 = (s32[1,1536]{1,0:T(1,128)S(1)}, s32[1,1536]{1,0:T(1,128)}, u32[]{:S(2)}) copy-start(s32[1,1536]{1,0:T(1,128)} %param.35) | copy-start | bytes 18436
  44.8 39.2 %all-to-all-start = ((bf16[8,96,512]{2,1,0:T(8,128)(2,1)}), bf16[8,96,512]{2,1,0:T(8,128)(2,1)S(1)}, u32[]{:S(2)}, u32[]{:S(2)}) async-start(bf16[8,96,512]{2,1,0:T(8,128)(2,1)} %bitcast.2), calls=%async_computation | async-start | bytes 1572864 | tf_op jit(solution)/shard_map/all_to_all | solution.py:1251
  84.0 53.4 %copy-start.23 = (s32[768]{0:T(1024)}, s32[768]{0:T(1024)S(1)}, u32[]{:S(2)}) copy-start(s32[768]{0:T(1024)S(1)} %get-tuple-element.83) | copy-start | bytes 9220
  84.0 53.4 %copy-start.25 = (s32[768]{0:T(1024)}, s32[768]{0:T(1024)S(1)}, u32[]{:S(2)}) copy-start(s32[768]{0:T(1024)S(1)} %get-tuple-element.84) | copy-start | bytes 9220
  84.0 3.1 copy-start.5
  87.1 6.2 copy-start.8
  87.1 8.2 %copy-start.17 = (s32[768,2]{0,1:T(2,128)S(1)}, s32[768,2]{0,1:T(2,128)}, u32[]{:S(2)}) copy-start(s32[768,2]{0,1:T(2,128)} %param.33) | copy-start | bytes 18436
  87.1 10.5 %copy-start.4 = (bf16[768,512]{1,0:T(8,128)(2,1)S(1)}, bf16[768,512]{1,0:T(8,128)(2,1)}, u32[]{:S(2)}) copy-start(bf16[768,512]{1,0:T(8,128)(2,1)} %get-tuple-element.50.heads) | copy-start | bytes 2359300
  87.1 53.5 %all-to-all-start.1 = ((bf16[8,240,512]{2,1,0:T(8,128)(2,1)}), bf16[8,240,512]{2,1,0:T(8,128)(2,1)}, u32[]{:S(2)}, u32[]{:S(2)}) async-start(bf16[8,240,512]{2,1,0:T(8,128)(2,1)} %bitcast.15), calls=%async_computation.1 | async-start | bytes 3932160 | tf_op jit(solution)/shard_map/all_to_all | solution.py:1251
  93.2 4.4 copy-start.2
  95.6 30.1 %copy-start.3 = (f32[768,2]{1,0:T(8,128)}, f32[768,2]{1,0:T(8,128)S(1)}, u32[]{:S(2)}) copy-start(f32[768,2]{1,0:T(8,128)S(1)} %copy.117.gates) | copy-start | bytes 18436
  96.4 41.0 %copy-start.21 = (f32[512]{0:T(512)}, f32[512]{0:T(512)S(1)}, u32[]{:S(2)}) copy-start(f32[512]{0:T(512)S(1)} %dynamic_slice.29) | copy-start | bytes 6148
  97.6 28.1 %copy-start.27 = (f32[768]{0:T(1024)}, f32[768]{0:T(1024)S(1)}, u32[]{:S(2)}) copy-start(f32[768]{0:T(1024)S(1)} %reduce.9) | copy-start | bytes 9220
  347.0 2.4 copy-start.24
  349.4 2.2 copy-start.26
  351.6 6.7 copy-start.7
  351.6 3.3 copy-start.22
  359.9 3.1 copy-start.6
  363.0 7.7 %copy-start.20 = (s32[768,2]{0,1:T(2,128)S(1)}, s32[768,2]{0,1:T(2,128)}, u32[]{:S(2)}) copy-start(s32[768,2]{0,1:T(2,128)} %param.34) | copy-start | bytes 18436
  381.9 25.0 %copy-start.10 = (bf16[768,512]{1,0:T(8,128)(2,1)}, bf16[768,512]{1,0:T(8,128)(2,1)S(1)}, u32[]{:S(2)}) copy-start(bf16[768,512]{1,0:T(8,128)(2,1)S(1)} %get-tuple-element.59) | copy-start | bytes 2359300
  381.9 27.1 %all-to-all-start.2 = ((bf16[8,96,512]{2,1,0:T(8,128)(2,1)}), bf16[8,96,512]{2,1,0:T(8,128)(2,1)}, u32[]{:S(2)}, u32[]{:S(2)}) async-start(bf16[8,96,512]{2,1,0:T(8,128)(2,1)} %bitcast.23), calls=%async_computation.2 | async-start | bytes 1572864 | tf_op jit(solution)/shard_map/all_to_all | solution.py:1251
  387.3 305.1 %all-reduce.6.cloned.1.call-start = ((), (), s32[]{:S(2)}) async-start(), calls=%async_computation.3 | async-start | bytes 4194304 | tf_op jit(solution)/shard_map/psum | solution.py:1483
  387.3 19.5 %collective-permute-start = (bf16[768,512]{1,0:T(8,128)(2,1)S(1)}, bf16[768,512]{1,0:T(8,128)(2,1)}, u32[]{:S(2)}, u32[]{:S(2)}) collective-permute-start(bf16[768,512]{1,0:T(8,128)(2,1)S(1)} %get-tuple-element.59), channel_id=1, source_target_pairs={{0,2},{1,3},{2,0},{3,1},{4,6},{5,7},{6,4},{7,5},{8,10},{9,11},{10,... | collective-permute-start | bytes 2359304 | tf_op jit(solution)/shard_map/ppermute | solution.py:745
  388.2 19.9 %copy-start.14 = (f32[768,1]{1,0:T(8,128)S(1)}, f32[768,1]{1,0:T(8,128)}, u32[]{:S(2)}) copy-start(f32[768,1]{1,0:T(8,128)} %get-tuple-element.55) | copy-start | bytes 9220
  406.9 2.1 copy-start.32
  406.9 5.0 collective-permute-start.1
  406.9 5.0 collective-permute-start.2
  408.1 70.7 %copy-start.29 = (f32[512]{0:T(512)}, f32[512]{0:T(512)S(1)}, u32[]{:S(2)}) copy-start(f32[512]{0:T(512)S(1)} %dynamic_slice.30) | copy-start | bytes 6148
  408.9 2.9 copy-start.11
  415.8 23.9 %copy-start.18 = (s32[768,2]{0,1:T(2,128)S(1)}, s32[768,2]{0,1:T(2,128)}, u32[]{:S(2)}) copy-start(s32[768,2]{0,1:T(2,128)} %param.33) | copy-start | bytes 18436
  458.6 19.0 %copy-start.9 = (f32[768,128]{1,0:T(8,128)S(1)}, f32[768,128]{1,0:T(8,128)}, u32[]{:S(2)}) copy-start(f32[768,128]{1,0:T(8,128)} %get-tuple-element.51) | copy-start | bytes 1179652
  477.3 1.6 copy-start.28
  679.8 4.4 copy-start.13
  684.2 2.6 copy-start.12
  686.8 2.6 copy-start.15
  686.8 3.9 copy-start.33
  690.7 5.8 copy-start.1
Sparse Core Ops, SparseCore 0:
  458.7 132.8 all-reduce.5

commit v4 on v3

--- a/solution.py
+++ b/solution.py
@@ -736,38 +736,90 @@
     )(source[None], source_grads[None], gates, gate_w, up_w, down_w)
 
 
-def across_spots(rows):
-    parts = lax.axis_size("tensor")
-    pairs = [
-        [(index, (index + 2 * step) % parts) for index in range(parts)]
-        for step in range(parts // 2)
-    ]
-    return [rows] + [lax.ppermute(rows, "tensor", pair) for pair in pairs[1:]]
-
-
-def across_cores(pieces):
-    swap = [(index, index ^ 1) for index in range(lax.axis_size("tensor"))]
-    return [part for piece in pieces for part in (piece, lax.ppermute(piece, "tensor", swap))]
-
-
-def closing_kernel(count, *refs):
-    normed_t, gain, marks, hidden, scaled, routed, small_in = refs[:7]
-    grads, weights, refs = refs[7 : 7 + count], refs[7 + count : 7 + 2 * count], refs[7 + 2 * count :]
-    refs = refs[len(refs) - (count + 2 + 20 + 8) :]
+class Exchange:
+    @staticmethod
+    def scratch(pieces, parts, rows, lanes):
+        wide = (rows + 127) // 128 * 128
+        return [
+            pltpu.VMEM((pieces, lanes, wide), jnp.float32),
+            pltpu.VMEM((pieces, parts - 1, lanes, wide), jnp.float32),
+            pltpu.SemaphoreType.DMA((pieces, parts - 1)),
+            pltpu.SemaphoreType.DMA((pieces, parts - 1)),
+        ]
+
+    def __init__(self, place, refs):
+        self.place = place
+        self.own, self.got, self.sent, self.landed = refs
+
+    def copy(self, piece, step):
+        return remote(
+            self.own.at[piece],
+            self.got.at[piece, step - 1],
+            self.sent.at[piece, step - 1],
+            self.landed.at[piece, step - 1],
+            self.place.device(self.place.expert, self.place.along(step)),
+        )
+
+    def start(self, piece, values):
+        _, lanes, wide = self.own.shape
+        rows = values.shape[0]
+        if rows < wide:
+            blank = jnp.zeros((wide - rows, 128), jnp.float32)
+            values = jnp.concatenate([values, blank], axis=0)
+        self.own[piece] = values.T[:lanes]
+        for step in range(1, self.place.parts):
+            self.copy(piece, step).start()
+
+    def total(self, piece, rows):
+        _, lanes, wide = self.own.shape
+        total = self.own[piece]
+        for step in range(1, self.place.parts):
+            self.copy(piece, step).wait_recv()
+            total = total + self.got[piece, step - 1]
+        blank = jnp.zeros((128 - lanes, wide), jnp.float32)
+        return jnp.concatenate([total, blank], axis=0).T[:rows]
+
+    def finish(self, piece):
+        for step in range(1, self.place.parts):
+            self.copy(piece, step).wait_send()
+
+
+def closing_kernel(jobs, *refs):
     (
-        hold, partial, stat_own, stat_in, ready, gathered, small_own, small_got, small_sum,
-        ring_send, ring_land, stat_send, stat_land, back_send, back_land,
-        small_send, small_land, last_send, last_land, own_sem,
-    ) = refs[count + 2 : count + 22]
-    summed, back, small_out = refs[:count], refs[count], refs[count + 1]
+        normed_t, gain, marks, small_in, query_grad, key_grad, value_grad, gated_t, hidden_grads,
+        hidden_hbm, scaled_hbm, routed_hbm, query_hbm, key_hbm, value_hbm,
+    ), refs = refs[:15], refs[15:]
+    grads = (query_grad, key_grad, value_grad)
+    count = len(grads)
+    lefts, rights, refs = refs[:3], refs[3:6], refs[6:]
+    summed, back, small_out, products, refs = refs[:4], refs[4], refs[5], refs[6:9], refs[9:]
+    (
+        hold, hold_out, partial, ready, gathered, small_own, small_got, small_sum,
+        hidden, scaled, routed, w_query, w_key, w_value, right, left, product,
+        ring_send, ring_land, back_send, back_land,
+        small_send, small_land, last_send, last_land, own_sem, load_sem, job_sem,
+    ) = refs[:28]
+    weights = (w_query, w_key, w_value)
     place = Place()
-    collect = Collect(place, refs[count + 22 :])
+    exchange = Exchange(place, refs[28:32])
+    collect = Collect(place, refs[32:])
     groups, parts = place.groups, place.parts
-    pieces, _, rows = collect.core_in.shape[0], None, collect.core_in.shape[3]
+    pieces, rows = collect.core_in.shape[0], collect.core_in.shape[3]
     width = hidden.shape[1]
     block = hold.shape[3]
     bucket = back.shape[1]
     each = rows // bucket
+    loads = [
+        pltpu.make_async_copy(held, kept, load_sem.at[number])
+        for number, (held, kept) in enumerate(
+            (
+                (query_hbm, w_query), (key_hbm, w_key), (value_hbm, w_value),
+                (hidden_hbm, hidden), (scaled_hbm, scaled), (routed_hbm, routed),
+            )
+        )
+    ]
+    for load in loads:
+        load.start()
     place.meet(True, True)
 
     parity, half = lax.rem(place.expert, 2), lax.div(place.expert, 2)
@@ -793,14 +845,39 @@
             place.device(member(at + sign), place.tensor),
         )
 
+    out_rows, out_columns = hold_out.shape[2:]
+
+    def first_column(sign, step):
+        spot = lax.rem(at - sign * step + 2 * groups, groups)
+        return pl.multiple_of(spot * out_columns, 128)
+
     def slot(step, way, number):
+        if number == count:
+            return hold_out.at[step, way]
         return hold.at[step, way, number]
 
     def spot_out(step, way, sign, number):
+        if number == count:
+            return summed[number].at[
+                pl.ds(way * out_rows, out_rows), pl.ds(first_column(sign, step), out_columns)
+            ]
         return summed[number].at[pl.ds(first_row(way, sign, step), block)]
 
+    def own_part(step, way, sign, number):
+        if number == count:
+            return jnp.dot(
+                gated_t[way * out_rows : (way + 1) * out_rows, :],
+                hidden_grads[:, pl.ds(first_column(sign, step), out_columns)],
+                preferred_element_type=jnp.float32,
+            )
+        return jnp.dot(
+            normed_t[pl.ds(first_row(way, sign, step), block), :],
+            grads[number][...],
+            preferred_element_type=jnp.float32,
+        )
+
     def ring(step):
-        for number in range(count):
+        for number in range(count + 1):
             for way, sign in ways:
 
                 @pl.when((step >= 1) & (step < groups))
@@ -815,22 +892,16 @@
 
                 @pl.when(step < groups)
                 def _():
-                    first = first_row(way, sign, step)
-                    own = jnp.dot(
-                        normed_t[pl.ds(first, block), :],
-                        grads[number][...],
-                        preferred_element_type=jnp.float32,
-                    )
+                    own = own_part(step, way, sign, number)
+                    held = slot(step, way, number)
 
                     @pl.when(step == 0)
                     def _():
-                        hold[0, way, number] = own.astype(jnp.bfloat16)
+                        held[...] = own.astype(jnp.bfloat16)
 
                     @pl.when(step > 0)
                     def _():
-                        hold[step, way, number] = (
-                            own + hold[step, way, number].astype(jnp.float32)
-                        ).astype(jnp.bfloat16)
+                        held[...] = (own + held[...].astype(jnp.float32)).astype(jnp.bfloat16)
 
                 @pl.when(step < groups - 1)
                 def _():
@@ -850,7 +921,7 @@
                     ring_copy(step, way, sign, number, held, held).start()
 
     def ring_finish(step, carry):
-        for number in range(count):
+        for number in range(count + 1):
             for way, sign in ways:
                 held = slot(0, way, number)
                 ring_copy(step, way, sign, number, held, held).wait_send()
@@ -872,22 +943,11 @@
                 collect.stage[side, 0, spot, core] = part.astype(jnp.bfloat16)
         collect.first(piece)
 
-    def stat_copy(piece, step):
-        return remote(
-            stat_own.at[piece],
-            stat_in.at[piece, step - 1],
-            stat_send.at[piece, step - 1],
-            stat_land.at[piece, step - 1],
-            place.device(place.expert, place.along(step)),
-        )
-
     def measure(piece):
         total = collect.third(piece)[0]
         partial[piece] = total
         inner = jnp.sum(total * scaled[band(piece), :] * gain[...], axis=1, keepdims=True)
-        stat_own[piece] = jnp.broadcast_to(inner, (rows, 128))
-        for step in range(1, parts):
-            stat_copy(piece, step).start()
+        exchange.start(piece, jnp.broadcast_to(inner, (rows, 128)))
 
     def back_copy(target, piece, number):
         return remote(
@@ -899,10 +959,7 @@
         )
 
     def conclude(piece):
-        inner = stat_own[piece]
-        for step in range(1, parts):
-            stat_copy(piece, step).wait_recv()
-            inner = inner + stat_in[piece, step - 1]
+        inner = exchange.total(piece, rows)
         mean = (inner[:, :1] + marks[band(piece), 1:2]) / (width * parts)
         grad = partial[piece] + routed[band(piece), :]
         part = scaled[band(piece), :]
@@ -921,7 +978,7 @@
                 own = pltpu.make_async_copy(
                     ready.at[piece, pl.ds(number * bucket, bucket)],
                     back.at[place.expert],
-                    own_sem.at[0, count],
+                    own_sem.at[0, count + 1],
                 )
                 own.start()
                 own.wait()
@@ -944,7 +1001,7 @@
             place.device(place.expert, place.along(step)),
         )
 
-    own_small = pltpu.make_async_copy(small_sum, small_out.at[place.tensor], own_sem.at[1, count])
+    own_small = pltpu.make_async_copy(small_sum, small_out.at[place.tensor], own_sem.at[1, count + 1])
 
     def small_first():
         small_own[...] = small_in[...]
@@ -964,20 +1021,95 @@
 
     gathered[...] = jnp.zeros_like(gathered)
     turns = max(2 * groups - 1, pieces + 5)
+    tiles = sum(job[0] for job in jobs)
+    each_turn = -(-tiles // turns)
+
+    def job_of(number, first, action):
+        start = 0
+        for index, (many, size, wide) in enumerate(jobs):
+            when(
+                (number >= start) & (number < start + many),
+                functools.partial(action, index, size, wide),
+                number - start,
+            )
+            start += many
+
+    def right_copy(index, wide):
+        return pltpu.make_async_copy(rights[index], right.at[:, pl.ds(0, wide)], job_sem.at[4])
+
+    def left_copy(index, size, tile, side):
+        first = pl.multiple_of(tile * size, 128)
+        return pltpu.make_async_copy(
+            lefts[index].at[:, pl.ds(first, size)],
+            left.at[side, :, pl.ds(0, size)],
+            job_sem.at[side],
+        )
+
+    def product_copy(index, size, wide, tile, side):
+        first = pl.multiple_of(tile * size, 8)
+        return pltpu.make_async_copy(
+            product.at[side, pl.ds(0, size), pl.ds(0, wide)],
+            products[index].at[pl.ds(first, size)],
+            job_sem.at[2 + side],
+        )
+
+    def multiply(number):
+        side = lax.rem(number, 2)
+
+        def fetch_next(index, size, wide, tile):
+            left_copy(index, size, tile, 1 - side).start()
+
+        def stored(index, size, wide, tile):
+            product_copy(index, size, wide, tile, side).wait()
+
+        def work(index, size, wide, tile):
+            @pl.when(tile == 0)
+            def _():
+                right_copy(index, wide).start()
+                right_copy(index, wide).wait()
+
+            left_copy(index, size, tile, side).wait()
+            value = dot_tn(left[side, :, :size], right[:, :wide])
+            product[side, :size, :wide] = value
+            product_copy(index, size, wide, tile, side).start()
+
+        job_of(number + 1, None, fetch_next)
+        job_of(number - 2, None, stored)
+        job_of(number, None, work)
+
+    left_copy(0, jobs[0][1], 0, 0).start()
 
     def turn_step(turn, carry):
         when(turn < 2 * groups - 1, ring, turn)
+
+        @pl.when(turn == 0)
+        def _():
+            for load in loads:
+                load.wait()
+
         when((turn >= 3) & (turn < pieces + 3), conclude, turn - 3)
         when((turn >= 2) & (turn < pieces + 2), measure, turn - 2)
         when((turn >= 1) & (turn < pieces + 1), collect.second, turn - 1)
         when(turn < pieces, project, turn)
         when(turn == pieces + 3, small_first)
         when(turn == pieces + 4, small_second)
+        lax.fori_loop(
+            turn * each_turn,
+            jnp.minimum((turn + 1) * each_turn, tiles),
+            lambda number, held: (multiply(number), held)[1],
+            0,
+        )
         return carry
 
     lax.fori_loop(0, turns, turn_step, 0)
+    for number in (tiles - 2, tiles - 1):
+        index, tile = 0, number
+        while tile >= jobs[index][0]:
+            tile -= jobs[index][0]
+            index += 1
+        product_copy(index, jobs[index][1], jobs[index][2], tile, number % 2).wait()
     lax.fori_loop(0, 2 * groups - 2, ring_finish, 0)
-    for number in range(count):
+    for number in range(count + 1):
         for way, sign in ways:
             pltpu.make_async_copy(
                 slot(groups - 1, way, number),
@@ -994,8 +1126,7 @@
         last_copy(step, origin).wait_recv()
 
     def settle(piece, carry):
-        for step in range(1, parts):
-            stat_copy(piece, step).wait_send()
+        exchange.finish(piece)
         for number in range(each):
             target = piece * each + number
 
@@ -1015,7 +1146,10 @@
     lax.fori_loop(0, pieces, settle, 0)
 
 
-def closing(normed_t, gain, marks, hidden, scaled, routed, small, grads, weights, after, pieces, collective):
+def closing(
+    normed_t, gain, marks, small, grads, gated_t, hidden_grads, hidden, scaled, routed, weights,
+    lefts, rights, pieces, collective,
+):
     groups, parts = lax.axis_size("expert"), lax.axis_size("tensor")
     spots = parts // 2
     model_width, tokens = normed_t.shape
@@ -1028,43 +1162,186 @@
     inside = pl.BlockSpec(memory_space=pltpu.VMEM)
     anywhere = pl.BlockSpec(memory_space=pl.ANY)
     dma = pltpu.SemaphoreType.DMA
+    jobs = []
+    for left, right in zip(lefts, rights):
+        jobs.append((left.shape[1] // 128, 128, right.shape[1]))
+    depth = lefts[0].shape[0]
+    tile = max(job[1] for job in jobs)
+    wide = max(job[2] for job in jobs)
     return pl.pallas_call(
-        functools.partial(closing_kernel, count),
+        functools.partial(closing_kernel, tuple(jobs)),
         out_shape=(
             *(jax.ShapeDtypeStruct((model_width, columns), low) for _ in range(count)),
+            jax.ShapeDtypeStruct((columns, model_width), low),
             jax.ShapeDtypeStruct((groups, tokens // groups, width), low),
             jax.ShapeDtypeStruct((parts,) + small.shape, full),
+            *(
+                jax.ShapeDtypeStruct((left.shape[1], right.shape[1]), full)
+                for left, right in zip(lefts, rights)
+            ),
         ),
-        in_specs=[inside] * (7 + 2 * count) + [anywhere] * len(after),
-        out_specs=(anywhere,) * (count + 2),
+        in_specs=[inside] * 9 + [anywhere] * 12,
+        out_specs=(anywhere,) * 9,
         scratch_shapes=[
             pltpu.VMEM((groups, 2, count, block, columns), low),
+            pltpu.VMEM((groups, 2, columns // 2, model_width // groups), low),
             pltpu.VMEM((pieces, rows, width), full),
-            pltpu.VMEM((pieces, rows, 128), full),
-            pltpu.VMEM((pieces, parts - 1, rows, 128), full),
             pltpu.VMEM((pieces, rows, width), low),
             pltpu.VMEM((1, width), full),
             pltpu.VMEM(small.shape, full),
             pltpu.VMEM((groups - 1,) + small.shape, full),
             pltpu.VMEM(small.shape, full),
-            dma((2 * groups - 2, 2, count)),
-            dma((2 * groups - 2, 2, count)),
-            dma((pieces, parts - 1)),
-            dma((pieces, parts - 1)),
+            pltpu.VMEM((tokens, width), full),
+            pltpu.VMEM((tokens, width), full),
+            pltpu.VMEM((tokens, width), full),
+            *(pltpu.VMEM(weight.shape, low) for weight in weights),
+            pltpu.VMEM((depth, wide), low),
+            pltpu.VMEM((2, depth, tile), low),
+            pltpu.VMEM((2, tile, wide), full),
+            dma((2 * groups - 2, 2, count + 1)),
+            dma((2 * groups - 2, 2, count + 1)),
             dma((groups,)),
             dma((groups,)),
             dma((groups - 1,)),
             dma((groups - 1,)),
             dma((parts - 1,)),
             dma((parts - 1,)),
-            dma((2, count + 1)),
+            dma((2, count + 2)),
+            dma((6,)),
+            dma((5,)),
         ]
+        + Exchange.scratch(pieces, parts, rows, 8)
         + Collect.scratch(pieces, 1, spots, rows, width),
         compiler_params=pltpu.CompilerParams(
-            collective_id=collective, has_side_effects=True, vmem_limit_bytes=56 * MIB
+            collective_id=collective, has_side_effects=True, vmem_limit_bytes=60 * MIB
         ),
-        cost_estimate=lasting(140),
-    )(normed_t, gain, marks, hidden, scaled, routed, small, *grads, *weights, *after)
+        cost_estimate=lasting(200),
+    )(
+        normed_t, gain, marks, small, *grads, gated_t, hidden_grads, hidden, scaled, routed, *weights,
+        *lefts, *rights,
+    )
+
+
+def precise_dot(left, right):
+    return jnp.dot(
+        left, right, precision=lax.Precision.HIGHEST, preferred_element_type=jnp.float32
+    )
+
+
+def settle_kernel(
+    came, picks, gates, logits, factor, hidden, grads, gain, router_t,
+    mixed, hidden_grad, gathered, router_grad, gain_grad,
+    row_grads, ready, *refs,
+):
+    place = Place()
+    exchange = Exchange(place, refs[:4])
+    pieces, rows, width = row_grads.shape
+    spread = Spread(place, ready, gathered, refs[4:], False)
+    slots, experts_of = came.shape[1], logits.shape[1]
+    low = jnp.bfloat16
+    place.meet(False, True)
+    router_grad[...] = jnp.zeros_like(router_grad)
+    gain_grad[...] = jnp.zeros_like(gain_grad)
+
+    def band(piece):
+        return pl.ds(pl.multiple_of(piece * rows, rows), rows)
+
+    def scaled_of(piece):
+        return hidden[band(piece), :] * factor[band(piece), :]
+
+    def gather(piece):
+        here = band(piece)
+        numbers = lax.broadcasted_iota(jnp.int32, (rows, slots), 1)
+        chosen = [(picks[here, way : way + 1] == numbers).astype(low) for way in range(2)]
+        result = hidden[here, :]
+        grad = grads[here, :].astype(jnp.float32)
+        lane = lax.broadcasted_iota(jnp.int32, (rows, 128), 1)
+        stats = jnp.zeros((rows, 128), jnp.float32)
+        for way in range(2):
+            value = jnp.dot(chosen[way], came[0], preferred_element_type=jnp.float32)
+            result = result + gates[here, way : way + 1] * value
+            stats = jnp.where(lane == way, jnp.sum(value * grad, axis=1, keepdims=True), stats)
+        mixed[here, :] = result.astype(low)
+        total = jnp.dot(chosen[0] + chosen[1], came[1], preferred_element_type=jnp.float32)
+        row_grads[piece] = total
+        inner = jnp.sum(total * scaled_of(piece) * gain[...], axis=1, keepdims=True)
+        exchange.start(piece, jnp.where(lane == 2, inner, stats))
+
+    def settle(piece):
+        here = band(piece)
+        stats = exchange.total(piece, rows)
+        gate = [gates[here, way : way + 1] for way in range(2)]
+        shared = gate[0] * stats[:, :1] + gate[1] * stats[:, 1:2]
+        names = lax.broadcasted_iota(jnp.int32, (rows, experts_of), 1)
+        logit_grad = jnp.zeros((rows, experts_of), jnp.float32)
+        for way in range(2):
+            term = gate[way] * (stats[:, way : way + 1] - shared)
+            logit_grad = logit_grad + jnp.where(picks[here, 2 + way : 3 + way] == names, term, 0.0)
+        mean = (
+            stats[:, 2:3] + jnp.sum(logit_grad * logits[here, :], axis=1, keepdims=True)
+        ) / (width * place.parts)
+        scaled = scaled_of(piece)
+        grad = row_grads[piece] + precise_dot(logit_grad, router_t[...])
+        gain_grad[...] += jnp.sum(grad * scaled, axis=0, keepdims=True)
+        router_grad[...] += lax.dot_general(
+            logit_grad,
+            scaled * gain[...],
+            (((0,), (0,)), ((), ())),
+            precision=lax.Precision.HIGHEST,
+            preferred_element_type=jnp.float32,
+        )
+        result = grads[here, :].astype(jnp.float32) + factor[here, :] * (
+            grad * gain[...] - scaled * mean
+        )
+        hidden_grad[here, :] = result
+        ready[0, piece] = result.astype(low)
+        spread.first(piece)
+
+    def step(turn, carry):
+        when(turn < pieces, gather, turn)
+        when((turn >= 2) & (turn <= pieces + 1), settle, turn - 2)
+        when(turn >= 3, spread.second, turn - 3)
+        return carry
+
+    lax.fori_loop(0, pieces + 3, step, 0)
+
+    def last(piece, carry):
+        spread.third(piece)
+        spread.finish(piece)
+        exchange.finish(piece)
+        return carry
+
+    lax.fori_loop(0, pieces, last, 0)
+
+
+def settle(came, picks, gates, logits, factor, hidden, grads, gain, router_t, pieces, collective):
+    parts = lax.axis_size("tensor")
+    tokens, width = hidden.shape
+    rows = tokens // pieces
+    low, full = jnp.bfloat16, jnp.float32
+    inside = pl.BlockSpec(memory_space=pltpu.VMEM)
+    return pl.pallas_call(
+        settle_kernel,
+        out_shape=(
+            jax.ShapeDtypeStruct((tokens, width), low),
+            jax.ShapeDtypeStruct((tokens, width), full),
+            jax.ShapeDtypeStruct((1, pieces, rows, width * parts), low),
+            jax.ShapeDtypeStruct(router_t.shape, full),
+            jax.ShapeDtypeStruct((1, width), full),
+        ),
+        in_specs=[inside] * 9,
+        out_specs=(inside, inside, pl.BlockSpec(memory_space=pl.ANY), inside, inside),
+        scratch_shapes=[
+            pltpu.VMEM((pieces, rows, width), full),
+            pltpu.VMEM((1, pieces, rows, width), low),
+        ]
+        + Exchange.scratch(pieces, parts, rows, 8)
+        + Spread.scratch(pieces, parts // 2),
+        compiler_params=pltpu.CompilerParams(
+            collective_id=collective, has_side_effects=True, vmem_limit_bytes=48 * MIB
+        ),
+        cost_estimate=lasting(30),
+    )(came, picks, gates, logits, factor, hidden, grads, gain, router_t)
 
 
 def dot_tn(left, right):
@@ -1162,8 +1439,8 @@
 def attend_back_kernel(
     grads, w_out, gates, heads, query, keys, values, log_total, cosine, sine,
     segment_column, segment_row,
-    query_grad, key_grad, value_grad, gate_grad, weight_grad,
-    heads_grad, gated, key_sum, value_sum,
+    query_grad, key_grad, value_grad, gate_grad, gated_t,
+    heads_grad, key_sum, value_sum,
 ):
     tokens, columns = query.shape
     low = jnp.bfloat16
@@ -1180,8 +1457,7 @@
                 plain[:, column] * head, axis=1, keepdims=True
             )
             heads_grad[rows, column] = (plain[:, column] * gate).astype(low)
-            gated[rows, column] = (head * gate).astype(low)
-    weight_grad[...] = dot_tn(gated[...], grads[...]).astype(low)
+            gated_t[column, rows] = (head * gate).T.astype(low)
 
     def unturn(value, rows):
         turned = pltpu.roll(value * sine[rows, :], HEAD // 2, 1)
@@ -1228,12 +1504,11 @@
             block,
             block,
             jax.ShapeDtypeStruct(gates.shape, full),
-            jax.ShapeDtypeStruct(w_out.shape, low),
+            jax.ShapeDtypeStruct((columns, tokens), low),
         ),
         in_specs=[inside] * 12,
         out_specs=(inside,) * 5,
         scratch_shapes=[
-            pltpu.VMEM((tokens, columns), low),
             pltpu.VMEM((tokens, columns), low),
             pltpu.VMEM((tokens, HEAD), full),
             pltpu.VMEM((tokens, HEAD), full),
@@ -1255,27 +1530,6 @@
         concat_axis=0,
         tiled=True,
     ).reshape(count, width)
-
-
-def side_by_side(pieces):
-    parts = len(pieces)
-    spots = parts // 2
-    index = lax.axis_index("tensor")
-    spot, core = index // 2, index % 2
-    pairs = []
-    for step in range(spots):
-        same, other = pieces[2 * step], pieces[2 * step + 1]
-        pairs.append(
-            (jnp.where(core == 0, same, other), jnp.where(core == 0, other, same))
-        )
-    ordered = []
-    for here in range(spots):
-        for side in range(2):
-            value = pairs[0][side]
-            for step in range(1, spots):
-                value = jnp.where((spot - here) % spots == step, pairs[step][side], value)
-            ordered.append(value)
-    return jnp.concatenate(ordered, axis=1)
 
 
 def gather_tensor(rows):
@@ -1365,7 +1619,6 @@
     gate_table = jnp.sum(attn_gates[:, :, None] * attn_mask, axis=1)
     gate_local = lax.dynamic_slice_in_dim(gate_table, part_index * local_experts, local_experts, 1)
     grad_cols_low, heads_low = lax.optimization_barrier((grad_cols_low, heads_low))
-    grad_cols = grad_cols_low.astype(jnp.float32)
     slot_grads = jnp.dot(to_slot, grad_cols_low, preferred_element_type=jnp.float32).astype(low)
     slot_grads = jnp.repeat(slot_grads.reshape(expert_count, capacity, col_width), sharers, axis=0)
     slot_grads = to_expert(slot_grads.reshape(group_count * capacity, col_width), group_count)
@@ -1396,7 +1649,7 @@
     mlp_logits = stats[1:].T * factor_two
     scaled_two = hidden * factor_two
     normed_two = scaled_two * gain_two
-    mlp_gates, mlp_mask = pair_gates(mlp_logits, mlp_routes)
+    mlp_gates, _ = pair_gates(mlp_logits, mlp_routes)
     slot_rows = jnp.dot(
         to_slot, normed_two.astype(low), preferred_element_type=jnp.float32
     ).astype(low)
@@ -1426,47 +1679,22 @@
                 axis=2,
             )
         ).astype(low)
-    made, row_grads = returned.reshape(2, slots, col_width)
-    from_slot = [(chosen[way][:, None] == slot_ids[None, :]).astype(low) for way in range(2)]
-    pair_values = jnp.stack(
-        [
-            jnp.dot(from_slot[way], made, preferred_element_type=jnp.float32)
-            for way in range(2)
-        ],
-        axis=1,
-    )
-    row_grad_sum = jnp.dot(
-        from_slot[0] + from_slot[1], row_grads, preferred_element_type=jnp.float32
-    )
-    mixed_cols = hidden + jnp.sum(mlp_gates[:, :, None] * pair_values, axis=1)
-    back_mixed = to_expert(mixed_cols.astype(low), group_count)
-    weighed_two = scaled_two * gain_two
-    stats = jnp.stack(
-        [
-            jnp.sum(pair_values[:, 0] * grad_cols, axis=1),
-            jnp.sum(pair_values[:, 1] * grad_cols, axis=1),
-            jnp.sum(row_grad_sum * weighed_two, axis=1),
-        ]
-    )
-    stats = jnp.sum(gather_tensor(stats), axis=0)
-    mlp_logit_grad = pair_back(mlp_gates, mlp_mask, stats[:2].T)
-    norm_two_grad = row_grad_sum + jnp.dot(mlp_logit_grad, router_two.T, precision=PRECISE)
-    mlp_router_grad = jnp.dot(normed_two.T, mlp_logit_grad, precision=PRECISE)
-    mlp_gain_grad = jnp.sum(norm_two_grad * scaled_two, axis=0)
-    mean_two = (stats[2] + jnp.sum(mlp_logit_grad * mlp_logits, axis=1)) / model_width
-    hidden_grad = grad_cols + factor_two * (norm_two_grad * gain_two - scaled_two * mean_two[:, None])
-    rows = inbox.reshape(-1, model_width)
-    grad_rows = slot_grads.reshape(-1, model_width)
-    units = middle.shape[2]
-
-    def rows_product(left, right):
-        return jnp.einsum("sa,sb->ab", left, right, preferred_element_type=jnp.float32)
-
-    hidden_pieces = across_spots(hidden_grad.astype(low))
-    gate_w_grad = rows_product(rows, gate_grad.reshape(-1, units))
-    *hidden_pieces, gate_w_grad = lax.optimization_barrier((*hidden_pieces, gate_w_grad))
-    hidden_grad_low = side_by_side(across_cores(hidden_pieces))
-    query_pre_grad, key_pre_grad, value_pre_grad, local_gate_grad, out_w_grad = attend_back(
+    mixed_cols, hidden_grad, hidden_grad_low, mlp_router_grad, mlp_gain_grad = settle(
+        returned.reshape(2, slots, col_width),
+        jnp.concatenate([destination, mlp_routes], axis=1),
+        mlp_gates,
+        mlp_logits,
+        factor_two,
+        hidden,
+        grad_cols_low,
+        gain_two[None],
+        router_two.T,
+        pieces,
+        4,
+    )
+    back_mixed = to_expert(mixed_cols, group_count)
+    hidden_grad_low = hidden_grad_low.reshape(tok_rows, model_width)
+    query_pre_grad, key_pre_grad, value_pre_grad, local_gate_grad, gated_t = attend_back(
         hidden_grad_low,
         w_out,
         gate_local,
@@ -1479,8 +1707,6 @@
         sine * sign,
         segment,
     )
-    out_w_grad, middle, up_grad = lax.optimization_barrier((out_w_grad, middle, up_grad))
-    out_w_grad = lax.psum(out_w_grad, "expert").astype(jnp.float32)
     gate_grads = gather_tensor(local_gate_grad.T)
     gate_grads = gate_grads.reshape(part_count * local_experts, tok_rows).T
     attn_pair_grad = jnp.sum(attn_mask * gate_grads[:, None, :], axis=2)
@@ -1492,8 +1718,8 @@
         [
             jnp.zeros((1, col_width), jnp.float32),
             attn_router_grad.T,
-            mlp_gain_grad[None],
-            mlp_router_grad.T,
+            mlp_gain_grad,
+            mlp_router_grad,
         ],
         axis=0,
     )
@@ -1501,19 +1727,26 @@
     marks = jnp.stack(
         [factor_one[:, 0], jnp.sum(attn_logit_grad * attn_logits, axis=1)], axis=1
     )
-    up_w_grad = rows_product(rows, up_grad.reshape(-1, units))
-    down_grad = rows_product(middle.reshape(-1, units), grad_rows)
-    *weight_grads, back_grad, small = closing(
+    rows = inbox.reshape(-1, model_width)
+    units = middle.shape[2]
+    middle, gate_grad, up_grad = (
+        jnp.pad(values.reshape(-1, units), ((0, 0), (0, -units % 128)))
+        for values in (middle, gate_grad, up_grad)
+    )
+    *weight_grads, back_grad, small, gate_w_grad, up_w_grad, down_grad = closing(
         normed_t,
         gain_one[None],
         jnp.pad(marks, ((0, 0), (0, 126))),
+        small,
+        (query_pre_grad, key_pre_grad, value_pre_grad),
+        gated_t,
+        hidden_grad_low,
         hidden_grad,
         scaled_cols,
         jnp.dot(attn_logit_grad, router_one.T, precision=PRECISE),
-        small,
-        (query_pre_grad, key_pre_grad, value_pre_grad),
         (w_query, w_key, w_value),
-        (gate_w_grad, up_w_grad, down_grad),
+        (rows, rows, middle),
+        (gate_grad, up_grad, slot_grads.reshape(-1, model_width)),
         pieces,
         3,
     )
@@ -1532,12 +1765,12 @@
         weight_grads[0],
         weight_grads[1],
         weight_grads[2],
-        out_w_grad,
+        weight_grads[3],
         small[1 + experts_of],
         small[2 + experts_of : 2 + experts_of + expert_count].T,
-        gate_w_grad[None],
-        up_w_grad[None],
-        down_grad[None],
+        gate_w_grad[None, :, :units],
+        up_w_grad[None, :, :units],
+        down_grad[None, :units],
     )
 
 

time: 709 us -> 666 us (0.939)
  matrix products: 91.4 us -> 20.4 us
  Pallas kernels: 500 us -> 537 us
  local copies, waits for them, and re-layouts: 23.3 us -> 44.6 us
  between operations: 15 us -> 1.42 us
  other arithmetic: 36.9 us -> 27 us
    dot_general x8 -> x0, matrix products: 70.2 us -> none  [the longest x3 56.2 us: rows_product(): jnp.einsum('sa,sb->ab', left, right, preferred_element_type=jnp.float32)]
    pallas_call x1 -> x2, Pallas kernels: 196 us -> 235 us  [the longest x1 203 us: closing(): pl.pallas_call(functools.partial(closing_kernel, tuple(jobs)), out_shape=...]
    unnamed x74 -> x57, local copies, waits for them, and re-layouts: 2.72 us -> 33.5 us
    all_gather x3 -> x2, blocking collectives: 16 us -> 10.8 us  [gather_tensor(): return lax.all_gather(rows, 'tensor', axis=0)]
  transfers between devices with their start and end apart: 7 -> 3, of which waited for: 0 -> 0; matrix products, arithmetic and copies ran while one was open for 12% -> 7% of each run, Pallas kernels for 35% -> 38%
where the time goes in v4:
time: 666 us; the launch traced here: 660 us
  Pallas kernels  537 us (81%)
  local copies, waits for them, and re-layouts  44.6 us (7%)
  other arithmetic  27 us (4%)
  matrix products  20.4 us (3%)
  starting transfers between devices  19.6 us (3%)
  blocking collectives  10.8 us (2%)
    pallas_call x1, Pallas kernels, experts(): pl.pallas_call(functools.partial(experts_kernel, sharers), out_shape=(jax...  205 us
    pallas_call x1, Pallas kernels, closing(): pl.pallas_call(functools.partial(closing_kernel, tuple(jobs)), out_shape=...  203 us
    unnamed x57, local copies, waits for them, and re-layouts  33.5 us
    pallas_call x1, Pallas kernels, settle(): pl.pallas_call(settle_kernel, out_shape=(jax.ShapeDtypeStruct((tokens, wi...  32.2 us
    pallas_call x1, Pallas kernels, spread_rows(): pl.pallas_call(functools.partial(spread_kernel, over_expert), out_shape=j...  31.2 us
    pallas_call x1, Pallas kernels, collect_rows(): pl.pallas_call(functools.partial(collect_kernel, make, len(operands)), ou...  28.1 us
    pallas_call x1, Pallas kernels, attend(): pl.pallas_call(attend_kernel, out_shape=(jax.ShapeDtypeStruct((tokens, mo...  21.5 us
    all_to_all x3, starting transfers between devices, to_expert(): lax.all_to_all(rows.reshape(group_count, count // group_count, width), 'e...  19.6 us
  transfers between devices with their start and end apart: 3, of which 0 were waited for; matrix products, arithmetic and copies ran while one was open for 7% of the time, Pallas kernels for 38%

profile of v4, /device:TPU:20, one launch (start us, length us, event | category | flops | bytes accessed | tf_op | source)
XLA Modules:
  0.0 660.4 jit_solution(8111471918462654693)
XLA Ops:
  0.7 0.9 fusion.43
  1.5 1.0 copy-done
  2.6 1.7 fusion.24
  4.2 2.8 fusion.23
  7.0 31.2 %shard_map.273 = bf16[1,8,96,2048]{3,2,1,0:T(8,128)(2,1)} custom-call(bf16[1,8,96,512]{3,2,1,0:T(8,128)(2,1)} %bitcast.93), custom_call_target="tpu_custom_call" | custom-call | bytes 90000000 | tf_op jit(solution)/shard_map/pallas_call | solution.py:413
  38.3 7.9 %all-to-all-start = ((bf16[8,96,512]{2,1,0:T(8,128)(2,1)}), bf16[8,96,512]{2,1,0:T(8,128)(2,1)S(1)}, u32[]{:S(2)}, u32[]{:S(2)}) async-start(bf16[8,96,512]{2,1,0:T(8,128)(2,1)} %bitcast.2), calls=%async_computation | async-start | bytes 1572864 | tf_op jit(solution)/shard_map/all_to_all | solution.py:1526
  47.2 2.0 convert_reduce_fusion
  49.8 0.9 broadcast_in_dim.141.segment_column
  51.5 0.9 pad.16.router
  52.4 2.6 sine_multiply_fusion
  55.1 21.5 %shard_map.274 = (bf16[768,2048]{1,0:T(8,128)(2,1)}, bf16[2048,768]{1,0:T(8,128)(2,1)}, f32[768,1]{1,0:T(8,128)}, f32[768,128]{1,0:T(8,128)}, bf16[768,512]{1,0:...) custom-call(bf16[768,2048]{1,0:T(8,128)(2,1)} %bitcast.75, ...), custom_call_target="tpu_custom_call" | custom-call | bytes 60000000 | tf_op jit(solution)/shard_map/pallas_call | solution.py:1419
  76.6 1.3 slice_add_fusion
  78.6 3.1 fusion.8
  81.7 6.3 all-to-all-start.1
  88.0 0.8 dynamic_slice.30
  88.8 0.8 dynamic_slice.29
  90.1 0.7 dynamic-slice_bitcast_fusion.router_t
  90.8 2.1 pad_add_fusion.picks
  92.9 28.1 %shard_map.275 = f32[4,192,512]{2,1,0:T(8,128)S(1)} custom-call(bf16[4,192,512]{2,1,0:T(8,128)(2,1)S(1)} %bitcast.68, f32[4,192,2]{2,1,0:T(8,128)S(1)} %bitcast.67, bf16[512,2048]{1,0:T(8,128)(2,1)S(1)} %copy-done.2), custom_call_target="tpu_custom_call" | custom-call | bytes 78000000 | tf_op jit(solution)/shard_map/pallas_call | solution.py:458
  121.0 2.8 multiply_reduce_fusion
  123.9 1.4 fusion.21
  125.3 5.6 all-gather.2
  132.2 1.4 select_reduce_fusion
  133.9 3.2 fusion.5
  137.1 0.6 broadcast_in_dim.134.refs_2_
  137.8 205.4 %shard_map.276 = (bf16[1,8,240,2048]{3,2,1,0:T(8,128)(2,1)}, bf16[1,8,240,2048]{3,2,1,0:T(8,128)(2,1)}, bf16[8,240,2048]{2,1,0:T(8,128)(2,1)}, bf16[8,240,1408]{...) custom-call(bf16[1,8,240,512]{3,2,1,0:T(8,128)(2,1)} %bitcast.92, ...), custom_call_target="tpu_custom_call" | custom-call | bytes 540000000 | tf_op jit(solution)/shard_map/pallas_call | solution.py:698
  343.2 32.2 %shard_map.277 = (bf16[768,512]{1,0:T(8,128)(2,1)}, f32[768,512]{1,0:T(8,128)S(1)}, bf16[1,4,192,2048]{3,2,1,0:T(8,128)(2,1)}, f32[8,512]{1,0:T(8,128)S(1)}, f32[1,512]{1,0:T(1,128)S(1)}) custom-call(bf16[2,1920,512]{2,1,0:T(8,128)(2,1)} %bitcast.90, s32[768,4]{1,0:T(8,128)S(1)} %copy-done.7, f32[768,2]{1,0:T(8,128)S(1)} %exponential_divide_fusion.gates, ...), custom_call_target="tpu_custom_call" | custom-call | bytes 90000000 | tf_op jit(solution)/shard_map/pallas_call | solution.py:1323
  375.4 1.1 copy-done.8
  376.6 15.5 %shard_map.278 = (bf16[768,512]{1,0:T(8,128)(2,1)}, bf16[768,512]{1,0:T(8,128)(2,1)}, bf16[768,512]{1,0:T(8,128)(2,1)}, f32[768,2]{1,0:T(8,128)}, bf16[512,768]{1,0:T(8,128)(2,1)}) custom-call(bf16[768,2048]{1,0:T(8,128)(2,1)} %bitcast.78, bf16[512,2048]{1,0:T(8,128)(2,1)} %w_out.1, f32[768,2]{1,0:T(8,128)} %copy-done.3, ...), custom_call_target="tpu_custom_call" | custom-call | bytes 75000000 | tf_op jit(solution)/shard_map/pallas_call | solution.py:1500
  392.1 1.2 copy.116
  393.3 5.5 all-to-all-start.2
  398.8 5.2 all-gather.3
  404.3 1.8 fusion.19
  406.1 0.6 pad.19.refs_3_
  407.3 0.8 pad.18.refs_2_
  408.1 2.0 fusion.39.refs_11_
  410.0 202.5 %shard_map.279 = (bf16[2048,512]{1,0:T(8,128)(2,1)}, bf16[2048,512]{1,0:T(8,128)(2,1)}, bf16[2048,512]{1,0:T(8,128)(2,1)}, bf16[512,2048]{1,0:T(8,128)(2,1)}, bf...) custom-call(bf16[2048,768]{1,0:T(8,128)(2,1)} %get-tuple-element.58., ...), custom_call_target="tpu_custom_call" | custom-call | bytes 600000000 | tf_op jit(solution)/shard_map/pallas_call | solution.py:1171
  612.6 4.3 convert_element_type.73
  616.9 2.6 convert_element_type.74
  619.6 2.6 convert_element_type.75
  622.2 2.5 convert_element_type.76
  624.7 0.6 fusion.58
  625.3 0.7 fusion.57
  626.0 1.7 fusion.26
  627.7 2.8 fusion.25
  630.5 9.4 %copy.125 = f32[1,2048,1408]{2,1,0:T(8,128)} copy(f32[1,2048,1408]{2,1,0:T(8,128)} %bitcast.82) | data formatting | bytes 23068672
  640.0 9.4 %copy.126 = f32[1,2048,1408]{2,1,0:T(8,128)} copy(f32[1,2048,1408]{2,1,0:T(8,128)} %bitcast.81) | data formatting | bytes 23068672
  649.4 10.8 %copy.127 = f32[1,1408,2048]{2,1,0:T(8,128)} copy(f32[1,1408,2048]{2,1,0:T(8,128)} %bitcast.80) | data formatting | bytes 23068672
  (111 shorter events, 6.0 us)
Async XLA Ops:
  0.6 1.9 copy-start
  7.0 39.1 %copy-start.20 = (s32[768,2]{0,1:T(2,128)S(1)}, s32[768,2]{0,1:T(2,128)}, u32[]{:S(2)}) copy-start(s32[768,2]{0,1:T(2,128)} %param.34) | copy-start | bytes 18436
  7.0 39.4 %copy-start.24 = (s32[1,3]{1,0:T(1,128)S(1)}, s32[1,3]{1,0:T(1,128)}, u32[]{:S(2)}) copy-start(s32[1,3]{1,0:T(1,128)} %param.32) | copy-start | bytes 40
  7.0 39.7 %copy-start.22 = (s32[1,1536]{1,0:T(1,128)S(1)}, s32[1,1536]{1,0:T(1,128)}, u32[]{:S(2)}) copy-start(s32[1,1536]{1,0:T(1,128)} %param.35) | copy-start | bytes 18436
  7.0 39.8 %copy-start.18 = (f32[2048,8]{0,1:T(8,128)S(1)}, f32[2048,8]{0,1:T(8,128)}, u32[]{:S(2)}) copy-start(f32[2048,8]{0,1:T(8,128)} %param.21) | copy-start | bytes 196612
  38.3 40.3 %all-to-all-start = ((bf16[8,96,512]{2,1,0:T(8,128)(2,1)}), bf16[8,96,512]{2,1,0:T(8,128)(2,1)S(1)}, u32[]{:S(2)}, u32[]{:S(2)}) async-start(bf16[8,96,512]{2,1,0:T(8,128)(2,1)} %bitcast.2), calls=%async_computation | async-start | bytes 1572864 | tf_op jit(solution)/shard_map/all_to_all | solution.py:1526
  46.4 8.7 %copy-start.12 = (s32[768,2]{1,0:T(8,128)}, s32[768,2]{1,0:T(8,128)S(1)}, u32[]{:S(2)}) copy-start(s32[768,2]{1,0:T(8,128)S(1)} %copy.103) | copy-start | bytes 18436
  55.0 23.0 %copy-start.19 = (s32[768,2]{0,1:T(2,128)S(1)}, s32[768,2]{0,1:T(2,128)}, u32[]{:S(2)}) copy-start(s32[768,2]{0,1:T(2,128)} %param.33) | copy-start | bytes 18436
  78.2 3.5 copy-start.11
  78.6 3.1 copy-start.5
  81.7 7.8 %copy-start.16 = (f32[768,1]{1,0:T(8,128)S(1)}, f32[768,1]{1,0:T(8,128)}, u32[]{:S(2)}) copy-start(f32[768,1]{1,0:T(8,128)} %get-tuple-element.59) | copy-start | bytes 9220
  81.7 11.2 %copy-start.2 = (bf16[512,2048]{1,0:T(8,128)(2,1)S(1)}, bf16[512,2048]{1,0:T(8,128)(2,1)}, u32[]{:S(2)}) copy-start(bf16[512,2048]{1,0:T(8,128)(2,1)} %w_out.1) | copy-start | bytes 6291460
  81.7 11.2 %copy-start.4 = (bf16[768,512]{1,0:T(8,128)(2,1)S(1)}, bf16[768,512]{1,0:T(8,128)(2,1)}, u32[]{:S(2)}) copy-start(bf16[768,512]{1,0:T(8,128)(2,1)} %get-tuple-element.53.heads) | copy-start | bytes 2359300
  81.7 55.4 %all-to-all-start.1 = ((bf16[8,240,512]{2,1,0:T(8,128)(2,1)}), bf16[8,240,512]{2,1,0:T(8,128)(2,1)}, u32[]{:S(2)}, u32[]{:S(2)}) async-start(bf16[8,240,512]{2,1,0:T(8,128)(2,1)} %bitcast.91), calls=%async_computation.1 | async-start | bytes 3932160 | tf_op jit(solution)/shard_map/all_to_all | solution.py:1526
  88.8 315.5 %copy-start.21 = (f32[512]{0:T(512)}, f32[512]{0:T(512)S(1)}, u32[]{:S(2)}) copy-start(f32[512]{0:T(512)S(1)} %dynamic_slice.30) | copy-start | bytes 6148
  90.1 31.0 %copy-start.3 = (f32[768,2]{1,0:T(8,128)}, f32[768,2]{1,0:T(8,128)S(1)}, u32[]{:S(2)}) copy-start(f32[768,2]{1,0:T(8,128)S(1)} %copy.121.gates) | copy-start | bytes 18436
  123.8 10.1 %copy-start.9 = (f32[768,512]{1,0:T(8,128)}, f32[768,512]{1,0:T(8,128)S(1)}, u32[]{:S(2)}) copy-start(f32[768,512]{1,0:T(8,128)S(1)} %get-tuple-element.92.hidden) | copy-start | bytes 4718596
  137.8 205.4 %copy-start.6 = (bf16[8,96,512]{2,1,0:T(8,128)(2,1)S(1)}, bf16[8,96,512]{2,1,0:T(8,128)(2,1)}, u32[]{:S(2)}) copy-start(bf16[8,96,512]{2,1,0:T(8,128)(2,1)} %copy-done.5) | copy-start | bytes 2359300
  137.8 205.4 %copy-start.7 = (s32[768,4]{1,0:T(8,128)S(1)}, s32[768,4]{1,0:T(8,128)}, u32[]{:S(2)}) copy-start(s32[768,4]{1,0:T(8,128)} %pad_add_fusion.picks) | copy-start | bytes 36868
  375.4 1.1 copy-start.8
  392.1 14.6 %copy-start.10 = (f32[768,128]{1,0:T(8,128)S(1)}, f32[768,128]{1,0:T(8,128)}, u32[]{:S(2)}) copy-start(f32[768,128]{1,0:T(8,128)} %get-tuple-element.54) | copy-start | bytes 1179652
  393.3 234.4 %all-to-all-start.2 = ((bf16[8,96,512]{2,1,0:T(8,128)(2,1)}), bf16[8,96,512]{2,1,0:T(8,128)(2,1)}, u32[]{:S(2)}, u32[]{:S(2)}) async-start(bf16[8,96,512]{2,1,0:T(8,128)(2,1)} %bitcast.25), calls=%async_computation.2 | async-start | bytes 1572864 | tf_op jit(solution)/shard_map/all_to_all | solution.py:1526
  612.6 4.4 copy-start.15
  616.9 2.6 copy-start.14
  619.5 2.6 copy-start.13
  622.2 2.5 copy-start.17
  622.2 3.8 copy-start.23
  649.4 10.8 %copy-start.1 = (bf16[768,2048]{1,0:T(8,128)(2,1)S(1)}, bf16[768,2048]{1,0:T(8,128)(2,1)}, u32[]{:S(2)}) copy-start(bf16[768,2048]{1,0:T(8,128)(2,1)} %param.18) | copy-start | bytes 9437188

commit v5 on v4

--- a/solution.py
+++ b/solution.py
@@ -38,11 +38,6 @@
     ).astype(jnp.float32)
     picked = jnp.sum(chosen_mask * logits[:, None, :], axis=2)
     return (jax.nn.softmax(picked, axis=1), chosen_mask)
-
-
-def pair_back(gates, chosen_mask, gate_grads):
-    inner = gates * (gate_grads - jnp.sum(gates * gate_grads, axis=1, keepdims=True))
-    return jnp.sum(chosen_mask * inner[:, :, None], axis=1)
 
 
 def slot_table(routes, priority, capacity):
@@ -736,6 +731,82 @@
     )(source[None], source_grads[None], gates, gate_w, up_w, down_w)
 
 
+class Return:
+    @staticmethod
+    def scratch(pieces, rows, width, groups):
+        return [
+            pltpu.VMEM((pieces, rows, width), jnp.bfloat16),
+            pltpu.SemaphoreType.DMA((groups,)),
+            pltpu.SemaphoreType.DMA((groups,)),
+            pltpu.SemaphoreType.DMA,
+        ]
+
+    def __init__(self, place, back, refs):
+        self.place, self.back = place, back
+        self.ready, self.sent, self.landed, self.kept = refs
+        self.bucket = back.shape[1]
+        self.each = self.ready.shape[1] // self.bucket
+
+    def block(self, piece, number):
+        return self.ready.at[piece, pl.ds(number * self.bucket, self.bucket)]
+
+    def copy(self, piece, number, index):
+        target = piece * self.each + number
+        return remote(
+            self.block(piece, number),
+            self.back.at[index],
+            self.sent.at[target],
+            self.landed.at[index],
+            self.place.device(target, self.place.tensor),
+        )
+
+    def start(self, piece, values):
+        place = self.place
+        self.ready[piece] = values
+        for number in range(self.each):
+            target = piece * self.each + number
+
+            @pl.when(target != place.expert)
+            def _():
+                self.copy(piece, number, place.expert).start()
+
+            @pl.when(target == place.expert)
+            def _():
+                own = pltpu.make_async_copy(
+                    self.block(piece, number), self.back.at[place.expert], self.kept
+                )
+                own.start()
+                own.wait()
+
+    def finish(self, piece):
+        for number in range(self.each):
+            target = piece * self.each + number
+
+            @pl.when(target != self.place.expert)
+            def _():
+                self.copy(piece, number, self.place.expert).wait_send()
+                self.copy(piece, number, target).wait_recv()
+
+
+def pair_grad(gates, gate_grads, names, count):
+    shared = gates[0] * gate_grads[0] + gates[1] * gate_grads[1]
+    lane = lax.broadcasted_iota(jnp.int32, (gates[0].shape[0], count), 1)
+    return sum(
+        jnp.where(name == lane, gate * (grad - shared), 0.0)
+        for gate, grad, name in zip(gates, gate_grads, names)
+    )
+
+
+def precise_dot(left, right, contract=(1, 0)):
+    return lax.dot_general(
+        left,
+        right,
+        (((contract[0],), (contract[1],)), ((), ())),
+        precision=lax.Precision.HIGHEST,
+        preferred_element_type=jnp.float32,
+    )
+
+
 class Exchange:
     @staticmethod
     def scratch(pieces, parts, rows, lanes):
@@ -786,35 +857,36 @@
 
 def closing_kernel(jobs, *refs):
     (
-        normed_t, gain, marks, small_in, query_grad, key_grad, value_grad, gated_t, hidden_grads,
-        hidden_hbm, scaled_hbm, routed_hbm, query_hbm, key_hbm, value_hbm,
-    ), refs = refs[:15], refs[15:]
+        normed_t, gain, factor, gates, routes, logits, gate_grads, router_t, gain_two, router_two,
+        query_grad, key_grad, value_grad, gated_t, hidden_grads,
+        hidden_hbm, resid_hbm, query_hbm, key_hbm, value_hbm,
+    ), refs = refs[:20], refs[20:]
     grads = (query_grad, key_grad, value_grad)
     count = len(grads)
     lefts, rights, refs = refs[:3], refs[3:6], refs[6:]
     summed, back, small_out, products, refs = refs[:4], refs[4], refs[5], refs[6:9], refs[9:]
     (
-        hold, hold_out, partial, ready, gathered, small_own, small_got, small_sum,
-        hidden, scaled, routed, w_query, w_key, w_value, right, left, product,
-        ring_send, ring_land, back_send, back_land,
-        small_send, small_land, last_send, last_land, own_sem, load_sem, job_sem,
-    ) = refs[:28]
+        hold, hold_out, partial, small_own, small_got, small_sum,
+        hidden, resid, w_query, w_key, w_value, right, left, product,
+        ring_send, ring_land, small_send, small_land, last_send, last_land,
+        own_sem, load_sem, job_sem,
+    ) = refs[:23]
     weights = (w_query, w_key, w_value)
     place = Place()
-    exchange = Exchange(place, refs[28:32])
-    collect = Collect(place, refs[32:])
+    exchange, of_gates = Exchange(place, refs[23:27]), Exchange(place, refs[27:31])
+    giving = Return(place, back, refs[31:35])
+    collect = Collect(place, refs[35:])
     groups, parts = place.groups, place.parts
     pieces, rows = collect.core_in.shape[0], collect.core_in.shape[3]
     width = hidden.shape[1]
     block = hold.shape[3]
-    bucket = back.shape[1]
-    each = rows // bucket
+    experts_of = logits.shape[1]
     loads = [
         pltpu.make_async_copy(held, kept, load_sem.at[number])
         for number, (held, kept) in enumerate(
             (
                 (query_hbm, w_query), (key_hbm, w_key), (value_hbm, w_value),
-                (hidden_hbm, hidden), (scaled_hbm, scaled), (routed_hbm, routed),
+                (hidden_hbm, hidden), (resid_hbm, resid),
             )
         )
     ]
@@ -943,45 +1015,48 @@
                 collect.stage[side, 0, spot, core] = part.astype(jnp.bfloat16)
         collect.first(piece)
 
+    def scaled_of(piece):
+        return resid[band(piece), :].astype(jnp.float32) * factor[band(piece), :]
+
+    def tell(piece):
+        lane = lax.broadcasted_iota(jnp.int32, (rows, 128), 1)
+        values = jnp.zeros((rows, 128), jnp.float32)
+        held = gate_grads.shape[1]
+        for number in range(held):
+            column = gate_grads[band(piece), number : number + 1]
+            values = jnp.where(lane == place.tensor * held + number, column, values)
+        of_gates.start(piece, values)
+
     def measure(piece):
         total = collect.third(piece)[0]
         partial[piece] = total
-        inner = jnp.sum(total * scaled[band(piece), :] * gain[...], axis=1, keepdims=True)
+        inner = jnp.sum(total * scaled_of(piece) * gain[...], axis=1, keepdims=True)
         exchange.start(piece, jnp.broadcast_to(inner, (rows, 128)))
 
-    def back_copy(target, piece, number):
-        return remote(
-            ready.at[piece, pl.ds(number * bucket, bucket)],
-            back.at[place.expert],
-            back_send.at[target],
-            back_land.at[place.expert],
-            place.device(target, place.tensor),
-        )
-
     def conclude(piece):
-        inner = exchange.total(piece, rows)
-        mean = (inner[:, :1] + marks[band(piece), 1:2]) / (width * parts)
-        grad = partial[piece] + routed[band(piece), :]
-        part = scaled[band(piece), :]
-        gathered[...] += jnp.sum(grad * part, axis=0, keepdims=True)
-        result = hidden[band(piece), :] + marks[band(piece), 0:1] * (grad * gain[...] - part * mean)
-        ready[piece] = result.astype(jnp.bfloat16)
-        for number in range(each):
-            target = piece * each + number
-
-            @pl.when(target != place.expert)
-            def _():
-                back_copy(target, piece, number).start()
-
-            @pl.when(target == place.expert)
-            def _():
-                own = pltpu.make_async_copy(
-                    ready.at[piece, pl.ds(number * bucket, bucket)],
-                    back.at[place.expert],
-                    own_sem.at[0, count + 1],
-                )
-                own.start()
-                own.wait()
+        here = band(piece)
+        every = of_gates.total(piece, rows)[:, :experts_of]
+        lane = lax.broadcasted_iota(jnp.int32, (rows, experts_of), 1)
+        names = [routes[here, way : way + 1] for way in range(2)]
+        logit_grad = pair_grad(
+            [gates[here, way : way + 1] for way in range(2)],
+            [
+                jnp.sum(jnp.where(name == lane, every, 0.0), axis=1, keepdims=True)
+                for name in names
+            ],
+            names,
+            experts_of,
+        )
+        inner = exchange.total(piece, rows)[:, :1] + jnp.sum(
+            logit_grad * logits[here, :], axis=1, keepdims=True
+        )
+        mean = inner / (width * parts)
+        scaled = scaled_of(piece)
+        grad = partial[piece] + precise_dot(logit_grad, router_t[...])
+        small_own[0:1, :] += jnp.sum(grad * scaled, axis=0, keepdims=True)
+        small_own[1 : 1 + experts_of, :] += precise_dot(logit_grad, scaled * gain[...], (0, 0))
+        result = hidden[here, :] + factor[here, :] * (grad * gain[...] - scaled * mean)
+        giving.start(piece, result.astype(jnp.bfloat16))
 
     def small_copy(step):
         return remote(
@@ -1001,11 +1076,12 @@
             place.device(place.expert, place.along(step)),
         )
 
-    own_small = pltpu.make_async_copy(small_sum, small_out.at[place.tensor], own_sem.at[1, count + 1])
+    own_small = pltpu.make_async_copy(small_sum, small_out.at[place.tensor], own_sem.at[0, count + 1])
 
     def small_first():
-        small_own[...] = small_in[...]
-        small_own[0:1, :] = gathered[...]
+        first = 1 + experts_of
+        small_own[first : first + 1, :] = gain_two[...]
+        small_own[first + 1 : first + 1 + router_two.shape[0], :] = router_two[...]
         for step in range(1, groups):
             small_copy(step).start()
 
@@ -1019,7 +1095,7 @@
         for step in range(1, parts):
             last_copy(step, place.tensor).start()
 
-    gathered[...] = jnp.zeros_like(gathered)
+    small_own[...] = jnp.zeros_like(small_own)
     turns = max(2 * groups - 1, pieces + 5)
     tiles = sum(job[0] for job in jobs)
     each_turn = -(-tiles // turns)
@@ -1069,8 +1145,9 @@
                 right_copy(index, wide).wait()
 
             left_copy(index, size, tile, side).wait()
-            value = dot_tn(left[side, :, :size], right[:, :wide])
-            product[side, :size, :wide] = value
+            product[side, :size, :wide] = dot_tn(left[side, :, :size], right[:, :wide]).astype(
+                jnp.bfloat16
+            )
             product_copy(index, size, wide, tile, side).start()
 
         job_of(number + 1, None, fetch_next)
@@ -1091,6 +1168,7 @@
         when((turn >= 2) & (turn < pieces + 2), measure, turn - 2)
         when((turn >= 1) & (turn < pieces + 1), collect.second, turn - 1)
         when(turn < pieces, project, turn)
+        when(turn < pieces, tell, turn)
         when(turn == pieces + 3, small_first)
         when(turn == pieces + 4, small_second)
         lax.fori_loop(
@@ -1127,27 +1205,15 @@
 
     def settle(piece, carry):
         exchange.finish(piece)
-        for number in range(each):
-            target = piece * each + number
-
-            @pl.when(target != place.expert)
-            def _():
-                back_copy(target, piece, number).wait_send()
-                remote(
-                    ready.at[piece, pl.ds(number * bucket, bucket)],
-                    back.at[target],
-                    back_send.at[target],
-                    back_land.at[target],
-                    place.device(target, place.tensor),
-                ).wait_recv()
-
+        of_gates.finish(piece)
+        giving.finish(piece)
         return carry
 
     lax.fori_loop(0, pieces, settle, 0)
 
 
 def closing(
-    normed_t, gain, marks, small, grads, gated_t, hidden_grads, hidden, scaled, routed, weights,
+    normed_t, columns_in, grads, gated_t, hidden_grads, hidden, resid, weights,
     lefts, rights, pieces, collective,
 ):
     groups, parts = lax.axis_size("expert"), lax.axis_size("tensor")
@@ -1156,6 +1222,9 @@
     columns = grads[0].shape[1]
     width = hidden.shape[1]
     count = len(grads)
+    small = jax.ShapeDtypeStruct(
+        ((2 + columns_in[4].shape[1] + columns_in[-1].shape[0] + 7) // 8 * 8, width), jnp.float32
+    )
     rows = tokens // pieces
     block = model_width // (2 * groups)
     low, full = jnp.bfloat16, jnp.float32
@@ -1176,70 +1245,62 @@
             jax.ShapeDtypeStruct((groups, tokens // groups, width), low),
             jax.ShapeDtypeStruct((parts,) + small.shape, full),
             *(
-                jax.ShapeDtypeStruct((left.shape[1], right.shape[1]), full)
+                jax.ShapeDtypeStruct((left.shape[1], right.shape[1]), low)
                 for left, right in zip(lefts, rights)
             ),
         ),
-        in_specs=[inside] * 9 + [anywhere] * 12,
+        in_specs=[inside] * 15 + [anywhere] * 11,
         out_specs=(anywhere,) * 9,
         scratch_shapes=[
             pltpu.VMEM((groups, 2, count, block, columns), low),
             pltpu.VMEM((groups, 2, columns // 2, model_width // groups), low),
             pltpu.VMEM((pieces, rows, width), full),
-            pltpu.VMEM((pieces, rows, width), low),
-            pltpu.VMEM((1, width), full),
             pltpu.VMEM(small.shape, full),
             pltpu.VMEM((groups - 1,) + small.shape, full),
             pltpu.VMEM(small.shape, full),
             pltpu.VMEM((tokens, width), full),
-            pltpu.VMEM((tokens, width), full),
-            pltpu.VMEM((tokens, width), full),
+            pltpu.VMEM((tokens, width), low),
             *(pltpu.VMEM(weight.shape, low) for weight in weights),
             pltpu.VMEM((depth, wide), low),
             pltpu.VMEM((2, depth, tile), low),
-            pltpu.VMEM((2, tile, wide), full),
+            pltpu.VMEM((2, tile, wide), low),
             dma((2 * groups - 2, 2, count + 1)),
             dma((2 * groups - 2, 2, count + 1)),
-            dma((groups,)),
-            dma((groups,)),
             dma((groups - 1,)),
             dma((groups - 1,)),
             dma((parts - 1,)),
             dma((parts - 1,)),
             dma((2, count + 2)),
-            dma((6,)),
+            dma((5,)),
             dma((5,)),
         ]
         + Exchange.scratch(pieces, parts, rows, 8)
+        + Exchange.scratch(pieces, parts, rows, (columns_in[4].shape[1] + 7) // 8 * 8)
+        + Return.scratch(pieces, rows, width, groups)
         + Collect.scratch(pieces, 1, spots, rows, width),
         compiler_params=pltpu.CompilerParams(
             collective_id=collective, has_side_effects=True, vmem_limit_bytes=60 * MIB
         ),
         cost_estimate=lasting(200),
     )(
-        normed_t, gain, marks, small, *grads, gated_t, hidden_grads, hidden, scaled, routed, *weights,
+        normed_t, *columns_in, *grads, gated_t, hidden_grads, hidden, resid, *weights,
         *lefts, *rights,
-    )
-
-
-def precise_dot(left, right):
-    return jnp.dot(
-        left, right, precision=lax.Precision.HIGHEST, preferred_element_type=jnp.float32
     )
 
 
 def settle_kernel(
     came, picks, gates, logits, factor, hidden, grads, gain, router_t,
-    mixed, hidden_grad, gathered, router_grad, gain_grad,
+    back, hidden_grad, gathered, router_grad, gain_grad,
     row_grads, ready, *refs,
 ):
     place = Place()
     exchange = Exchange(place, refs[:4])
+    giving = Return(place, back, refs[4:8])
     pieces, rows, width = row_grads.shape
-    spread = Spread(place, ready, gathered, refs[4:], False)
+    spread = Spread(place, ready, gathered, refs[8:], False)
     slots, experts_of = came.shape[1], logits.shape[1]
     low = jnp.bfloat16
-    place.meet(False, True)
+    place.meet(True, True)
     router_grad[...] = jnp.zeros_like(router_grad)
     gain_grad[...] = jnp.zeros_like(gain_grad)
 
@@ -1261,35 +1322,28 @@
             value = jnp.dot(chosen[way], came[0], preferred_element_type=jnp.float32)
             result = result + gates[here, way : way + 1] * value
             stats = jnp.where(lane == way, jnp.sum(value * grad, axis=1, keepdims=True), stats)
-        mixed[here, :] = result.astype(low)
         total = jnp.dot(chosen[0] + chosen[1], came[1], preferred_element_type=jnp.float32)
         row_grads[piece] = total
         inner = jnp.sum(total * scaled_of(piece) * gain[...], axis=1, keepdims=True)
         exchange.start(piece, jnp.where(lane == 2, inner, stats))
+        giving.start(piece, result.astype(low))
 
     def settle(piece):
         here = band(piece)
         stats = exchange.total(piece, rows)
-        gate = [gates[here, way : way + 1] for way in range(2)]
-        shared = gate[0] * stats[:, :1] + gate[1] * stats[:, 1:2]
-        names = lax.broadcasted_iota(jnp.int32, (rows, experts_of), 1)
-        logit_grad = jnp.zeros((rows, experts_of), jnp.float32)
-        for way in range(2):
-            term = gate[way] * (stats[:, way : way + 1] - shared)
-            logit_grad = logit_grad + jnp.where(picks[here, 2 + way : 3 + way] == names, term, 0.0)
+        logit_grad = pair_grad(
+            [gates[here, way : way + 1] for way in range(2)],
+            [stats[:, way : way + 1] for way in range(2)],
+            [picks[here, 2 + way : 3 + way] for way in range(2)],
+            experts_of,
+        )
         mean = (
             stats[:, 2:3] + jnp.sum(logit_grad * logits[here, :], axis=1, keepdims=True)
         ) / (width * place.parts)
         scaled = scaled_of(piece)
         grad = row_grads[piece] + precise_dot(logit_grad, router_t[...])
         gain_grad[...] += jnp.sum(grad * scaled, axis=0, keepdims=True)
-        router_grad[...] += lax.dot_general(
-            logit_grad,
-            scaled * gain[...],
-            (((0,), (0,)), ((), ())),
-            precision=lax.Precision.HIGHEST,
-            preferred_element_type=jnp.float32,
-        )
+        router_grad[...] += precise_dot(logit_grad, scaled * gain[...], (0, 0))
         result = grads[here, :].astype(jnp.float32) + factor[here, :] * (
             grad * gain[...] - scaled * mean
         )
@@ -1309,33 +1363,36 @@
         spread.third(piece)
         spread.finish(piece)
         exchange.finish(piece)
+        giving.finish(piece)
         return carry
 
     lax.fori_loop(0, pieces, last, 0)
 
 
 def settle(came, picks, gates, logits, factor, hidden, grads, gain, router_t, pieces, collective):
-    parts = lax.axis_size("tensor")
+    groups, parts = lax.axis_size("expert"), lax.axis_size("tensor")
     tokens, width = hidden.shape
     rows = tokens // pieces
     low, full = jnp.bfloat16, jnp.float32
     inside = pl.BlockSpec(memory_space=pltpu.VMEM)
+    anywhere = pl.BlockSpec(memory_space=pl.ANY)
     return pl.pallas_call(
         settle_kernel,
         out_shape=(
-            jax.ShapeDtypeStruct((tokens, width), low),
+            jax.ShapeDtypeStruct((groups, tokens // groups, width), low),
             jax.ShapeDtypeStruct((tokens, width), full),
             jax.ShapeDtypeStruct((1, pieces, rows, width * parts), low),
             jax.ShapeDtypeStruct(router_t.shape, full),
             jax.ShapeDtypeStruct((1, width), full),
         ),
         in_specs=[inside] * 9,
-        out_specs=(inside, inside, pl.BlockSpec(memory_space=pl.ANY), inside, inside),
+        out_specs=(anywhere, inside, anywhere, inside, inside),
         scratch_shapes=[
             pltpu.VMEM((pieces, rows, width), full),
             pltpu.VMEM((1, pieces, rows, width), low),
         ]
         + Exchange.scratch(pieces, parts, rows, 8)
+        + Return.scratch(pieces, rows, width, groups)
         + Spread.scratch(pieces, parts // 2),
         compiler_params=pltpu.CompilerParams(
             collective_id=collective, has_side_effects=True, vmem_limit_bytes=48 * MIB
@@ -1679,7 +1736,7 @@
                 axis=2,
             )
         ).astype(low)
-    mixed_cols, hidden_grad, hidden_grad_low, mlp_router_grad, mlp_gain_grad = settle(
+    back_mixed, hidden_grad, hidden_grad_low, mlp_router_grad, mlp_gain_grad = settle(
         returned.reshape(2, slots, col_width),
         jnp.concatenate([destination, mlp_routes], axis=1),
         mlp_gates,
@@ -1692,7 +1749,7 @@
         pieces,
         4,
     )
-    back_mixed = to_expert(mixed_cols, group_count)
+    back_mixed = back_mixed.reshape(tok_rows, col_width)
     hidden_grad_low = hidden_grad_low.reshape(tok_rows, model_width)
     query_pre_grad, key_pre_grad, value_pre_grad, local_gate_grad, gated_t = attend_back(
         hidden_grad_low,
@@ -1707,26 +1764,6 @@
         sine * sign,
         segment,
     )
-    gate_grads = gather_tensor(local_gate_grad.T)
-    gate_grads = gate_grads.reshape(part_count * local_experts, tok_rows).T
-    attn_pair_grad = jnp.sum(attn_mask * gate_grads[:, None, :], axis=2)
-    attn_logit_grad = pair_back(attn_gates, attn_mask, attn_pair_grad)
-    scaled_cols = resid_cols * factor_one
-    normed_cols = scaled_cols * gain_one
-    attn_router_grad = jnp.dot(normed_cols.T, attn_logit_grad, precision=PRECISE)
-    small = jnp.concatenate(
-        [
-            jnp.zeros((1, col_width), jnp.float32),
-            attn_router_grad.T,
-            mlp_gain_grad,
-            mlp_router_grad,
-        ],
-        axis=0,
-    )
-    small = jnp.pad(small, ((0, -small.shape[0] % 8), (0, 0)))
-    marks = jnp.stack(
-        [factor_one[:, 0], jnp.sum(attn_logit_grad * attn_logits, axis=1)], axis=1
-    )
     rows = inbox.reshape(-1, model_width)
     units = middle.shape[2]
     middle, gate_grad, up_grad = (
@@ -1735,15 +1772,22 @@
     )
     *weight_grads, back_grad, small, gate_w_grad, up_w_grad, down_grad = closing(
         normed_t,
-        gain_one[None],
-        jnp.pad(marks, ((0, 0), (0, 126))),
-        small,
+        (
+            gain_one[None],
+            factor_one,
+            attn_gates,
+            attn_routes,
+            attn_logits,
+            local_gate_grad,
+            router_one.T,
+            mlp_gain_grad,
+            mlp_router_grad,
+        ),
         (query_pre_grad, key_pre_grad, value_pre_grad),
         gated_t,
         hidden_grad_low,
         hidden_grad,
-        scaled_cols,
-        jnp.dot(attn_logit_grad, router_one.T, precision=PRECISE),
+        own_cols(resid_low),
         (w_query, w_key, w_value),
         (rows, rows, middle),
         (gate_grad, up_grad, slot_grads.reshape(-1, model_width)),
@@ -1768,9 +1812,9 @@
         weight_grads[3],
         small[1 + experts_of],
         small[2 + experts_of : 2 + experts_of + expert_count].T,
-        gate_w_grad[None, :, :units],
-        up_w_grad[None, :, :units],
-        down_grad[None, :units],
+        gate_w_grad[None, :, :units].astype(jnp.float32),
+        up_w_grad[None, :, :units].astype(jnp.float32),
+        down_grad[None, :units].astype(jnp.float32),
     )
 
 

time: 666 us -> 642 us (0.964)
  local copies, waits for them, and re-layouts: 44.6 us -> 19.4 us
  other arithmetic: 27 us -> 41.5 us
    unnamed x57 -> x69, local copies, waits for them, and re-layouts: 33.5 us -> 7.54 us
    convert_element_type x0 -> x3, other arithmetic: none -> 16.9 us  [the longest x1 6 us: body(): down_grad[None, :units].astype(jnp.float32)]
    all_to_all x3 -> x2, starting transfers between devices: 19.6 us -> 14.1 us  [to_expert(): lax.all_to_all(rows.reshape(group_count, count // group_count, width), 'e...]
  transfers between devices with their start and end apart: 3 -> 2, of which waited for: 0 -> 0; matrix products, arithmetic and copies ran while one was open for 7% -> 4% of each run, Pallas kernels for 38% -> 8%
where the time goes in v5:
time: 642 us; the launch traced here: 636 us
  Pallas kernels  538 us (84%)
  other arithmetic  41.5 us (6%)
  local copies, waits for them, and re-layouts  19.4 us (3%)
  matrix products  16.2 us (3%)
  starting transfers between devices  14.1 us (2%)
    pallas_call x1, Pallas kernels, experts(): pl.pallas_call(functools.partial(experts_kernel, sharers), out_shape=(jax...  205 us
    pallas_call x1, Pallas kernels, closing(): pl.pallas_call(functools.partial(closing_kernel, tuple(jobs)), out_shape=...  204 us
    pallas_call x1, Pallas kernels, settle(): pl.pallas_call(settle_kernel, out_shape=(jax.ShapeDtypeStruct((groups, to...  31.9 us
    pallas_call x1, Pallas kernels, spread_rows(): pl.pallas_call(functools.partial(spread_kernel, over_expert), out_shape=j...  31.2 us
    pallas_call x1, Pallas kernels, collect_rows(): pl.pallas_call(functools.partial(collect_kernel, make, len(operands)), ou...  28.1 us
    pallas_call x1, Pallas kernels, attend(): pl.pallas_call(attend_kernel, out_shape=(jax.ShapeDtypeStruct((tokens, mo...  21.6 us
    pallas_call x1, Pallas kernels, attend_back(): pl.pallas_call(attend_back_kernel, out_shape=(block, block, block, jax.Sh...  15.5 us
    all_to_all x2, starting transfers between devices, to_expert(): lax.all_to_all(rows.reshape(group_count, count // group_count, width), 'e...  14.1 us
  transfers between devices with their start and end apart: 2, of which 0 were waited for; matrix products, arithmetic and copies ran while one was open for 4% of the time, Pallas kernels for 8%

profile of v5, /device:TPU:20, one launch (start us, length us, event | category | flops | bytes accessed | tf_op | source)
XLA Modules:
  0.0 636.3 jit_solution(4228779845121706216)
XLA Ops:
  0.7 0.9 fusion.38
  1.5 1.0 copy-done
  2.6 1.7 fusion.22
  4.2 2.8 fusion.21
  7.0 31.2 %shard_map.273 = bf16[1,8,96,2048]{3,2,1,0:T(8,128)(2,1)} custom-call(bf16[1,8,96,512]{3,2,1,0:T(8,128)(2,1)} %bitcast.96), custom_call_target="tpu_custom_call" | custom-call | bytes 90000000 | tf_op jit(solution)/shard_map/pallas_call | solution.py:408
  38.3 7.9 %all-to-all-start = ((bf16[8,96,512]{2,1,0:T(8,128)(2,1)}), bf16[8,96,512]{2,1,0:T(8,128)(2,1)S(1)}, u32[]{:S(2)}, u32[]{:S(2)}) async-start(bf16[8,96,512]{2,1,0:T(8,128)(2,1)} %bitcast.2), calls=%async_computation | async-start | bytes 1572864 | tf_op jit(solution)/shard_map/all_to_all | solution.py:1583
  46.4 0.6 broadcast_in_dim.114.segment_row
  47.0 0.9 broadcast_in_dim.124.segment_column
  48.7 2.0 convert_reduce_fusion
  51.5 0.9 pad.8.router
  52.4 2.5 sine_multiply_fusion
  54.9 21.6 %shard_map.274 = (bf16[768,2048]{1,0:T(8,128)(2,1)}, bf16[2048,768]{1,0:T(8,128)(2,1)}, f32[768,1]{1,0:T(8,128)}, f32[768,128]{1,0:T(8,128)}, bf16[768,512]{1,0:...) custom-call(bf16[768,2048]{1,0:T(8,128)(2,1)} %bitcast.76, ...), custom_call_target="tpu_custom_call" | custom-call | bytes 60000000 | tf_op jit(solution)/shard_map/pallas_call | solution.py:1476
  76.5 1.3 slice_add_fusion.refs_5_
  78.7 0.7 copy-done.13
  79.7 0.4 slice_reduce_fusion.3
  80.4 3.1 fusion.8
  83.5 0.9 copy-done.5
  84.4 6.3 all-to-all-start.1
  90.7 1.3 dynamic_slice.31
  92.1 1.0 copy.111.refs_4_
  93.0 0.8 dynamic_slice.30
  94.0 0.7 dynamic-slice_bitcast_fusion
  94.7 2.1 pad_add_fusion.picks
  96.7 28.1 %shard_map.275 = f32[4,192,512]{2,1,0:T(8,128)S(1)} custom-call(bf16[4,192,512]{2,1,0:T(8,128)(2,1)S(1)} %bitcast.68, f32[4,192,2]{2,1,0:T(8,128)S(1)} %bitcast.67, bf16[512,2048]{1,0:T(8,128)(2,1)S(1)} %copy-done.2), custom_call_target="tpu_custom_call" | custom-call | bytes 78000000 | tf_op jit(solution)/shard_map/pallas_call | solution.py:453
  124.8 2.4 multiply_reduce_fusion
  127.2 0.7 fusion.19
  128.0 5.6 all-gather.1
  134.9 1.4 select_reduce_fusion
  136.6 4.6 fusion.5
  141.2 0.6 broadcast_in_dim.121.refs_2_
  141.8 205.4 %shard_map.276 = (bf16[1,8,240,2048]{3,2,1,0:T(8,128)(2,1)}, bf16[1,8,240,2048]{3,2,1,0:T(8,128)(2,1)}, bf16[8,240,2048]{2,1,0:T(8,128)(2,1)}, bf16[8,240,1408]{...) custom-call(bf16[1,8,240,512]{3,2,1,0:T(8,128)(2,1)} %bitcast.95, ...), custom_call_target="tpu_custom_call" | custom-call | bytes 540000000 | tf_op jit(solution)/shard_map/pallas_call | solution.py:693
  347.2 31.9 %shard_map.277 = (bf16[8,96,512]{2,1,0:T(8,128)(2,1)S(1)}, f32[768,512]{1,0:T(8,128)S(1)}, bf16[1,4,192,2048]{3,2,1,0:T(8,128)(2,1)}, f32[8,512]{1,0:T(8,128)S(1)}, f32[1,512]{1,0:T(1,128)S(1)}) custom-call(bf16[2,1920,512]{2,1,0:T(8,128)(2,1)} %bitcast.93, s32[768,4]{1,0:T(8,128)S(1)} %copy-done.7, f32[768,2]{1,0:T(8,128)S(1)} %exponential_divide_fusion.gates, ...), custom_call_target="tpu_custom_call" | custom-call | bytes 90000000 | tf_op jit(solution)/shard_map/pallas_call | solution.py:1379
  379.2 1.1 copy-done.8
  380.3 0.6 copy-done.9
  380.9 15.5 %shard_map.278 = (bf16[768,512]{1,0:T(8,128)(2,1)}, bf16[768,512]{1,0:T(8,128)(2,1)}, bf16[768,512]{1,0:T(8,128)(2,1)}, f32[768,2]{1,0:T(8,128)}, bf16[512,768]{1,0:T(8,128)(2,1)}) custom-call(bf16[768,2048]{1,0:T(8,128)(2,1)} %bitcast.78, bf16[512,2048]{1,0:T(8,128)(2,1)} %w_out.1, f32[768,2]{1,0:T(8,128)} %copy-done.3, ...), custom_call_target="tpu_custom_call" | custom-call | bytes 75000000 | tf_op jit(solution)/shard_map/pallas_call | solution.py:1557
  396.5 204.0 %shard_map.279 = (bf16[2048,512]{1,0:T(8,128)(2,1)}, bf16[2048,512]{1,0:T(8,128)(2,1)}, bf16[2048,512]{1,0:T(8,128)(2,1)}, bf16[512,2048]{1,0:T(8,128)(2,1)}, bf...) custom-call(bf16[2048,768]{1,0:T(8,128)(2,1)} %get-tuple-element.58., ...), custom_call_target="tpu_custom_call" | custom-call | bytes 600000000 | tf_op jit(solution)/shard_map/pallas_call | solution.py:1240
  600.5 1.6 fusion.51
  602.1 1.6 fusion.50
  603.7 1.7 fusion.23
  605.4 1.7 fusion.24
  607.1 2.6 convert_element_type.87
  609.7 2.7 convert_element_type.88
  612.5 2.7 convert_element_type.89
  615.2 1.0 copy-done.16
  616.2 2.7 convert_element_type.90
  618.9 5.7 bitcast_convert_fusion.2
  624.6 5.2 bitcast_convert_fusion.1
  629.8 6.0 bitcast_convert_fusion
  (111 shorter events, 5.0 us)
Async XLA Ops:
  0.6 1.9 copy-start
  7.0 39.1 %copy-start.26 = (s32[1,3]{1,0:T(1,128)S(1)}, s32[1,3]{1,0:T(1,128)}, u32[]{:S(2)}) copy-start(s32[1,3]{1,0:T(1,128)} %param.32) | copy-start | bytes 40
  7.0 40.9 %copy-start.22 = (s32[768,2]{0,1:T(2,128)S(1)}, s32[768,2]{0,1:T(2,128)}, u32[]{:S(2)}) copy-start(s32[768,2]{0,1:T(2,128)} %param.34) | copy-start | bytes 18436
  7.0 41.2 %copy-start.24 = (s32[1,1536]{1,0:T(1,128)S(1)}, s32[1,1536]{1,0:T(1,128)}, u32[]{:S(2)}) copy-start(s32[1,1536]{1,0:T(1,128)} %param.35) | copy-start | bytes 18436
  7.0 41.3 %copy-start.20 = (f32[2048,8]{0,1:T(8,128)S(1)}, f32[2048,8]{0,1:T(8,128)}, u32[]{:S(2)}) copy-start(f32[2048,8]{0,1:T(8,128)} %param.21) | copy-start | bytes 196612
  38.3 41.8 %all-to-all-start = ((bf16[8,96,512]{2,1,0:T(8,128)(2,1)}), bf16[8,96,512]{2,1,0:T(8,128)(2,1)S(1)}, u32[]{:S(2)}, u32[]{:S(2)}) async-start(bf16[8,96,512]{2,1,0:T(8,128)(2,1)} %bitcast.2), calls=%async_computation | async-start | bytes 1572864 | tf_op jit(solution)/shard_map/all_to_all | solution.py:1583
  48.1 28.4 %copy-start.15 = (s32[768,2]{1,0:T(8,128)}, s32[768,2]{1,0:T(8,128)S(1)}, u32[]{:S(2)}) copy-start(s32[768,2]{1,0:T(8,128)S(1)} %copy.96) | copy-start | bytes 18436
  54.9 23.0 %copy-start.21 = (s32[768,2]{0,1:T(2,128)S(1)}, s32[768,2]{0,1:T(2,128)}, u32[]{:S(2)}) copy-start(s32[768,2]{0,1:T(2,128)} %param.33) | copy-start | bytes 18436
  77.8 0.7 copy-start.14
  78.7 0.8 copy-start.13
  79.7 0.7 copy-start.12
  83.5 0.9 copy-start.5
  84.4 9.5 %copy-start.23 = (f32[2048,8]{0,1:T(8,128)S(1)}, f32[2048,8]{0,1:T(8,128)}, u32[]{:S(2)}) copy-start(f32[2048,8]{0,1:T(8,128)} %param.27) | copy-start | bytes 196612
  84.4 12.3 %copy-start.2 = (bf16[512,2048]{1,0:T(8,128)(2,1)S(1)}, bf16[512,2048]{1,0:T(8,128)(2,1)}, u32[]{:S(2)}) copy-start(bf16[512,2048]{1,0:T(8,128)(2,1)} %w_out.1) | copy-start | bytes 6291460
  84.4 12.3 %copy-start.4 = (bf16[768,512]{1,0:T(8,128)(2,1)S(1)}, bf16[768,512]{1,0:T(8,128)(2,1)}, u32[]{:S(2)}) copy-start(bf16[768,512]{1,0:T(8,128)(2,1)} %get-tuple-element.53.heads) | copy-start | bytes 2359300
  84.4 56.8 %all-to-all-start.1 = ((bf16[8,240,512]{2,1,0:T(8,128)(2,1)}), bf16[8,240,512]{2,1,0:T(8,128)(2,1)}, u32[]{:S(2)}, u32[]{:S(2)}) async-start(bf16[8,240,512]{2,1,0:T(8,128)(2,1)} %bitcast.94), calls=%async_computation.1 | async-start | bytes 3932160 | tf_op jit(solution)/shard_map/all_to_all | solution.py:1583
  94.0 33.2 %copy-start.3 = (f32[768,2]{1,0:T(8,128)}, f32[768,2]{1,0:T(8,128)S(1)}, u32[]{:S(2)}) copy-start(f32[768,2]{1,0:T(8,128)S(1)} %copy.113.gates) | copy-start | bytes 18436
  127.2 6.5 %copy-start.11 = (f32[768,512]{1,0:T(8,128)}, f32[768,512]{1,0:T(8,128)S(1)}, u32[]{:S(2)}) copy-start(f32[768,512]{1,0:T(8,128)S(1)} %get-tuple-element.92.hidden) | copy-start | bytes 4718596
  141.8 205.4 %copy-start.6 = (bf16[8,96,512]{2,1,0:T(8,128)(2,1)S(1)}, bf16[8,96,512]{2,1,0:T(8,128)(2,1)}, u32[]{:S(2)}) copy-start(bf16[8,96,512]{2,1,0:T(8,128)(2,1)} %copy-done.5) | copy-start | bytes 2359300
  141.8 205.4 %copy-start.7 = (s32[768,4]{1,0:T(8,128)S(1)}, s32[768,4]{1,0:T(8,128)}, u32[]{:S(2)}) copy-start(s32[768,4]{1,0:T(8,128)} %pad_add_fusion.picks) | copy-start | bytes 36868
  379.2 1.1 copy-start.8
  380.3 0.6 copy-start.9
  380.9 15.5 %copy-start.10 = (f32[1,512]{1,0:T(1,128)}, f32[1,512]{1,0:T(1,128)S(1)}, u32[]{:S(2)}) copy-start(f32[1,512]{1,0:T(1,128)S(1)} %get-tuple-element.66.refs_8_) | copy-start | bytes 6148
  600.5 4.9 copy-start.25
  603.7 3.4 copy-start.19
  607.1 2.6 copy-start.18
  609.7 2.7 copy-start.17
  609.7 9.1 %slice-start.4 = ((s8[5767168]{0:T(1024)(128)(4,1)}), s8[4194304]{0:T(1024)(128)(4,1)S(1)}, s32[]{:S(2)}) async-start(s8[5767168]{0:T(1024)(128)(4,1)} %bitcast.85), calls=%async_computation.6 | async-start | bytes 8388608
  612.5 3.7 copy-start.16
  612.5 6.4 %slice-start.5 = ((s8[5767168]{0:T(1024)(128)(4,1)}), s8[1572864]{0:T(1024)(128)(4,1)S(1)}, s32[]{:S(2)}) async-start(s8[5767168]{0:T(1024)(128)(4,1)} %bitcast.85), calls=%async_computation.7 | async-start | bytes 3145728
  616.2 8.4 %slice-start.2 = ((s8[5767168]{0:T(1024)(128)(4,1)}), s8[4194304]{0:T(1024)(128)(4,1)S(1)}, s32[]{:S(2)}) async-start(s8[5767168]{0:T(1024)(128)(4,1)} %bitcast.83), calls=%async_computation.4 | async-start | bytes 8388608
  618.9 5.7 slice-start.3
  618.9 10.9 %slice-start = ((s8[5767168]{0:T(1024)(128)(4,1)}), s8[4194304]{0:T(1024)(128)(4,1)S(1)}, s32[]{:S(2)}) async-start(s8[5767168]{0:T(1024)(128)(4,1)} %bitcast.81), calls=%async_computation.2 | async-start | bytes 8388608
  624.6 5.2 slice-start.1
  629.8 6.0 copy-start.1

commit v6 on v5

--- a/solution.py
+++ b/solution.py
@@ -3,6 +3,7 @@
 
 import jax
 import jax.numpy as jnp
+import numpy as np
 from jax import lax
 from jax.experimental import pallas as pl
 from jax.experimental.pallas import tpu as pltpu
@@ -12,46 +13,24 @@
 QH = 2
 
 
-PRECISE = lax.Precision.HIGH
 EPSILON = 1e-06
 MASKED = -1e30
 
 
-def rotary_tables(lengths, tok_rows):
-    seq_ends = jnp.cumsum(lengths)
-    seq_starts = seq_ends - lengths
-    places = jnp.arange(tok_rows, dtype=jnp.int32)
-    segment = jnp.sum((places[:, None] >= seq_ends[None, :]).astype(jnp.int32), axis=1)
-    matches = segment[:, None] == jnp.arange(lengths.shape[0], dtype=jnp.int32)[None, :]
-    seq_first = jnp.sum(jnp.where(matches, seq_starts[None, :], 0), axis=1)
-    offsets = (places - seq_first).astype(jnp.float32)
-    frequency = jnp.exp(-math.log(10000.0) * jnp.arange(0, HEAD, 2, dtype=jnp.float32) / HEAD)
-    angles = offsets[:, None] * frequency[None, :]
-    angles = jnp.concatenate([angles, angles], axis=1)
-    return (segment, jnp.cos(angles), jnp.sin(angles))
-
-
-def pair_gates(logits, routes):
-    columns = logits.shape[1]
-    chosen_mask = (
-        routes[:, :, None] == jnp.arange(columns, dtype=jnp.int32)[None, None, :]
-    ).astype(jnp.float32)
-    picked = jnp.sum(chosen_mask * logits[:, None, :], axis=2)
-    return (jax.nn.softmax(picked, axis=1), chosen_mask)
-
-
-def slot_table(routes, priority, capacity):
-    target = routes.reshape(-1)
-    ahead = (target[None, :] == target[:, None]) & (priority[None, :] < priority[:, None])
-    position = jnp.sum(ahead.astype(jnp.int32), axis=1)
-    return (target, position, position < capacity)
+def rotary_tables(tokens):
+    frequency = np.exp(-math.log(10000.0) * np.arange(0, HEAD, 2, dtype=np.float32) / HEAD)
+    angles = np.arange(tokens, dtype=np.float32)[:, None] * frequency.astype(np.float32)[None, :]
+    angles = np.concatenate([angles, angles], axis=1).astype(np.float64)
+    return jnp.asarray(np.cos(angles), jnp.float32), jnp.asarray(np.sin(angles), jnp.float32)
 
 
 MESH = pl.DeviceIdType.MESH
 MIB = 1 << 20
 AHEAD_DEAL = 2
 AHEAD = 2
-EARLY = 2
+FRONT = 3
+SQUARES = 8
+ROUTES, ROUTES_TWO, SLOTS = 0, 2, 4
 
 
 def flip(number, other, count):
@@ -379,17 +358,76 @@
     pl.when(condition)(functools.partial(action, *args))
 
 
-def spread_kernel(over_expert, source, target, *sems):
+def columns_of(rows):
+    blank = jnp.zeros((128 - rows.shape[0], rows.shape[1]), jnp.float32)
+    return jnp.concatenate([rows, blank], axis=0).T
+
+
+def deal_kernel(
+    capacity, experts_of, tokens, out_grad, ranks, rows_in,
+    full, dealt_grads, marks, mark_rows,
+    held, sending, slots, load_sem, *sems,
+):
     place = Place()
-    spread = Spread(place, source, target, sems, over_expert)
-    place.meet(over_expert)
+    count, width = held.shape[1:]
+    groups, bucket, _ = dealt_grads.shape
+    low = jnp.bfloat16
+    own = pl.ds(pl.multiple_of(place.tensor * width, 128), width)
+    loads = [
+        pltpu.make_async_copy(source.at[:, own], held.at[number], load_sem.at[number])
+        for number, source in enumerate((tokens, out_grad))
+    ]
+    for load in loads:
+        load.start()
+    spread = Spread(place, sending, full, sems, True)
+    place.meet(True)
+
+    def dealt(number, group):
+        rank = lax.broadcasted_iota(jnp.int32, (bucket, count), 0) + group * bucket
+        chosen = (ranks[...] == rank).astype(low)
+        return jnp.dot(chosen, held[number], preferred_element_type=jnp.float32).astype(low)
+
+    loads[0].wait()
+    for group in range(groups):
+        sending[0, group] = dealt(0, group)
     spread.start(AHEAD_DEAL)
+
+    def number_slots():
+        rows = rows_in[...].astype(jnp.float32)
+        columns = columns_of(rows)
+        lane = lax.broadcasted_iota(jnp.int32, (count, 128), 1)
+        found = jnp.zeros((count, 128), jnp.float32)
+        for way in range(2):
+            target = columns[:, ROUTES_TWO + way : ROUTES_TWO + way + 1]
+            order = columns[:, 4 + way : 5 + way]
+            position = jnp.zeros((count, 1), jnp.float32)
+            for other in range(2):
+                earlier = (rows[ROUTES_TWO + other : ROUTES_TWO + other + 1] == target) & (
+                    rows[4 + other : 5 + other] < order
+                )
+                position = position + jnp.sum(
+                    jnp.where(earlier, 1.0, 0.0), axis=1, keepdims=True
+                )
+            slot = jnp.where(
+                position < capacity, target * capacity + position, experts_of * capacity
+            )
+            marks[:, SLOTS + way : SLOTS + way + 1] = slot.astype(jnp.int32)
+            found = jnp.where(lane == way, slot, found)
+        marks[:, :SLOTS] = columns[:, :SLOTS].astype(jnp.int32)
+        slots[...] = found
+        mark_rows[...] = slots[...].T[:8].astype(jnp.int32)
+
+    def deal_grads():
+        loads[1].wait()
+        for group in range(groups):
+            dealt_grads[group] = dealt(1, group)
 
     def step(turn, carry):
         when(turn < spread.chunks, spread.first, turn)
-        if over_expert:
-            when(turn + 1 + AHEAD_DEAL < spread.chunks, spread.send, turn + 1 + AHEAD_DEAL)
+        when(turn + 1 + AHEAD_DEAL < spread.chunks, spread.send, turn + 1 + AHEAD_DEAL)
         when(turn >= 1, spread.second, turn - 1)
+        when(turn == 1, deal_grads)
+        when(turn == 2, number_slots)
         return carry
 
     lax.fori_loop(0, spread.chunks + 1, step, 0)
@@ -402,92 +440,48 @@
     lax.fori_loop(0, spread.chunks, last, 0)
 
 
-def spread_rows(rows, over_expert, collective, microseconds):
-    chunks, count, width = rows.shape
-    parts = lax.axis_size("tensor")
-    full = pl.pallas_call(
-        functools.partial(spread_kernel, over_expert),
-        out_shape=jax.ShapeDtypeStruct((1, chunks, count, width * parts), rows.dtype),
-        in_specs=[pl.BlockSpec(memory_space=pl.ANY)],
-        out_specs=pl.BlockSpec(memory_space=pl.ANY),
-        scratch_shapes=Spread.scratch(chunks, parts // 2),
-        compiler_params=pltpu.CompilerParams(collective_id=collective, has_side_effects=True),
-        cost_estimate=lasting(microseconds),
-    )(rows[None])
-    return full.reshape(chunks * count, width * parts)
-
-
-def collect_kernel(make, operand_count, *refs):
-    place = Place()
-    operands = refs[:operand_count]
-    result = refs[operand_count]
-    collect = Collect(place, refs[operand_count + 1 :])
-    place.meet(False)
-
-    def one(chunk):
-        collect.free_stage(chunk)
-        slot = lax.rem(chunk, 2)
-        width = result.shape[2]
-        for spot in range(place.spots):
-            for core in range(2):
-                first = (spot * 2 + core) * width
-                part = make(operands, chunk, first, width)
-                collect.stage[slot, 0, spot, core] = part.astype(jnp.bfloat16)
-        collect.first(chunk)
-
-    def close(chunk):
-        result[chunk] = collect.third(chunk)[0]
-
-    def step(turn, carry):
-        when(turn >= 2, close, turn - 2)
-        when((turn >= 1) & (turn <= collect.chunks), collect.second, turn - 1)
-        when(turn < collect.chunks, one, turn)
-        return carry
-
-    lax.fori_loop(0, collect.chunks + 2, step, 0)
-    collect.finish()
-
-
-def collect_rows(make, operands, chunks, rows, width, collective):
-    parts = lax.axis_size("tensor")
-    out = pl.pallas_call(
-        functools.partial(collect_kernel, make, len(operands)),
-        out_shape=jax.ShapeDtypeStruct((chunks, rows, width), jnp.float32),
-        in_specs=[pl.BlockSpec(memory_space=pltpu.VMEM)] * len(operands),
-        out_specs=pl.BlockSpec(memory_space=pltpu.VMEM),
-        scratch_shapes=Collect.scratch(chunks, 1, parts // 2, rows, width),
+def deal_rows(tokens, out_grad, ranks, rows_in, capacity, experts_of, collective):
+    groups, parts = lax.axis_size("expert"), lax.axis_size("tensor")
+    count, model_width = tokens.shape
+    width, bucket = model_width // parts, count // groups
+    low = tokens.dtype
+    inside = pl.BlockSpec(memory_space=pltpu.VMEM)
+    anywhere = pl.BlockSpec(memory_space=pl.ANY)
+    return pl.pallas_call(
+        functools.partial(deal_kernel, capacity, experts_of),
+        out_shape=(
+            jax.ShapeDtypeStruct((1, groups, bucket, model_width), low),
+            jax.ShapeDtypeStruct((groups, bucket, width), low),
+            jax.ShapeDtypeStruct((count, 8), jnp.int32),
+            jax.ShapeDtypeStruct((8, count), jnp.int32),
+        ),
+        in_specs=[anywhere] * 2 + [inside] * 2,
+        out_specs=(anywhere,) + (inside,) * 3,
+        scratch_shapes=[
+            pltpu.VMEM((2, count, width), low),
+            pltpu.VMEM((1, groups, bucket, width), low),
+            pltpu.VMEM((count, 128), jnp.float32),
+            pltpu.SemaphoreType.DMA((2,)),
+        ]
+        + Spread.scratch(groups, parts // 2),
         compiler_params=pltpu.CompilerParams(
-            collective_id=collective, has_side_effects=True, vmem_limit_bytes=48 * MIB
+            collective_id=collective, has_side_effects=True, vmem_limit_bytes=40 * MIB
         ),
-        cost_estimate=lasting(26),
-    )(*operands)
-    return out.reshape(chunks * rows, width)
-
-
-def make_attended(span, operands, chunk, first, width):
-    heads, gates, weight = operands
-    total = None
-    for expert in range(gates.shape[2]):
-        term = gates[chunk, :, expert : expert + 1] * jnp.dot(
-            heads[chunk, :, expert * span : (expert + 1) * span],
-            weight[expert * span : (expert + 1) * span, first : first + width],
-            preferred_element_type=jnp.float32,
-        )
-        total = term if total is None else total + term
-    return total
+        cost_estimate=lasting(35),
+    )(tokens, out_grad, ranks, rows_in)
 
 
 def experts_kernel(sharers, *refs):
     (
-        source, source_grads, gates, gate_hbm, up_hbm, down_hbm,
+        source, source_grads, gates, gate_hbm, up_hbm, down_hbm, early_grads,
         inbox, inbox_grads, grads_out, middle_out, gate_out, up_out, returned,
         gate_w, up_w, down_w, rows, grads, middle, gate_g, up_g, closing, gates_in,
         load_sem, store_sem, back_send, back_land, mark_send, mark_land,
-    ) = refs[:29]
+    ) = refs[:30]
     place = Place()
-    spread = Spread(place, source, inbox, refs[29:35], True, sharers)
-    spread_grads = Spread(place, source_grads, inbox_grads, refs[35:41], False, by_group=True)
-    collect = Collect(place, refs[41:])
+    spread = Spread(place, source, inbox, refs[30:36], True, sharers)
+    spread_grads = Spread(place, source_grads, inbox_grads, refs[36:42], True, sharers)
+    collect = Collect(place, refs[42:])
     chunks = spread.chunks
     width = source.shape[3]
     units = gate_w.shape[1]
@@ -531,8 +525,9 @@
     )
     own_mark.start()
     own_mark.wait()
-    for chunk in range(EARLY):
-        spread_grads.first(chunk)
+    early = min(FRONT, chunks)
+    for chunk in range(early, min(AHEAD + 1, chunks)):
+        spread_grads.send(chunk)
 
     def stores(owner):
         return [
@@ -545,6 +540,7 @@
     def fetches(owner):
         return [
             pltpu.make_async_copy(inbox.at[0, owner], rows, load_sem.at[3]),
+            pltpu.make_async_copy(early_grads.at[0, owner], grads, load_sem.at[4]),
             pltpu.make_async_copy(inbox_grads.at[0, owner], grads, load_sem.at[4]),
         ]
 
@@ -563,12 +559,13 @@
             mark_landed(chunk).wait_recv()
 
         spread.third(chunk)
-        spread_grads.third(chunk)
-        copies = fetches(owner)
-        for fetch in copies:
-            fetch.start()
-        for fetch in copies:
-            fetch.wait()
+        when(chunk >= early, spread_grads.third, chunk)
+        fetch, fetch_early, fetch_late = fetches(owner)
+        fetch.start()
+        when(chunk < early, fetch_early.start)
+        when(chunk >= early, fetch_late.start)
+        fetch.wait()
+        fetch_early.wait()
         wide = gates_in.shape[2]
         line = jnp.broadcast_to(gates_in[owner][:1], (capacity, wide))
         here = lax.broadcasted_iota(jnp.int32, (capacity, wide), 0) == lax.broadcasted_iota(
@@ -646,13 +643,17 @@
             own.start()
             own.wait()
 
+    def send_grads(chunk):
+        when(chunk >= early, spread_grads.send, chunk)
+
     def step(turn, carry):
         now = turn - 2
         when(turn < chunks, spread.first, turn)
         when(turn + 1 + AHEAD < chunks, spread.send, turn + 1 + AHEAD)
         when((turn >= 1) & (turn <= chunks), spread.second, turn - 1)
-        when(turn + EARLY < chunks, spread_grads.first, turn + EARLY)
-        when((turn >= 1) & (turn <= chunks), spread_grads.second, turn - 1)
+        when((turn >= early - 1 - AHEAD) & (turn + 1 + AHEAD < chunks), send_grads, turn + 1 + AHEAD)
+        when((turn >= early) & (turn < chunks), spread_grads.first, turn)
+        when((turn > early) & (turn <= chunks), spread_grads.second, turn - 1)
         when(now >= 0, work, now)
         return carry
 
@@ -664,7 +665,7 @@
 
     def last(turn, carry):
         spread.finish(turn)
-        spread_grads.finish(turn)
+        when(turn >= early, spread_grads.finish, turn)
 
         @pl.when(turn > 0)
         def _():
@@ -682,7 +683,7 @@
     collect.finish()
 
 
-def experts(source, source_grads, gates, gate_w, up_w, down_w, sharers, collective):
+def experts(source, source_grads, early_grads, gates, gate_w, up_w, down_w, sharers, collective):
     _, capacity, width = source.shape
     groups, parts = lax.axis_size("expert"), lax.axis_size("tensor")
     spots = parts // 2
@@ -701,7 +702,7 @@
             hidden_rows,
             jax.ShapeDtypeStruct((2, groups, capacity, width), low),
         ),
-        in_specs=[anywhere] * 6,
+        in_specs=[anywhere] * 7,
         out_specs=(anywhere,) * 7,
         scratch_shapes=[
             pltpu.VMEM((model_width, units), low),
@@ -728,7 +729,7 @@
             collective_id=collective, has_side_effects=True, vmem_limit_bytes=60 * MIB
         ),
         cost_estimate=lasting(180),
-    )(source[None], source_grads[None], gates, gate_w, up_w, down_w)
+    )(source[None], source_grads[None], gates, gate_w, up_w, down_w, early_grads)
 
 
 class Return:
@@ -857,7 +858,7 @@
 
 def closing_kernel(jobs, *refs):
     (
-        normed_t, gain, factor, gates, routes, logits, gate_grads, router_t, gain_two, router_two,
+        normed_t, gain, factor, gates, marks, logits, gate_grads, router_t, gain_two, router_two,
         query_grad, key_grad, value_grad, gated_t, hidden_grads,
         hidden_hbm, resid_hbm, query_hbm, key_hbm, value_hbm,
     ), refs = refs[:20], refs[20:]
@@ -881,12 +882,13 @@
     width = hidden.shape[1]
     block = hold.shape[3]
     experts_of = logits.shape[1]
+    own_columns = pl.ds(pl.multiple_of(place.tensor * width, 128), width)
     loads = [
         pltpu.make_async_copy(held, kept, load_sem.at[number])
         for number, (held, kept) in enumerate(
             (
                 (query_hbm, w_query), (key_hbm, w_key), (value_hbm, w_value),
-                (hidden_hbm, hidden), (resid_hbm, resid),
+                (hidden_hbm, hidden), (resid_hbm.at[:, own_columns], resid),
             )
         )
     ]
@@ -1037,7 +1039,7 @@
         here = band(piece)
         every = of_gates.total(piece, rows)[:, :experts_of]
         lane = lax.broadcasted_iota(jnp.int32, (rows, experts_of), 1)
-        names = [routes[here, way : way + 1] for way in range(2)]
+        names = [marks[here, ROUTES + way : ROUTES + way + 1] for way in range(2)]
         logit_grad = pair_grad(
             [gates[here, way : way + 1] for way in range(2)],
             [
@@ -1289,7 +1291,7 @@
 
 
 def settle_kernel(
-    came, picks, gates, logits, factor, hidden, grads, gain, router_t,
+    came, marks, gates, logits, factor, hidden, grads, gain, router_t,
     back, hidden_grad, gathered, router_grad, gain_grad,
     row_grads, ready, *refs,
 ):
@@ -1313,7 +1315,7 @@
     def gather(piece):
         here = band(piece)
         numbers = lax.broadcasted_iota(jnp.int32, (rows, slots), 1)
-        chosen = [(picks[here, way : way + 1] == numbers).astype(low) for way in range(2)]
+        chosen = [(marks[here, SLOTS + way : SLOTS + way + 1] == numbers).astype(low) for way in range(2)]
         result = hidden[here, :]
         grad = grads[here, :].astype(jnp.float32)
         lane = lax.broadcasted_iota(jnp.int32, (rows, 128), 1)
@@ -1334,7 +1336,7 @@
         logit_grad = pair_grad(
             [gates[here, way : way + 1] for way in range(2)],
             [stats[:, way : way + 1] for way in range(2)],
-            [picks[here, 2 + way : 3 + way] for way in range(2)],
+            [marks[here, ROUTES_TWO + way : ROUTES_TWO + way + 1] for way in range(2)],
             experts_of,
         )
         mean = (
@@ -1369,7 +1371,7 @@
     lax.fori_loop(0, pieces, last, 0)
 
 
-def settle(came, picks, gates, logits, factor, hidden, grads, gain, router_t, pieces, collective):
+def settle(came, marks, gates, logits, factor, hidden, grads, gain, router_t, pieces, collective):
     groups, parts = lax.axis_size("expert"), lax.axis_size("tensor")
     tokens, width = hidden.shape
     rows = tokens // pieces
@@ -1398,7 +1400,7 @@
             collective_id=collective, has_side_effects=True, vmem_limit_bytes=48 * MIB
         ),
         cost_estimate=lasting(30),
-    )(came, picks, gates, logits, factor, hidden, grads, gain, router_t)
+    )(came, marks, gates, logits, factor, hidden, grads, gain, router_t)
 
 
 def dot_tn(left, right):
@@ -1412,35 +1414,112 @@
     return [(first, size) for first in range(0, tokens, size)]
 
 
-def masked_scores(query, keys, segment_column, segment_row, first, size, column):
+def sequence_starts(lengths):
+    starts = [0]
+    for number in range(lengths.shape[1] - 1):
+        starts.append(starts[-1] + lengths[0, number])
+    return starts
+
+
+def masked_scores(query, keys, lengths, first, size, column):
     last = first + size
-    rows = slice(first, last)
-    scores = dot_nt(query[rows, column], keys[:last, column]) * (1.0 / math.sqrt(HEAD))
-    place = lax.broadcasted_iota(jnp.int32, (size, last), 0) + first
+    scores = dot_nt(query[first:last, column], keys[:last, column]) * (1.0 / math.sqrt(HEAD))
+    place = lax.broadcasted_iota(jnp.int32, (size, 1), 0) + first
+    start = jnp.zeros((size, 1), jnp.int32)
+    for value in sequence_starts(lengths)[1:]:
+        start = jnp.where(place >= value, value, start)
     other = lax.broadcasted_iota(jnp.int32, (size, last), 1)
-    allowed = (segment_column[rows, :] == segment_row[:, :last]) & (place >= other)
-    return jnp.where(allowed, scores, MASKED)
-
-
-def attend_kernel(
-    resid, gain, router, w_query, w_key, w_value, cosine, sine, segment_column, segment_row,
-    normed, normed_t, factor, logits, query, keys, values, heads, log_total,
-):
+    return jnp.where((other >= start) & (place >= other), scores, MASKED)
+
+
+def chosen_gates(logits, names):
+    lane = lax.broadcasted_iota(jnp.int32, logits.shape, 1)
+    picked = [
+        jnp.sum(jnp.where(name == lane, logits, 0.0), axis=1, keepdims=True) for name in names
+    ]
+    top = jnp.maximum(picked[0], picked[1])
+    expo = [jnp.exp(value - top) for value in picked]
+    total = expo[0] + expo[1]
+    return [value / total for value in expo]
+
+
+def front_kernel(sharers, *refs):
+    (
+        resid, gain, router_t, w_query, w_key, w_value, w_out, cosines, sines,
+        marks, mark_rows, gain_two, router_two_t, lengths, dealt,
+        normed_t, cosine, sine, factor, logits, gates, gate_local, query, keys, values, heads, log_total,
+        hidden, factor_two, logits_two, gates_two, sent_rows, lines,
+        grads_back, grads_out, inbox_grads,
+        normed_two, grads_here, grads_slots,
+        deal_send, deal_land, load_sem,
+    ), refs = refs[:42], refs[42:]
+    place = Place()
+    spread = Spread(place, grads_slots, inbox_grads, refs[:6], True, sharers)
+    exchange = Exchange(place, refs[6:10])
+    collect = Collect(place, refs[10:])
     tokens, columns = query.shape
+    width = hidden.shape[1]
+    groups = place.groups
+    capacity = sent_rows.shape[1]
+    experts_of = logits.shape[1]
+    held = gate_local.shape[1]
+    span = columns // held
     low = jnp.bfloat16
-    for first, size in bands(tokens):
+    parts = list(enumerate(bands(tokens)))
+    place.meet(True, True)
+
+    def deal_copy(step, index):
+        peer = flip(place.expert, step, groups)
+        return remote(
+            dealt.at[peer],
+            grads_back.at[index],
+            deal_send.at[step],
+            deal_land.at[step],
+            place.device(peer, place.tensor),
+        )
+
+    for step in range(1, groups):
+        deal_copy(step, place.expert).start()
+    own = pltpu.make_async_copy(
+        dealt.at[place.expert], grads_back.at[place.expert], deal_send.at[0]
+    )
+    own.start()
+    router_high = router_t[...].astype(low)
+    router_rest = (router_t[...] - router_high.astype(jnp.float32)).astype(low)
+    columns_here = pl.ds(pl.multiple_of(place.tensor * width, 128), width)
+    for _, (first, size) in parts:
         rows = slice(first, first + size)
+        spot = lax.broadcasted_iota(jnp.int32, (size, 1), 0) + first
+        start_cosine = jnp.broadcast_to(cosines[0:1, :], (size, HEAD))
+        start_sine = jnp.broadcast_to(sines[0:1, :], (size, HEAD))
+        for start in sequence_starts(lengths)[1:]:
+            start_cosine = jnp.where(spot >= start, cosines[pl.ds(start, 1), :], start_cosine)
+            start_sine = jnp.where(spot >= start, sines[pl.ds(start, 1), :], start_sine)
+        lane = lax.broadcasted_iota(jnp.int32, (size, HEAD), 1)
+        cosine[rows, :] = cosines[rows, :] * start_cosine + sines[rows, :] * start_sine
+        turned = sines[rows, :] * start_cosine - cosines[rows, :] * start_sine
+        sine[rows, :] = jnp.where(lane < HEAD // 2, -turned, turned)
         value = resid[rows, :].astype(jnp.float32)
         scale = lax.rsqrt(jnp.mean(value * value, axis=1, keepdims=True) + EPSILON)
         value = value * scale * gain[...]
         high = value.astype(low)
         rest = (value - high.astype(jnp.float32)).astype(low)
         factor[rows, :] = scale
-        normed[rows, :] = high
         normed_t[:, rows] = high.T
-        logits[rows, :] = jnp.dot(
-            high, router[...], preferred_element_type=jnp.float32
-        ) + jnp.dot(rest, router[...], preferred_element_type=jnp.float32)
+        known = sum(
+            dot_nt(left, right)
+            for left, right in ((high, router_high), (high, router_rest), (rest, router_high))
+        )
+        logits[rows, :] = known
+        names = [marks[rows, ROUTES + way : ROUTES + way + 1] for way in range(2)]
+        pair = chosen_gates(known, names)
+        for way in range(2):
+            gates[rows, way : way + 1] = pair[way]
+        for number in range(held):
+            expert = place.tensor * held + number
+            gate_local[rows, number : number + 1] = sum(
+                jnp.where(name == expert, gate, 0.0) for name, gate in zip(names, pair)
+            )
         values[rows, :] = jnp.dot(
             high, w_value[...], preferred_element_type=jnp.float32
         ).astype(low)
@@ -1451,12 +1530,51 @@
                 part = flat[:, column]
                 turned = pltpu.roll(part, HEAD // 2, 1)
                 out[rows, column] = (part * cosine[rows, :] + turned * sine[rows, :]).astype(low)
-    for head in range(columns // HEAD):
-        column = slice(head * HEAD, (head + 1) * HEAD)
-        for first, size in bands(tokens):
-            last = first + size
-            rows = slice(first, last)
-            scores = masked_scores(query, keys, segment_column, segment_row, first, size, column)
+
+    def selection(expert):
+        number = lax.broadcasted_iota(jnp.int32, (capacity, tokens), 0) + expert * capacity
+        return ((mark_rows[0:1, :] == number) | (mark_rows[1:2, :] == number)).astype(low)
+
+    early = min(FRONT, groups)
+
+    keep = pltpu.make_async_copy(grads_slots.at[0], grads_out, load_sem.at[groups])
+
+    def take_grads():
+        own.wait()
+        bucket = grads_back.shape[1]
+        for step in range(1, groups):
+            deal_copy(step, flip(place.expert, step, groups)).wait_recv()
+        fetches = [
+            pltpu.make_async_copy(
+                grads_back.at[group], grads_here.at[pl.ds(group * bucket, bucket)], load_sem.at[group]
+            )
+            for group in range(groups)
+        ]
+        for fetch in fetches:
+            fetch.start()
+        for fetch in fetches:
+            fetch.wait()
+        for expert in range(sent_rows.shape[0]):
+            grads_slots[0, expert] = jnp.dot(
+                selection(expert), grads_here[...], preferred_element_type=jnp.float32
+            ).astype(low)
+        keep.start()
+        spread.start(min(AHEAD, early - 1))
+
+    def tick(number):
+        if number < early:
+            spread.first(jnp.int32(number))
+        if number + 1 + AHEAD < early:
+            spread.send(jnp.int32(number + 1 + AHEAD))
+        if 1 <= number <= early:
+            spread.second(jnp.int32(number - 1))
+
+    def attend_band(number, first, size):
+        last = first + size
+        rows = slice(first, last)
+        for head in range(columns // HEAD):
+            column = slice(head * HEAD, (head + 1) * HEAD)
+            scores = masked_scores(query, keys, lengths, first, size, column)
             top = jnp.max(scores, axis=1, keepdims=True)
             expo = jnp.exp(scores - top)
             total = jnp.sum(expo, axis=1, keepdims=True)
@@ -1465,37 +1583,164 @@
                 probs, values[:last, column], preferred_element_type=jnp.float32
             ).astype(low)
             log_total[rows, head : head + 1] = top + jnp.log(total)
-
-
-def attend(resid, gain, router, weights, cosine, sine, segment):
+        collect.free_stage(jnp.int32(number))
+        for spot in range(place.spots):
+            for core in range(2):
+                start = (spot * 2 + core) * width
+                total = None
+                for expert in range(held):
+                    inner = slice(expert * span, (expert + 1) * span)
+                    term = gate_local[rows, expert : expert + 1] * jnp.dot(
+                        heads[rows, inner],
+                        w_out[inner, start : start + width],
+                        preferred_element_type=jnp.float32,
+                    )
+                    total = term if total is None else total + term
+                collect.stage[number % collect.slots, 0, spot, core] = total.astype(low)
+        collect.first(jnp.int32(number))
+
+    blank = jnp.zeros((128 - router_two_t.shape[0], width), jnp.float32)
+    router_wide = jnp.concatenate([router_two_t[...], blank], axis=0)
+
+    def measure(number, first, size):
+        rows = slice(first, first + size)
+        value = resid[rows, columns_here].astype(jnp.float32) + collect.third(jnp.int32(number))[0]
+        hidden[rows, :] = value
+        squares = jnp.sum(value * value, axis=1, keepdims=True)
+        known = precise_dot(value * gain_two[...], router_wide, (1, 1))
+        lane = lax.broadcasted_iota(jnp.int32, known.shape, 1)
+        exchange.start(number, jnp.where(lane == SQUARES, squares, known))
+
+    def conclude(number, first, size):
+        rows = slice(first, first + size)
+        total = exchange.total(number, size)
+        scale = lax.rsqrt(total[:, SQUARES : SQUARES + 1] / (width * place.parts) + EPSILON)
+        known = total[:, : logits_two.shape[1]] * scale
+        factor_two[rows, :] = scale
+        logits_two[rows, :] = known
+        names = [marks[rows, ROUTES_TWO + way : ROUTES_TWO + way + 1] for way in range(2)]
+        pair = chosen_gates(known, names)
+        for way in range(2):
+            gates_two[rows, way : way + 1] = pair[way]
+        normed_two[rows, :] = (hidden[rows, :] * scale * gain_two[...]).astype(low)
+
+    count = len(parts)
+    for turn in range(count + 3):
+        if turn < count:
+            attend_band(turn, *parts[turn][1])
+        if 2 <= turn < count + 2:
+            measure(turn - 2, *parts[turn - 2][1])
+        if 1 <= turn < count + 1:
+            collect.second(jnp.int32(turn - 1))
+        if turn >= 3:
+            conclude(turn - 3, *parts[turn - 3][1])
+        if turn == count:
+            take_grads()
+        if turn > count:
+            tick(turn - count - 1)
+    for expert in range(sent_rows.shape[0]):
+        sent_rows[expert] = jnp.dot(
+            selection(expert), normed_two[...], preferred_element_type=jnp.float32
+        ).astype(low)
+        wide = lines.shape[2]
+        lane = lax.broadcasted_iota(jnp.int32, (tokens, wide), 1)
+        number = jnp.where(lane < capacity, lane + expert * capacity, -1)
+        line = sum(
+            jnp.where(
+                marks[:, SLOTS + way : SLOTS + way + 1] == number, gates_two[:, way : way + 1], 0.0
+            )
+            for way in range(2)
+        )
+        lines[expert] = jnp.broadcast_to(jnp.sum(line, axis=0, keepdims=True), lines.shape[1:])
+    for number in range(2, early + 1):
+        tick(number)
+    keep.wait()
+    for step in range(1, groups):
+        deal_copy(step, place.expert).wait_send()
+    for number in range(count):
+        exchange.finish(number)
+    collect.finish()
+
+    def last(number, carry):
+        spread.third(number)
+        spread.finish(number)
+        return carry
+
+    lax.fori_loop(0, early, last, 0)
+
+
+def front(
+    resid, gain, router_t, weights, w_out, tables, marks, mark_rows, gain_two, router_two_t,
+    lengths, dealt, capacity, sharers, collective,
+):
+    groups, parts = lax.axis_size("expert"), lax.axis_size("tensor")
     tokens, model_width = resid.shape
     columns = weights[0].shape[1]
+    width = dealt.shape[2]
+    experts_of = router_t.shape[0]
+    held = columns // (QH * HEAD)
+    slots_of = router_two_t.shape[0]
     low, full = jnp.bfloat16, jnp.float32
     block = jax.ShapeDtypeStruct((tokens, columns), low)
+    wide = (capacity + 127) // 128 * 128
     inside = pl.BlockSpec(memory_space=pltpu.VMEM)
+    anywhere = pl.BlockSpec(memory_space=pl.ANY)
+
+    def column(count):
+        return jax.ShapeDtypeStruct((tokens, count), full)
+
+    pieces = len(bands(tokens))
+    dma = pltpu.SemaphoreType.DMA
     return pl.pallas_call(
-        attend_kernel,
+        functools.partial(front_kernel, sharers),
         out_shape=(
-            jax.ShapeDtypeStruct((tokens, model_width), low),
             jax.ShapeDtypeStruct((model_width, tokens), low),
-            jax.ShapeDtypeStruct((tokens, 1), full),
-            jax.ShapeDtypeStruct((tokens, router.shape[1]), full),
+            column(HEAD),
+            column(HEAD),
+            column(1),
+            column(experts_of),
+            column(2),
+            column(held),
             block,
             block,
             block,
             block,
-            jax.ShapeDtypeStruct((tokens, columns // HEAD), full),
+            column(columns // HEAD),
+            column(width),
+            column(1),
+            column(slots_of),
+            column(2),
+            jax.ShapeDtypeStruct((slots_of, capacity, width), low),
+            jax.ShapeDtypeStruct((slots_of, 8, wide), full),
+            jax.ShapeDtypeStruct(dealt.shape, low),
+            jax.ShapeDtypeStruct((slots_of, capacity, width), low),
+            jax.ShapeDtypeStruct((1, groups, capacity, model_width), low),
         ),
-        in_specs=[inside] * 10,
-        out_specs=(inside,) * 9,
-        compiler_params=pltpu.CompilerParams(vmem_limit_bytes=56 * MIB),
-        cost_estimate=lasting(20),
-    )(resid, gain, router, *weights, cosine, sine, segment[:, None], segment[None, :])
+        in_specs=[inside] * 13 + [pl.BlockSpec(memory_space=pltpu.SMEM), anywhere],
+        out_specs=(inside,) * 18 + (anywhere,) * 3,
+        scratch_shapes=[
+            pltpu.VMEM((tokens, width), low),
+            pltpu.VMEM((tokens, width), low),
+            pltpu.VMEM((1, slots_of, capacity, width), low),
+            dma((groups,)),
+            dma((groups,)),
+            dma((groups + 1,)),
+        ]
+        + Spread.scratch(groups, parts // 2)
+        + Exchange.scratch(pieces, parts, tokens // pieces, 16)
+        + Collect.scratch(pieces, 1, parts // 2, tokens // pieces, width, pieces),
+        compiler_params=pltpu.CompilerParams(
+            collective_id=collective, has_side_effects=True, vmem_limit_bytes=58 * MIB
+        ),
+        cost_estimate=lasting(60),
+    )(
+        resid, gain, router_t, *weights, w_out, *tables, marks, mark_rows, gain_two, router_two_t,
+        lengths, dealt,
+    )
 
 
 def attend_back_kernel(
-    grads, w_out, gates, heads, query, keys, values, log_total, cosine, sine,
-    segment_column, segment_row,
+    grads, w_out, gates, heads, query, keys, values, log_total, cosine, sine, lengths,
     query_grad, key_grad, value_grad, gate_grad, gated_t,
     heads_grad, key_sum, value_sum,
 ):
@@ -1525,7 +1770,7 @@
         for first, size in bands(tokens):
             last = first + size
             rows = slice(first, last)
-            scores = masked_scores(query, keys, segment_column, segment_row, first, size, column)
+            scores = masked_scores(query, keys, lengths, first, size, column)
             probs = jnp.exp(scores - log_total[rows, head : head + 1])
             value_part = dot_tn(probs.astype(low), heads_grad[rows, column])
             prob_grad = dot_nt(heads_grad[rows, column], values[:last, column])
@@ -1548,7 +1793,7 @@
         value_grad[:, column] = value_sum[...].astype(low)
 
 
-def attend_back(grads, w_out, gates, heads, query, keys, values, log_total, cosine, sine, segment):
+def attend_back(grads, w_out, gates, heads, query, keys, values, log_total, cosine, sine, lengths):
     tokens, model_width = grads.shape
     columns = query.shape[1]
     low, full = jnp.bfloat16, jnp.float32
@@ -1563,7 +1808,7 @@
             jax.ShapeDtypeStruct(gates.shape, full),
             jax.ShapeDtypeStruct((columns, tokens), low),
         ),
-        in_specs=[inside] * 12,
+        in_specs=[inside] * 10 + [pl.BlockSpec(memory_space=pltpu.SMEM)],
         out_specs=(inside,) * 5,
         scratch_shapes=[
             pltpu.VMEM((tokens, columns), low),
@@ -1573,24 +1818,8 @@
         compiler_params=pltpu.CompilerParams(vmem_limit_bytes=56 * MIB),
         cost_estimate=lasting(25),
     )(
-        grads, w_out, gates, heads, query, keys, values, log_total, cosine, sine,
-        segment[:, None], segment[None, :],
-    )
-
-
-def to_expert(rows, group_count):
-    count, width = rows.shape
-    return lax.all_to_all(
-        rows.reshape(group_count, count // group_count, width),
-        "expert",
-        split_axis=0,
-        concat_axis=0,
-        tiled=True,
-    ).reshape(count, width)
-
-
-def gather_tensor(rows):
-    return lax.all_gather(rows, "tensor", axis=0)
+        grads, w_out, gates, heads, query, keys, values, log_total, cosine, sine, lengths
+    )
 
 
 def body(
@@ -1628,100 +1857,46 @@
 
     deal_rank = deal // tok_rows * bucket_rows + (deal % tok_rows - group_index * bucket_rows)
     row_ids = jnp.arange(tok_rows, dtype=jnp.int32)
-    deal_mask = (row_ids[:, None] == deal_rank[None, :]).astype(low)
-    dealt = jnp.dot(deal_mask, own_cols(tokens), preferred_element_type=jnp.float32).astype(low)
-    resid_low = spread_rows(dealt.reshape(group_count, bucket_rows, col_width), True, 0, 30)
-    dealt_grads = jnp.dot(
-        deal_mask, own_cols(out_grad), preferred_element_type=jnp.float32
-    ).astype(low)
-    dealt_grads, resid_low = lax.optimization_barrier((dealt_grads, resid_low))
-    grad_cols_low = to_expert(dealt_grads, group_count)
-    gain_one, gain_two = own_cols(attn_gain), own_cols(mlp_gain)
-    router_one = lax.dynamic_slice_in_dim(attn_router, col_first, col_width, 0)
-    router_two = lax.dynamic_slice_in_dim(mlp_router, col_first, col_width, 0)
     expert_count = mlp_router.shape[1]
+    experts_of = attn_router.shape[1]
     sharers = group_count // expert_count
     capacity = 5 * tok_rows // (2 * expert_count)
-    target, position, kept = slot_table(mlp_routes, slot_order[0], capacity)
     slots = expert_count * capacity
-    destination = jnp.where(kept, target * capacity + position, slots).reshape(tok_rows, 2)
-    slot_ids = jnp.arange(slots, dtype=jnp.int32)
-    chosen = [destination[:, way] for way in range(2)]
-    to_slot = (
-        (slot_ids[:, None] == chosen[0][None, :]) | (slot_ids[:, None] == chosen[1][None, :])
-    ).astype(low)
-    resid_cols = own_cols(resid_low).astype(jnp.float32)
-    segment, cosine, sine = rotary_tables(seq_lengths[0], tok_rows)
-    sign = jnp.where(jnp.arange(HEAD) < HEAD // 2, -1.0, 1.0)
-    local_heads = w_query.shape[1] // HEAD
-    local_experts = local_heads // QH
-    span = QH * HEAD
-    experts_of = attn_router.shape[1]
-    router_high = lax.reduce_precision(attn_router, 8, 7)
-    router_parts = jnp.concatenate([router_high, attn_router - router_high], axis=1).astype(low)
-    router_parts = jnp.pad(router_parts, ((0, 0), (0, -router_parts.shape[1] % 128)))
-    normed_low, normed_t, factor_one, logit_parts, query, keys, values, heads_low, log_total = (
-        attend(
-            resid_low,
-            attn_gain[None],
-            router_parts,
-            (w_query, w_key, w_value),
-            cosine,
-            sine * sign,
-            segment,
-        )
-    )
-    attn_logits = logit_parts[:, :experts_of] + logit_parts[:, experts_of : 2 * experts_of]
-    attn_gates, attn_mask = pair_gates(attn_logits, attn_routes)
-    gate_table = jnp.sum(attn_gates[:, :, None] * attn_mask, axis=1)
-    gate_local = lax.dynamic_slice_in_dim(gate_table, part_index * local_experts, local_experts, 1)
-    grad_cols_low, heads_low = lax.optimization_barrier((grad_cols_low, heads_low))
-    slot_grads = jnp.dot(to_slot, grad_cols_low, preferred_element_type=jnp.float32).astype(low)
-    slot_grads = jnp.repeat(slot_grads.reshape(expert_count, capacity, col_width), sharers, axis=0)
-    slot_grads = to_expert(slot_grads.reshape(group_count * capacity, col_width), group_count)
-    pieces, piece_rows = 4, tok_rows // 4
-    attn_cols = collect_rows(
-        functools.partial(make_attended, span),
-        (
-            heads_low.reshape(pieces, piece_rows, local_heads * HEAD),
-            gate_local.reshape(pieces, piece_rows, local_experts),
-            w_out,
-        ),
-        pieces,
-        piece_rows,
-        col_width,
+    pieces = 4
+    orders = slot_order[0].reshape(tok_rows, 2)
+    rows_in = jnp.concatenate([attn_routes.T, mlp_routes.T, orders.T, orders.T], axis=0)
+    resid_low, dealt_grads, marks, mark_rows = deal_rows(
+        tokens, out_grad, deal_rank[None], rows_in, capacity, expert_count, 0
+    )
+    resid_low = resid_low.reshape(tok_rows, model_width)
+    gain_one, gain_two = own_cols(attn_gain), own_cols(mlp_gain)
+    router_one, router_two = own_cols(attn_router.T), own_cols(mlp_router.T)
+    (
+        normed_t, cosine, sine, factor_one, attn_logits, attn_gates, gate_local, query, keys, values,
+        heads_low, log_total, hidden, factor_two, mlp_logits, mlp_gates, slot_rows, gate_lines,
+        grad_cols_low, slot_grads, early_grads,
+    ) = front(
+        resid_low,
+        attn_gain[None],
+        attn_router.T,
+        (w_query, w_key, w_value),
+        w_out,
+        rotary_tables(tok_rows),
+        marks,
+        mark_rows,
+        gain_two[None],
+        router_two,
+        seq_lengths,
+        dealt_grads,
+        capacity,
+        sharers,
         1,
     )
-    hidden = resid_cols + attn_cols
-    weighed = hidden * gain_two
-    stats = jnp.concatenate(
-        [
-            jnp.sum(hidden * hidden, axis=1)[None, :],
-            jnp.dot(weighed, router_two, precision=PRECISE).T,
-        ],
-        axis=0,
-    )
-    stats = jnp.sum(gather_tensor(stats), axis=0)
-    factor_two = lax.rsqrt(stats[0] / model_width + EPSILON)[:, None]
-    mlp_logits = stats[1:].T * factor_two
-    scaled_two = hidden * factor_two
-    normed_two = scaled_two * gain_two
-    mlp_gates, _ = pair_gates(mlp_logits, mlp_routes)
-    slot_rows = jnp.dot(
-        to_slot, normed_two.astype(low), preferred_element_type=jnp.float32
-    ).astype(low)
-    slot_gates = sum(
-        jnp.sum(
-            jnp.where(slot_ids[:, None] == chosen[way][None, :], mlp_gates[:, way][None, :], 0.0),
-            axis=1,
-        )
-        for way in range(2)
-    )
-    gate_lines = jnp.pad(slot_gates.reshape(expert_count, capacity), ((0, 0), (0, -capacity % 128)))
-    gate_lines = jnp.broadcast_to(gate_lines[:, None, :], (expert_count, 8, gate_lines.shape[1]))
+    grad_cols_low = grad_cols_low.reshape(tok_rows, col_width)
     inbox, _, slot_grads, middle, gate_grad, up_grad, returned = experts(
-        slot_rows.reshape(expert_count, capacity, col_width),
-        slot_grads.reshape(group_count, capacity, col_width),
+        slot_rows,
+        slot_grads,
+        early_grads,
         gate_lines,
         w_gate[0],
         w_up[0],
@@ -1738,14 +1913,14 @@
         ).astype(low)
     back_mixed, hidden_grad, hidden_grad_low, mlp_router_grad, mlp_gain_grad = settle(
         returned.reshape(2, slots, col_width),
-        jnp.concatenate([destination, mlp_routes], axis=1),
+        marks,
         mlp_gates,
         mlp_logits,
         factor_two,
         hidden,
         grad_cols_low,
         gain_two[None],
-        router_two.T,
+        router_two,
         pieces,
         4,
     )
@@ -1761,8 +1936,8 @@
         values,
         log_total,
         cosine,
-        sine * sign,
-        segment,
+        sine,
+        seq_lengths,
     )
     rows = inbox.reshape(-1, model_width)
     units = middle.shape[2]
@@ -1776,10 +1951,10 @@
             gain_one[None],
             factor_one,
             attn_gates,
-            attn_routes,
+            marks,
             attn_logits,
             local_gate_grad,
-            router_one.T,
+            router_one,
             mlp_gain_grad,
             mlp_router_grad,
         ),
@@ -1787,7 +1962,7 @@
         gated_t,
         hidden_grad_low,
         hidden_grad,
-        own_cols(resid_low),
+        resid_low,
         (w_query, w_key, w_value),
         (rows, rows, middle),
         (gate_grad, up_grad, slot_grads.reshape(-1, model_width)),
@@ -1796,6 +1971,7 @@
     )
     back_grad = back_grad.reshape(tok_rows, col_width)
     weight_grads = [grad.astype(jnp.float32) for grad in weight_grads]
+    deal_mask = (row_ids[:, None] == deal_rank[None, :]).astype(low)
     mixed, tokens_grad = (
         jnp.einsum("ri,rc->ic", deal_mask, back, preferred_element_type=jnp.float32).astype(low)
         for back in (back_mixed, back_grad)

time: 642 us -> 628 us (0.978)
  Pallas kernels: 538 us -> 568 us
  starting transfers between devices: 14.1 us -> 0 us
  other arithmetic: 41.5 us -> 29.8 us
  matrix products: 16.2 us -> 4.7 us
    pallas_call x3 -> x2, Pallas kernels: 80.9 us -> 105 us  [the longest x1 72.9 us: front(): pl.pallas_call(functools.partial(front_kernel, sharers), out_shape=(jax.S...]
    all_to_all x2 -> x0, starting transfers between devices: 14.1 us -> none  [to_expert(): lax.all_to_all(rows.reshape(group_count, count // group_count, width), 'e...]
    dot_general x5 -> x0, matrix products: 12.8 us -> none  [the longest x1 4.58 us: body(): jnp.dot(to_slot, normed_two.astype(low), preferred_element_type=jnp.float32)]
    pallas_call x1, Pallas kernels: 205 us -> 212 us  [experts(): pl.pallas_call(functools.partial(experts_kernel, sharers), out_shape=(jax...]
  transfers between devices with their start and end apart: 2 -> 0, of which waited for: 0 -> 0; matrix products, arithmetic and copies ran while one was open for 4% -> 0% of each run, Pallas kernels for 8% -> 0%
where the time goes in v6:
time: 628 us; the launch traced here: 622 us
  Pallas kernels  568 us (90%)
  other arithmetic  29.8 us (5%)
  local copies, waits for them, and re-layouts  18.8 us (3%)
    pallas_call x1, Pallas kernels, experts(): pl.pallas_call(functools.partial(experts_kernel, sharers), out_shape=(jax...  212 us
    pallas_call x1, Pallas kernels, closing(): pl.pallas_call(functools.partial(closing_kernel, tuple(jobs)), out_shape=...  204 us
    pallas_call x1, Pallas kernels, front(): pl.pallas_call(functools.partial(front_kernel, sharers), out_shape=(jax.S...  72.9 us
    pallas_call x1, Pallas kernels, settle(): pl.pallas_call(settle_kernel, out_shape=(jax.ShapeDtypeStruct((groups, to...  31.7 us
    pallas_call x1, Pallas kernels, deal_rows(): pl.pallas_call(functools.partial(deal_kernel, capacity, experts_of), out_...  31.6 us
    pallas_call x1, Pallas kernels, attend_back(): pl.pallas_call(attend_back_kernel, out_shape=(block, block, block, jax.Sh...  15.7 us

profile of v6, /device:TPU:20, one launch (start us, length us, event | category | flops | bytes accessed | tf_op | source)
XLA Modules:
  0.0 622.5 jit_solution(4955451232992995968)
XLA Ops:
  0.7 1.3 dynamic_slice.12
  2.0 1.3 dynamic_slice.14
  3.3 0.7 fusion.7
  4.0 0.7 reduce
  4.8 1.4 dynamic-slice_bitcast_fusion
  6.1 0.3 reshape_squeeze.3
  6.5 0.1 copy.33
  6.6 0.7 pad_add_fusion.rows_in
  7.3 0.0 copy-start.3
  7.4 1.9 copy-done.3
  9.2 1.9 copy-done.4
  11.1 31.6 %shard_map.291 = (bf16[1,8,96,2048]{3,2,1,0:T(8,128)(2,1)S(1)}, bf16[8,96,512]{2,1,0:T(8,128)(2,1)S(1)}, s32[768,8]{1,0:T(8,128)S(1)}, s32[8,768]{1,0:T(8,128)S(1)}) custom-call(bf16[768,2048]{1,0:T(8,128)(2,1)S(1)} %copy-done.3, bf16[768,2048]{1,0:T(8,128)(2,1)S(1)} %copy-done.4, s32[1,768]{1,0:T(1,128)S(1)} %broadcast_in_dim.24.ranks, ...), custom_call_target="tpu_custom_call" | custom-call | bytes 105000000 | tf_op jit(solution)/shard_map/pallas_call | solution.py:450
  42.8 0.0 copy-start
  42.8 1.7 copy-done
  44.4 0.7 copy-done.1
  45.2 0.9 copy-done.7
  46.1 0.6 copy-done.12
  46.7 72.9 %shard_map.292 = (bf16[2048,768]{1,0:T(8,128)(2,1)}, f32[768,128]{1,0:T(8,128)}, f32[768,128]{1,0:T(8,128)}, f32[768,1]{1,0:T(8,128)}, f32[768,8]{1,0:T(8,128)},...) custom-call(bf16[768,2048]{1,0:T(8,128)(2,1)} %bitcast.47, ...), custom_call_target="tpu_custom_call" | custom-call | bytes 180000000 | tf_op jit(solution)/shard_map/pallas_call | solution.py:1694
  119.6 0.0 copy-start.2
  119.6 0.0 copy-start.6
  119.6 0.0 copy-start.8
  119.6 0.0 copy-start.9
  119.6 0.0 copy-start.10
  119.6 0.0 copy-start.11
  119.6 0.0 copy-start.13
  119.6 212.4 %shard_map.293 = (bf16[1,8,240,2048]{3,2,1,0:T(8,128)(2,1)}, bf16[1,8,240,2048]{3,2,1,0:T(8,128)(2,1)}, bf16[8,240,2048]{2,1,0:T(8,128)(2,1)}, bf16[8,240,1408]{...) custom-call(bf16[1,8,240,512]{3,2,1,0:T(8,128)(2,1)} %bitcast.71, ...), custom_call_target="tpu_custom_call" | custom-call | bytes 540000000 | tf_op jit(solution)/shard_map/pallas_call | solution.py:694
  332.1 0.0 copy-done.2
  332.2 31.7 %shard_map.294 = (bf16[8,96,512]{2,1,0:T(8,128)(2,1)S(1)}, f32[768,512]{1,0:T(8,128)S(1)}, bf16[1,4,192,2048]{3,2,1,0:T(8,128)(2,1)}, f32[8,512]{1,0:T(8,128)S(1)}, f32[1,512]{1,0:T(1,128)S(1)}) custom-call(bf16[2,1920,512]{2,1,0:T(8,128)(2,1)} %bitcast.70, s32[768,8]{1,0:T(8,128)S(1)} %copy-done.2, f32[768,2]{1,0:T(8,128)S(1)} %copy-done.10, ...), custom_call_target="tpu_custom_call" | custom-call | bytes 90000000 | tf_op jit(solution)/shard_map/pallas_call | solution.py:1381
  363.9 0.0 copy-start.5
  363.9 1.1 copy-done.5
  365.0 0.6 copy-done.14
  365.6 0.6 copy-done.15
  366.2 15.7 %shard_map.295 = (bf16[768,512]{1,0:T(8,128)(2,1)}, bf16[768,512]{1,0:T(8,128)(2,1)}, bf16[768,512]{1,0:T(8,128)(2,1)}, f32[768,2]{1,0:T(8,128)}, bf16[512,768]{1,0:T(8,128)(2,1)}) custom-call(bf16[768,2048]{1,0:T(8,128)(2,1)} %bitcast.55, bf16[512,2048]{1,0:T(8,128)(2,1)} %w_out.1, f32[768,2]{1,0:T(8,128)} %get-tuple-element.83.gates, ...), custom_call_target="tpu_custom_call" | custom-call | bytes 75000000 | tf_op jit(solution)/shard_map/pallas_call | solution.py:1802
  381.9 1.7 fusion.2
  383.6 203.8 %shard_map.296 = (bf16[2048,512]{1,0:T(8,128)(2,1)}, bf16[2048,512]{1,0:T(8,128)(2,1)}, bf16[2048,512]{1,0:T(8,128)(2,1)}, bf16[512,2048]{1,0:T(8,128)(2,1)}, bf...) custom-call(bf16[2048,768]{1,0:T(8,128)(2,1)} %get-tuple-element.78., ...), custom_call_target="tpu_custom_call" | custom-call | bytes 600000000 | tf_op jit(solution)/shard_map/pallas_call | solution.py:1242
  587.4 3.0 fusion.3
  590.3 1.6 fusion.11
  592.0 1.6 fusion.10
  593.6 2.6 convert_element_type.39
  596.2 2.7 convert_element_type.40
  599.0 2.7 convert_element_type.41
  601.7 1.0 copy-done.16
  602.7 2.7 convert_element_type.42
  605.4 0.0 slice-start
  605.4 5.7 bitcast_convert_fusion.2
  611.1 5.2 bitcast_convert_fusion.1
  616.3 0.0 slice-done.1
  616.3 6.0 bitcast_convert_fusion
  (33 shorter events, 0.1 us)
Async XLA Ops:
  7.3 1.9 copy-start.3
  9.2 1.9 copy-start.4
  42.8 1.7 copy-start
  44.4 0.7 copy-start.1
  45.2 0.9 copy-start.7
  46.1 0.6 copy-start.12
  119.6 212.5 %copy-start.2 = (s32[768,8]{1,0:T(8,128)S(1)}, s32[768,8]{1,0:T(8,128)}, u32[]{:S(2)}) copy-start(s32[768,8]{1,0:T(8,128)} %copy-done.1) | copy-start | bytes 73732
  119.6 212.5 %copy-start.6 = (bf16[8,96,512]{2,1,0:T(8,128)(2,1)S(1)}, bf16[8,96,512]{2,1,0:T(8,128)(2,1)}, u32[]{:S(2)}) copy-start(bf16[8,96,512]{2,1,0:T(8,128)(2,1)} %get-tuple-element.76) | copy-start | bytes 2359300
  119.6 212.5 %copy-start.8 = (f32[768,1]{1,0:T(8,128)S(1)}, f32[768,1]{1,0:T(8,128)}, u32[]{:S(2)}) copy-start(f32[768,1]{1,0:T(8,128)} %get-tuple-element.74.factor) | copy-start | bytes 9220
  119.6 212.5 %copy-start.9 = (f32[768,8]{1,0:T(8,128)S(1)}, f32[768,8]{1,0:T(8,128)}, u32[]{:S(2)}) copy-start(f32[768,8]{1,0:T(8,128)} %get-tuple-element.73.logits) | copy-start | bytes 73732
  119.6 212.5 %copy-start.10 = (f32[768,2]{1,0:T(8,128)S(1)}, f32[768,2]{1,0:T(8,128)}, u32[]{:S(2)}) copy-start(f32[768,2]{1,0:T(8,128)} %get-tuple-element.72.gates) | copy-start | bytes 18436
  119.6 212.5 %copy-start.11 = (f32[8,512]{1,0:T(8,128)S(1)}, f32[8,512]{1,0:T(8,128)}, u32[]{:S(2)}) copy-start(f32[8,512]{1,0:T(8,128)} %get-tuple-element.118.refs_12_.router_t) | copy-start | bytes 49156
  119.6 212.5 %copy-start.13 = (f32[512]{0:T(512)S(1)}, f32[512]{0:T(512)}, u32[]{:S(2)}) copy-start(f32[512]{0:T(512)} %dynamic_slice.12) | copy-start | bytes 6148
  363.9 1.1 copy-start.5
  365.0 0.6 copy-start.14
  365.6 0.6 copy-start.15
  587.3 6.3 %copy-start.19 = (bf16[2048,512]{1,0:T(8,128)(2,1)S(1)}, bf16[2048,512]{1,0:T(8,128)(2,1)}, u32[]{:S(2)}) copy-start(bf16[2048,512]{1,0:T(8,128)(2,1)} %get-tuple-element.106) | copy-start | bytes 6291460
  590.3 5.9 copy-start.18
  596.2 2.7 copy-start.17
  596.2 9.1 %slice-start.4 = ((s8[5767168]{0:T(1024)(128)(4,1)}), s8[4194304]{0:T(1024)(128)(4,1)S(1)}, s32[]{:S(2)}) async-start(s8[5767168]{0:T(1024)(128)(4,1)} %bitcast.65), calls=%async_computation.4 | async-start | bytes 8388608
  599.0 3.7 copy-start.16
  599.0 6.4 %slice-start.5 = ((s8[5767168]{0:T(1024)(128)(4,1)}), s8[1572864]{0:T(1024)(128)(4,1)S(1)}, s32[]{:S(2)}) async-start(s8[5767168]{0:T(1024)(128)(4,1)} %bitcast.65), calls=%async_computation.5 | async-start | bytes 3145728
  602.7 8.4 %slice-start.2 = ((s8[5767168]{0:T(1024)(128)(4,1)}), s8[4194304]{0:T(1024)(128)(4,1)S(1)}, s32[]{:S(2)}) async-start(s8[5767168]{0:T(1024)(128)(4,1)} %bitcast.63), calls=%async_computation.2 | async-start | bytes 8388608
  605.4 5.7 slice-start.3
  605.4 10.9 %slice-start = ((s8[5767168]{0:T(1024)(128)(4,1)}), s8[4194304]{0:T(1024)(128)(4,1)S(1)}, s32[]{:S(2)}) async-start(s8[5767168]{0:T(1024)(128)(4,1)} %bitcast.61), calls=%async_computation | async-start | bytes 8388608
  611.1 5.2 slice-start.1

commit v7 on v6

--- a/solution.py
+++ b/solution.py
@@ -858,8 +858,8 @@
 
 def closing_kernel(jobs, *refs):
     (
-        normed_t, gain, factor, gates, marks, logits, gate_grads, router_t, gain_two, router_two,
-        query_grad, key_grad, value_grad, gated_t, hidden_grads,
+        normed_hbm, gain, factor, gates, marks, logits, gate_grads, router_t, gain_two, router_two,
+        query_grad, key_grad, value_grad, gated_t, grads_hbm,
         hidden_hbm, resid_hbm, query_hbm, key_hbm, value_hbm,
     ), refs = refs[:20], refs[20:]
     grads = (query_grad, key_grad, value_grad)
@@ -870,13 +870,19 @@
         hold, hold_out, partial, small_own, small_got, small_sum,
         hidden, resid, w_query, w_key, w_value, right, left, product,
         ring_send, ring_land, small_send, small_land, last_send, last_land,
-        own_sem, load_sem, job_sem,
-    ) = refs[:23]
+        own_sem, load_sem, job_sem, normed_t, hidden_grads, first_sem,
+    ) = refs[:26]
     weights = (w_query, w_key, w_value)
     place = Place()
-    exchange, of_gates = Exchange(place, refs[23:27]), Exchange(place, refs[27:31])
-    giving = Return(place, back, refs[31:35])
-    collect = Collect(place, refs[35:])
+    exchange, of_gates = Exchange(place, refs[26:30]), Exchange(place, refs[30:34])
+    giving = Return(place, back, refs[34:38])
+    collect = Collect(place, refs[38:])
+    first_loads = [
+        pltpu.make_async_copy(normed_hbm, normed_t, first_sem.at[0]),
+        pltpu.make_async_copy(grads_hbm, hidden_grads, first_sem.at[1]),
+    ]
+    for load in first_loads:
+        load.start()
     groups, parts = place.groups, place.parts
     pieces, rows = collect.core_in.shape[0], collect.core_in.shape[3]
     width = hidden.shape[1]
@@ -1098,6 +1104,8 @@
             last_copy(step, place.tensor).start()
 
     small_own[...] = jnp.zeros_like(small_own)
+    for load in first_loads:
+        load.wait()
     turns = max(2 * groups - 1, pieces + 5)
     tiles = sum(job[0] for job in jobs)
     each_turn = -(-tiles // turns)
@@ -1251,7 +1259,7 @@
                 for left, right in zip(lefts, rights)
             ),
         ),
-        in_specs=[inside] * 15 + [anywhere] * 11,
+        in_specs=[anywhere] + [inside] * 13 + [anywhere] * 12,
         out_specs=(anywhere,) * 9,
         scratch_shapes=[
             pltpu.VMEM((groups, 2, count, block, columns), low),
@@ -1275,6 +1283,9 @@
             dma((2, count + 2)),
             dma((5,)),
             dma((5,)),
+            pltpu.VMEM(normed_t.shape, low),
+            pltpu.VMEM(hidden_grads.shape, low),
+            dma((2,)),
         ]
         + Exchange.scratch(pieces, parts, rows, 8)
         + Exchange.scratch(pieces, parts, rows, (columns_in[4].shape[1] + 7) // 8 * 8)
@@ -1445,15 +1456,23 @@
 
 def front_kernel(sharers, *refs):
     (
-        resid, gain, router_t, w_query, w_key, w_value, w_out, cosines, sines,
+        resid, gain, router_t, query_hbm, key_hbm, value_hbm, out_hbm, cosines, sines,
         marks, mark_rows, gain_two, router_two_t, lengths, dealt,
         normed_t, cosine, sine, factor, logits, gates, gate_local, query, keys, values, heads, log_total,
         hidden, factor_two, logits_two, gates_two, sent_rows, lines,
         grads_back, grads_out, inbox_grads,
-        normed_two, grads_here, grads_slots,
-        deal_send, deal_land, load_sem,
-    ), refs = refs[:42], refs[42:]
+        normed_two, grads_here, grads_slots, w_query, w_key, w_value, w_out,
+        deal_send, deal_land, load_sem, weight_sem,
+    ), refs = refs[:47], refs[47:]
     place = Place()
+    weight_loads = [
+        pltpu.make_async_copy(source, kept, weight_sem.at[number])
+        for number, (source, kept) in enumerate(
+            ((query_hbm, w_query), (key_hbm, w_key), (value_hbm, w_value), (out_hbm, w_out))
+        )
+    ]
+    for load in weight_loads:
+        load.start()
     spread = Spread(place, grads_slots, inbox_grads, refs[:6], True, sharers)
     exchange = Exchange(place, refs[6:10])
     collect = Collect(place, refs[10:])
@@ -1484,6 +1503,8 @@
         dealt.at[place.expert], grads_back.at[place.expert], deal_send.at[0]
     )
     own.start()
+    for load in weight_loads:
+        load.wait()
     router_high = router_t[...].astype(low)
     router_rest = (router_t[...] - router_high.astype(jnp.float32)).astype(low)
     columns_here = pl.ds(pl.multiple_of(place.tensor * width, 128), width)
@@ -1716,15 +1737,20 @@
             jax.ShapeDtypeStruct((slots_of, capacity, width), low),
             jax.ShapeDtypeStruct((1, groups, capacity, model_width), low),
         ),
-        in_specs=[inside] * 13 + [pl.BlockSpec(memory_space=pltpu.SMEM), anywhere],
+        in_specs=[inside] * 3
+        + [anywhere] * 4
+        + [inside] * 6
+        + [pl.BlockSpec(memory_space=pltpu.SMEM), anywhere],
         out_specs=(inside,) * 18 + (anywhere,) * 3,
         scratch_shapes=[
             pltpu.VMEM((tokens, width), low),
             pltpu.VMEM((tokens, width), low),
             pltpu.VMEM((1, slots_of, capacity, width), low),
+            *(pltpu.VMEM(weight.shape, low) for weight in (*weights, w_out)),
             dma((groups,)),
             dma((groups,)),
             dma((groups + 1,)),
+            dma((4,)),
         ]
         + Spread.scratch(groups, parts // 2)
         + Exchange.scratch(pieces, parts, tokens // pieces, 16)

time: 628 us -> 627 us (level)
  no operation moved by 1% of the time
where the time goes in v7:
time: 627 us; the launch traced here: 622 us
  Pallas kernels  567 us (90%)
  other arithmetic  29.8 us (5%)
  local copies, waits for them, and re-layouts  18.8 us (3%)
    pallas_call x1, Pallas kernels, experts(): pl.pallas_call(functools.partial(experts_kernel, sharers), out_shape=(jax...  212 us
    pallas_call x1, Pallas kernels, closing(): pl.pallas_call(functools.partial(closing_kernel, tuple(jobs)), out_shape=...  205 us
    pallas_call x1, Pallas kernels, front(): pl.pallas_call(functools.partial(front_kernel, sharers), out_shape=(jax.S...  70.6 us
    pallas_call x1, Pallas kernels, settle(): pl.pallas_call(settle_kernel, out_shape=(jax.ShapeDtypeStruct((groups, to...  31.7 us
    pallas_call x1, Pallas kernels, deal_rows(): pl.pallas_call(functools.partial(deal_kernel, capacity, experts_of), out_...  31.6 us
    pallas_call x1, Pallas kernels, attend_back(): pl.pallas_call(attend_back_kernel, out_shape=(block, block, block, jax.Sh...  15.7 us

profile of v7, /device:TPU:20, one launch (start us, length us, event | category | flops | bytes accessed | tf_op | source)
XLA Modules:
  0.0 621.8 jit_solution(10964910100037497291)
XLA Ops:
  0.7 1.3 dynamic_slice.12
  2.0 1.3 dynamic_slice.14
  3.3 0.7 fusion.7
  4.0 0.7 reduce
  4.8 1.4 dynamic-slice_bitcast_fusion
  6.1 0.3 reshape_squeeze.3
  6.5 0.1 copy.33
  6.6 0.7 pad_add_fusion.rows_in
  7.3 0.0 copy-start.3
  7.4 1.9 copy-done.3
  9.2 1.9 copy-done.4
  11.1 31.6 %shard_map.291 = (bf16[1,8,96,2048]{3,2,1,0:T(8,128)(2,1)S(1)}, bf16[8,96,512]{2,1,0:T(8,128)(2,1)S(1)}, s32[768,8]{1,0:T(8,128)S(1)}, s32[8,768]{1,0:T(8,128)S(1)}) custom-call(bf16[768,2048]{1,0:T(8,128)(2,1)S(1)} %copy-done.3, bf16[768,2048]{1,0:T(8,128)(2,1)S(1)} %copy-done.4, s32[1,768]{1,0:T(1,128)S(1)} %broadcast_in_dim.24.ranks, ...), custom_call_target="tpu_custom_call" | custom-call | bytes 105000000 | tf_op jit(solution)/shard_map/pallas_call | solution.py:450
  42.8 0.0 copy-start
  42.8 1.7 copy-done
  44.4 0.7 copy-done.1
  45.2 0.9 copy-done.7
  46.1 0.6 copy-done.12
  46.7 70.6 %shard_map.292 = (bf16[2048,768]{1,0:T(8,128)(2,1)}, f32[768,128]{1,0:T(8,128)}, f32[768,128]{1,0:T(8,128)}, f32[768,1]{1,0:T(8,128)}, f32[768,8]{1,0:T(8,128)},...) custom-call(bf16[768,2048]{1,0:T(8,128)(2,1)} %bitcast.47, ...), custom_call_target="tpu_custom_call" | custom-call | bytes 180000000 | tf_op jit(solution)/shard_map/pallas_call | solution.py:1715
  117.3 0.0 copy-start.2
  117.3 0.0 copy-start.6
  117.3 0.0 copy-start.8
  117.3 0.0 copy-start.9
  117.3 0.0 copy-start.10
  117.4 0.0 copy-start.11
  117.4 0.0 copy-start.13
  117.4 212.3 %shard_map.293 = (bf16[1,8,240,2048]{3,2,1,0:T(8,128)(2,1)}, bf16[1,8,240,2048]{3,2,1,0:T(8,128)(2,1)}, bf16[8,240,2048]{2,1,0:T(8,128)(2,1)}, bf16[8,240,1408]{...) custom-call(bf16[1,8,240,512]{3,2,1,0:T(8,128)(2,1)} %bitcast.71, ...), custom_call_target="tpu_custom_call" | custom-call | bytes 540000000 | tf_op jit(solution)/shard_map/pallas_call | solution.py:694
  329.8 31.7 %shard_map.294 = (bf16[8,96,512]{2,1,0:T(8,128)(2,1)S(1)}, f32[768,512]{1,0:T(8,128)S(1)}, bf16[1,4,192,2048]{3,2,1,0:T(8,128)(2,1)}, f32[8,512]{1,0:T(8,128)S(1)}, f32[1,512]{1,0:T(1,128)S(1)}) custom-call(bf16[2,1920,512]{2,1,0:T(8,128)(2,1)} %bitcast.70, s32[768,8]{1,0:T(8,128)S(1)} %copy-done.2, f32[768,2]{1,0:T(8,128)S(1)} %copy-done.10, ...), custom_call_target="tpu_custom_call" | custom-call | bytes 90000000 | tf_op jit(solution)/shard_map/pallas_call | solution.py:1392
  361.5 0.0 copy-start.5
  361.5 1.1 copy-done.5
  362.6 0.6 copy-done.14
  363.2 0.6 copy-done.15
  363.8 15.7 %shard_map.295 = (bf16[768,512]{1,0:T(8,128)(2,1)}, bf16[768,512]{1,0:T(8,128)(2,1)}, bf16[768,512]{1,0:T(8,128)(2,1)}, f32[768,2]{1,0:T(8,128)}, bf16[512,768]{1,0:T(8,128)(2,1)}) custom-call(bf16[768,2048]{1,0:T(8,128)(2,1)} %bitcast.55, bf16[512,2048]{1,0:T(8,128)(2,1)} %w_out.1, f32[768,2]{1,0:T(8,128)} %get-tuple-element.83.gates, ...), custom_call_target="tpu_custom_call" | custom-call | bytes 75000000 | tf_op jit(solution)/shard_map/pallas_call | solution.py:1828
  379.5 1.7 fusion.2
  381.2 205.4 %shard_map.296 = (bf16[2048,512]{1,0:T(8,128)(2,1)}, bf16[2048,512]{1,0:T(8,128)(2,1)}, bf16[2048,512]{1,0:T(8,128)(2,1)}, bf16[512,2048]{1,0:T(8,128)(2,1)}, bf...) custom-call(bf16[2048,768]{1,0:T(8,128)(2,1)} %get-tuple-element.78., ...), custom_call_target="tpu_custom_call" | custom-call | bytes 600000000 | tf_op jit(solution)/shard_map/pallas_call | solution.py:1250
  586.6 3.0 fusion.3
  589.6 1.6 fusion.11
  591.3 1.6 fusion.10
  592.9 2.6 convert_element_type.39
  595.5 2.7 convert_element_type.40
  598.3 0.0 copy-done.17
  598.3 2.7 convert_element_type.41
  601.0 1.0 copy-done.16
  602.0 2.7 convert_element_type.42
  604.7 0.0 slice-start
  604.7 5.7 bitcast_convert_fusion.2
  610.4 0.0 slice-done.3
  610.4 5.2 bitcast_convert_fusion.1
  615.6 6.0 bitcast_convert_fusion
  (33 shorter events, 0.1 us)
Async XLA Ops:
  7.3 1.9 copy-start.3
  9.2 1.9 copy-start.4
  42.8 1.7 copy-start
  44.4 0.7 copy-start.1
  45.2 0.9 copy-start.7
  46.1 0.6 copy-start.12
  117.3 212.4 %copy-start.2 = (s32[768,8]{1,0:T(8,128)S(1)}, s32[768,8]{1,0:T(8,128)}, u32[]{:S(2)}) copy-start(s32[768,8]{1,0:T(8,128)} %copy-done.1) | copy-start | bytes 73732
  117.3 212.4 %copy-start.6 = (bf16[8,96,512]{2,1,0:T(8,128)(2,1)S(1)}, bf16[8,96,512]{2,1,0:T(8,128)(2,1)}, u32[]{:S(2)}) copy-start(bf16[8,96,512]{2,1,0:T(8,128)(2,1)} %get-tuple-element.76) | copy-start | bytes 2359300
  117.3 212.4 %copy-start.8 = (f32[768,1]{1,0:T(8,128)S(1)}, f32[768,1]{1,0:T(8,128)}, u32[]{:S(2)}) copy-start(f32[768,1]{1,0:T(8,128)} %get-tuple-element.74.factor) | copy-start | bytes 9220
  117.3 212.4 %copy-start.9 = (f32[768,8]{1,0:T(8,128)S(1)}, f32[768,8]{1,0:T(8,128)}, u32[]{:S(2)}) copy-start(f32[768,8]{1,0:T(8,128)} %get-tuple-element.73.logits) | copy-start | bytes 73732
  117.3 212.4 %copy-start.10 = (f32[768,2]{1,0:T(8,128)S(1)}, f32[768,2]{1,0:T(8,128)}, u32[]{:S(2)}) copy-start(f32[768,2]{1,0:T(8,128)} %get-tuple-element.72.gates) | copy-start | bytes 18436
  117.4 212.4 %copy-start.11 = (f32[8,512]{1,0:T(8,128)S(1)}, f32[8,512]{1,0:T(8,128)}, u32[]{:S(2)}) copy-start(f32[8,512]{1,0:T(8,128)} %get-tuple-element.118.refs_12_.router_t) | copy-start | bytes 49156
  117.4 212.4 %copy-start.13 = (f32[512]{0:T(512)S(1)}, f32[512]{0:T(512)}, u32[]{:S(2)}) copy-start(f32[512]{0:T(512)} %dynamic_slice.12) | copy-start | bytes 6148
  361.5 1.1 copy-start.5
  362.6 0.6 copy-start.14
  363.2 0.6 copy-start.15
  586.6 6.3 %copy-start.19 = (bf16[2048,512]{1,0:T(8,128)(2,1)S(1)}, bf16[2048,512]{1,0:T(8,128)(2,1)}, u32[]{:S(2)}) copy-start(bf16[2048,512]{1,0:T(8,128)(2,1)} %get-tuple-element.106) | copy-start | bytes 6291460
  589.6 5.9 copy-start.18
  595.5 2.7 copy-start.17
  595.5 9.1 %slice-start.4 = ((s8[5767168]{0:T(1024)(128)(4,1)}), s8[4194304]{0:T(1024)(128)(4,1)S(1)}, s32[]{:S(2)}) async-start(s8[5767168]{0:T(1024)(128)(4,1)} %bitcast.65), calls=%async_computation.4 | async-start | bytes 8388608
  598.3 3.7 copy-start.16
  598.3 6.4 %slice-start.5 = ((s8[5767168]{0:T(1024)(128)(4,1)}), s8[1572864]{0:T(1024)(128)(4,1)S(1)}, s32[]{:S(2)}) async-start(s8[5767168]{0:T(1024)(128)(4,1)} %bitcast.65), calls=%async_computation.5 | async-start | bytes 3145728
  602.0 8.4 %slice-start.2 = ((s8[5767168]{0:T(1024)(128)(4,1)}), s8[4194304]{0:T(1024)(128)(4,1)S(1)}, s32[]{:S(2)}) async-start(s8[5767168]{0:T(1024)(128)(4,1)} %bitcast.63), calls=%async_computation.2 | async-start | bytes 8388608
  604.7 5.7 slice-start.3
  604.7 10.9 %slice-start = ((s8[5767168]{0:T(1024)(128)(4,1)}), s8[4194304]{0:T(1024)(128)(4,1)S(1)}, s32[]{:S(2)}) async-start(s8[5767168]{0:T(1024)(128)(4,1)} %bitcast.61), calls=%async_computation | async-start | bytes 8388608
  610.4 5.2 slice-start.1

commit v8 on v7

--- a/solution.py
+++ b/solution.py
@@ -1888,7 +1888,7 @@
     sharers = group_count // expert_count
     capacity = 5 * tok_rows // (2 * expert_count)
     slots = expert_count * capacity
-    pieces = 4
+    pieces = 8
     orders = slot_order[0].reshape(tok_rows, 2)
     rows_in = jnp.concatenate([attn_routes.T, mlp_routes.T, orders.T, orders.T], axis=0)
     resid_low, dealt_grads, marks, mark_rows = deal_rows(

time: 627 us -> 635 us (1.013)
  Pallas kernels: 567 us -> 575 us
where the time goes in v8:
time: 635 us; the launch traced here: 629 us
  Pallas kernels  575 us (91%)
  other arithmetic  29.8 us (5%)
  local copies, waits for them, and re-layouts  18.8 us (3%)
    pallas_call x1, Pallas kernels, experts(): pl.pallas_call(functools.partial(experts_kernel, sharers), out_shape=(jax...  212 us
    pallas_call x1, Pallas kernels, closing(): pl.pallas_call(functools.partial(closing_kernel, tuple(jobs)), out_shape=...  210 us
    pallas_call x1, Pallas kernels, front(): pl.pallas_call(functools.partial(front_kernel, sharers), out_shape=(jax.S...  70.5 us
    pallas_call x1, Pallas kernels, settle(): pl.pallas_call(settle_kernel, out_shape=(jax.ShapeDtypeStruct((groups, to...  34.8 us
    pallas_call x1, Pallas kernels, deal_rows(): pl.pallas_call(functools.partial(deal_kernel, capacity, experts_of), out_...  31.6 us
    pallas_call x1, Pallas kernels, attend_back(): pl.pallas_call(attend_back_kernel, out_shape=(block, block, block, jax.Sh...  15.7 us

profile of v8, /device:TPU:20, one launch (start us, length us, event | category | flops | bytes accessed | tf_op | source)
XLA Modules:
  0.0 629.2 jit_solution(3860712006477319879)
XLA Ops:
  0.7 1.3 dynamic_slice.12
  2.0 1.3 dynamic_slice.14
  3.3 0.7 fusion.7
  4.0 0.7 reduce
  4.8 1.4 dynamic-slice_bitcast_fusion
  6.1 0.3 reshape_squeeze.3
  6.5 0.1 copy.33
  6.6 0.7 pad_add_fusion.rows_in
  7.3 0.0 copy-start.3
  7.4 1.9 copy-done.3
  9.2 1.9 copy-done.4
  11.1 31.6 %shard_map.291 = (bf16[1,8,96,2048]{3,2,1,0:T(8,128)(2,1)S(1)}, bf16[8,96,512]{2,1,0:T(8,128)(2,1)S(1)}, s32[768,8]{1,0:T(8,128)S(1)}, s32[8,768]{1,0:T(8,128)S(1)}) custom-call(bf16[768,2048]{1,0:T(8,128)(2,1)S(1)} %copy-done.3, bf16[768,2048]{1,0:T(8,128)(2,1)S(1)} %copy-done.4, s32[1,768]{1,0:T(1,128)S(1)} %broadcast_in_dim.24.ranks, ...), custom_call_target="tpu_custom_call" | custom-call | bytes 105000000 | tf_op jit(solution)/shard_map/pallas_call | solution.py:450
  42.7 0.0 copy-start
  42.7 1.7 copy-done
  44.4 0.7 copy-done.1
  45.1 0.9 copy-done.7
  46.0 0.6 copy-done.12
  46.6 70.5 %shard_map.292 = (bf16[2048,768]{1,0:T(8,128)(2,1)}, f32[768,128]{1,0:T(8,128)}, f32[768,128]{1,0:T(8,128)}, f32[768,1]{1,0:T(8,128)}, f32[768,8]{1,0:T(8,128)},...) custom-call(bf16[768,2048]{1,0:T(8,128)(2,1)} %bitcast.47, ...), custom_call_target="tpu_custom_call" | custom-call | bytes 180000000 | tf_op jit(solution)/shard_map/pallas_call | solution.py:1715
  117.1 0.0 copy-start.2
  117.1 0.0 copy-start.6
  117.1 0.0 copy-start.8
  117.2 0.0 copy-start.11
  117.2 0.0 copy-start.13
  117.2 212.3 %shard_map.293 = (bf16[1,8,240,2048]{3,2,1,0:T(8,128)(2,1)}, bf16[1,8,240,2048]{3,2,1,0:T(8,128)(2,1)}, bf16[8,240,2048]{2,1,0:T(8,128)(2,1)}, bf16[8,240,1408]{...) custom-call(bf16[1,8,240,512]{3,2,1,0:T(8,128)(2,1)} %bitcast.71, ...), custom_call_target="tpu_custom_call" | custom-call | bytes 540000000 | tf_op jit(solution)/shard_map/pallas_call | solution.py:694
  329.6 34.8 %shard_map.294 = (bf16[8,96,512]{2,1,0:T(8,128)(2,1)S(1)}, f32[768,512]{1,0:T(8,128)S(1)}, bf16[1,8,96,2048]{3,2,1,0:T(8,128)(2,1)}, f32[8,512]{1,0:T(8,128)S(1)}, f32[1,512]{1,0:T(1,128)S(1)}) custom-call(bf16[2,1920,512]{2,1,0:T(8,128)(2,1)} %bitcast.70, s32[768,8]{1,0:T(8,128)S(1)} %copy-done.2, f32[768,2]{1,0:T(8,128)S(1)} %copy-done.10, ...), custom_call_target="tpu_custom_call" | custom-call | bytes 90000000 | tf_op jit(solution)/shard_map/pallas_call | solution.py:1392
  364.4 0.0 copy-start.5
  364.4 1.1 copy-done.5
  365.5 0.6 copy-done.14
  366.1 0.6 copy-done.15
  366.7 15.7 %shard_map.295 = (bf16[768,512]{1,0:T(8,128)(2,1)}, bf16[768,512]{1,0:T(8,128)(2,1)}, bf16[768,512]{1,0:T(8,128)(2,1)}, f32[768,2]{1,0:T(8,128)}, bf16[512,768]{1,0:T(8,128)(2,1)}) custom-call(bf16[768,2048]{1,0:T(8,128)(2,1)} %bitcast.55, bf16[512,2048]{1,0:T(8,128)(2,1)} %w_out.1, f32[768,2]{1,0:T(8,128)} %get-tuple-element.83.gates, ...), custom_call_target="tpu_custom_call" | custom-call | bytes 75000000 | tf_op jit(solution)/shard_map/pallas_call | solution.py:1828
  382.4 1.7 fusion.2
  384.1 209.7 %shard_map.296 = (bf16[2048,512]{1,0:T(8,128)(2,1)}, bf16[2048,512]{1,0:T(8,128)(2,1)}, bf16[2048,512]{1,0:T(8,128)(2,1)}, bf16[512,2048]{1,0:T(8,128)(2,1)}, bf...) custom-call(bf16[2048,768]{1,0:T(8,128)(2,1)} %get-tuple-element.78., ...), custom_call_target="tpu_custom_call" | custom-call | bytes 600000000 | tf_op jit(solution)/shard_map/pallas_call | solution.py:1250
  593.8 0.0 copy-start.19
  593.8 3.0 fusion.3
  596.8 1.6 fusion.11
  598.5 1.6 fusion.10
  600.1 0.0 copy-done.19
  600.1 2.6 convert_element_type.39
  602.7 0.0 copy-done.18
  602.7 2.7 convert_element_type.40
  605.5 2.7 convert_element_type.41
  608.2 1.0 copy-done.16
  609.2 2.7 convert_element_type.42
  611.8 0.0 slice-done.4
  611.9 0.0 slice-start
  611.9 5.7 bitcast_convert_fusion.2
  617.6 5.2 bitcast_convert_fusion.1
  622.8 6.0 bitcast_convert_fusion
  (33 shorter events, 0.1 us)
Async XLA Ops:
  7.3 1.9 copy-start.3
  9.2 1.9 copy-start.4
  42.7 1.7 copy-start
  44.4 0.7 copy-start.1
  45.1 0.9 copy-start.7
  46.0 0.6 copy-start.12
  117.1 212.4 %copy-start.2 = (s32[768,8]{1,0:T(8,128)S(1)}, s32[768,8]{1,0:T(8,128)}, u32[]{:S(2)}) copy-start(s32[768,8]{1,0:T(8,128)} %copy-done.1) | copy-start | bytes 73732
  117.1 212.4 %copy-start.6 = (bf16[8,96,512]{2,1,0:T(8,128)(2,1)S(1)}, bf16[8,96,512]{2,1,0:T(8,128)(2,1)}, u32[]{:S(2)}) copy-start(bf16[8,96,512]{2,1,0:T(8,128)(2,1)} %get-tuple-element.76) | copy-start | bytes 2359300
  117.1 212.4 %copy-start.8 = (f32[768,1]{1,0:T(8,128)S(1)}, f32[768,1]{1,0:T(8,128)}, u32[]{:S(2)}) copy-start(f32[768,1]{1,0:T(8,128)} %get-tuple-element.74.factor) | copy-start | bytes 9220
  117.1 212.4 %copy-start.9 = (f32[768,8]{1,0:T(8,128)S(1)}, f32[768,8]{1,0:T(8,128)}, u32[]{:S(2)}) copy-start(f32[768,8]{1,0:T(8,128)} %get-tuple-element.73.logits) | copy-start | bytes 73732
  117.2 212.4 %copy-start.10 = (f32[768,2]{1,0:T(8,128)S(1)}, f32[768,2]{1,0:T(8,128)}, u32[]{:S(2)}) copy-start(f32[768,2]{1,0:T(8,128)} %get-tuple-element.72.gates) | copy-start | bytes 18436
  117.2 212.4 %copy-start.11 = (f32[8,512]{1,0:T(8,128)S(1)}, f32[8,512]{1,0:T(8,128)}, u32[]{:S(2)}) copy-start(f32[8,512]{1,0:T(8,128)} %get-tuple-element.118.refs_12_.router_t) | copy-start | bytes 49156
  117.2 212.4 %copy-start.13 = (f32[512]{0:T(512)S(1)}, f32[512]{0:T(512)}, u32[]{:S(2)}) copy-start(f32[512]{0:T(512)} %dynamic_slice.12) | copy-start | bytes 6148
  364.4 1.1 copy-start.5
  365.5 0.6 copy-start.14
  366.1 0.6 copy-start.15
  593.8 6.3 copy-start.19
  596.8 5.9 copy-start.18
  602.7 2.7 copy-start.17
  602.7 9.1 %slice-start.4 = ((s8[5767168]{0:T(1024)(128)(4,1)}), s8[4194304]{0:T(1024)(128)(4,1)S(1)}, s32[]{:S(2)}) async-start(s8[5767168]{0:T(1024)(128)(4,1)} %bitcast.65), calls=%async_computation.4 | async-start | bytes 8388608
  605.5 3.7 copy-start.16
  605.5 6.4 %slice-start.5 = ((s8[5767168]{0:T(1024)(128)(4,1)}), s8[1572864]{0:T(1024)(128)(4,1)S(1)}, s32[]{:S(2)}) async-start(s8[5767168]{0:T(1024)(128)(4,1)} %bitcast.65), calls=%async_computation.5 | async-start | bytes 3145728
  609.2 8.4 %slice-start.2 = ((s8[5767168]{0:T(1024)(128)(4,1)}), s8[4194304]{0:T(1024)(128)(4,1)S(1)}, s32[]{:S(2)}) async-start(s8[5767168]{0:T(1024)(128)(4,1)} %bitcast.63), calls=%async_computation.2 | async-start | bytes 8388608
  611.8 5.7 slice-start.3
  611.9 10.9 %slice-start = ((s8[5767168]{0:T(1024)(128)(4,1)}), s8[4194304]{0:T(1024)(128)(4,1)S(1)}, s32[]{:S(2)}) async-start(s8[5767168]{0:T(1024)(128)(4,1)} %bitcast.61), calls=%async_computation | async-start | bytes 8388608
  617.6 5.2 slice-start.1
